TPU v7x, 32 devices: a whole 2x2x4 slice. The times are simulated.
32 devices in a mesh: dp: 4 (over y, x), ctx: 8 (over z, core).
Axes of the slice: x: 2, y: 2, z: 4, core: 2. Of those that a mesh axis runs over, the one named last changes fastest.
Arguments:
- tokens: bfloat16 [1024, 8, 2048], P('ctx', 'dp'), may hold values from -6 to 6
- positions: int32 [1024, 8], P('ctx', 'dp'), may hold values from 0 to 1023, as said below
- attn_norm: bfloat16 [2048], P(('dp', 'ctx')), may hold values from 0.5 to 1.5
- query_proj: bfloat16 [2048, 2048], P(('dp', 'ctx')), may hold values from -0.125 to 0.125
- key_projected: bfloat16 [2048, 1024], P(('dp', 'ctx')), may hold values from -0.125 to 0.125
- value_projected: bfloat16 [2048, 1024], P(('dp', 'ctx')), may hold values from -0.125 to 0.125
- head_norms: bfloat16 [2, 128], replicated, may hold values from 0.5 to 1.5
- out_proj: bfloat16 [2048, 2048], P(('dp', 'ctx')), may hold values from -0.5 to 0.5
- mlp_norm: bfloat16 [2048], P(('dp', 'ctx')), may hold values from 0.5 to 1.5
- gate_proj: bfloat16 [2048, 6144], P(('dp', 'ctx')), may hold values from -0.125 to 0.125
- up_proj: bfloat16 [2048, 6144], P(('dp', 'ctx')), may hold values from -0.125 to 0.125
- down_proj: bfloat16 [2048, 6144], P(('dp', 'ctx')), may hold values from -0.078125 to 0.078125
- out_grad: bfloat16 [1024, 8, 2048], P('ctx', 'dp'), may hold values from -6 to 6
Outputs:
- layer_out: bfloat16 [1024, 8, 2048], P('ctx', 'dp')
- input_grad: float32 [1024, 8, 2048], P('ctx', 'dp')
- attn_norm_grad: float32 [2048], P(('dp', 'ctx'))
- query_grad: float32 [2048, 2048], P(('dp', 'ctx'))
- key_grad: float32 [2048, 1024], P(('dp', 'ctx'))
- value_grad: float32 [2048, 1024], P(('dp', 'ctx'))
- head_norm_grad: float32 [2, 128], replicated
- out_proj_grad: float32 [2048, 2048], P(('dp', 'ctx'))
- mlp_norm_grad: float32 [2048], P(('dp', 'ctx'))
- gate_grad: float32 [2048, 6144], P(('dp', 'ctx'))
- up_grad: float32 [2048, 6144], P(('dp', 'ctx'))
- down_grad: float32 [2048, 6144], P(('dp', 'ctx'))
Inputs may be any that keep to these rules, and one draw needn't show every extreme that they name: Each of the 8 sequences is a pack of documents: positions count from 0 at a document's first token and rise by one a token; every sequence begins at position 0; among the 2 sequences of each index of dp one is a single document.
All inputs are finite; a program needn't handle non-finite values.
Results may differ from a plain program's by a relative error of at most 0.017.
Values may be sent and summed in bfloat16 or wider, within the bound.
No kernel may reach another device: no remote copies, remote signals or barrier semaphores. Data moves between devices by JAX's collectives and lax.ppermute only.
A program may use at most 576 MiB of HBM per device.

v0:
```python
import jax
import jax.numpy as jnp
from jax import lax
from jax.sharding import PartitionSpec as P

QUERY_HEADS = 16
KEY_VALUE_HEADS = 8
HEAD_DIMENSION = 128


epsilon = 1e-06
theta_base = 1000000.0


def norm_factor(matrix):
    return lax.rsqrt(jnp.mean(matrix * matrix, axis=-1, keepdims=True) + epsilon)


def norm_back(matrix, factor, upstream):
    return factor * upstream - matrix * (factor * factor * factor) * jnp.mean(
        upstream * matrix, axis=-1, keepdims=True
    )


def rotary_tables(places, head_size):
    half_width = head_size // 2
    frequency = theta_base ** (-(jnp.arange(half_width, dtype=jnp.float32) * 2.0 / head_size))
    angles = places.astype(jnp.float32)[..., None] * frequency
    return (jnp.cos(angles), jnp.sin(angles))


def apply_rotary(matrix, cosine_lookup, sine_lookup):
    half_width = matrix.shape[-1] // 2
    first_half = matrix[..., :half_width]
    second_half = matrix[..., half_width:]
    return jnp.concatenate(
        [
            first_half * cosine_lookup - second_half * sine_lookup,
            second_half * cosine_lookup + first_half * sine_lookup,
        ],
        axis=-1,
    )


def dot_transposed(operand, matrix):
    return lax.dot_general(
        operand, matrix, (((1,), (1,)), ((), ())), preferred_element_type=jnp.float32
    )


def row_contract(operand, matrix):
    return lax.dot_general(
        operand, matrix, (((0,), (0,)), ((), ())), preferred_element_type=jnp.float32
    )


def per_device(
    tokens,
    positions,
    attn_norm,
    query_proj,
    key_projected,
    value_projected,
    head_norms,
    out_proj,
    mlp_norm,
    gate_proj,
    up_proj,
    down_proj,
    out_grad,
):
    block_length, sequence_count, model_width = tokens.shape
    total_rows = block_length * sequence_count
    groups_per_head = QUERY_HEADS // KEY_VALUE_HEADS
    ctx_count = lax.axis_size("ctx")
    total_keys = block_length * ctx_count
    score_scaling = HEAD_DIMENSION ** (-0.5)
    current_key_block = 512
    block_offsets = jnp.arange(total_keys // current_key_block, dtype=jnp.int32) * current_key_block
    query_index = lax.axis_index("ctx") * block_length + jnp.arange(block_length, dtype=jnp.int32)
    earliest = (query_index[:, None] - positions).T
    inputs = tokens.astype(jnp.float32).reshape(total_rows, model_width)
    attn_full = (
        lax.all_gather(attn_norm, ("dp", "ctx"), axis=0, tiled=True),
        lax.all_gather(mlp_norm, ("dp", "ctx"), axis=0, tiled=True),
        lax.all_gather(query_proj, ("dp", "ctx"), axis=0, tiled=True),
        lax.all_gather(key_projected, ("dp", "ctx"), axis=0, tiled=True),
        lax.all_gather(value_projected, ("dp", "ctx"), axis=0, tiled=True),
        lax.all_gather(out_proj, ("dp", "ctx"), axis=0, tiled=True),
    )
    factor_one = norm_factor(inputs)
    normed_one = inputs * factor_one
    first_hidden_state = (normed_one * attn_full[0].astype(jnp.float32)).astype(jnp.bfloat16)
    query_raw = jnp.dot(
        first_hidden_state, attn_full[2], preferred_element_type=jnp.float32
    ).reshape(block_length, sequence_count, QUERY_HEADS, HEAD_DIMENSION)
    key_raw = jnp.dot(first_hidden_state, attn_full[3], preferred_element_type=jnp.float32).reshape(
        block_length, sequence_count, KEY_VALUE_HEADS, HEAD_DIMENSION
    )
    value_low = (
        jnp.dot(first_hidden_state, attn_full[4], preferred_element_type=jnp.float32)
        .astype(jnp.bfloat16)
        .reshape(block_length, sequence_count, KEY_VALUE_HEADS * HEAD_DIMENSION)
    )
    gain_query = head_norms[0].astype(jnp.float32)
    gain_key = head_norms[1].astype(jnp.float32)
    cosine_lookup, sine_lookup = rotary_tables(positions, HEAD_DIMENSION)
    cosine_lookup = cosine_lookup[:, :, None]
    sine_lookup = sine_lookup[:, :, None]
    factor_query = norm_factor(query_raw)
    query_hat = query_raw * factor_query
    query_low = (
        apply_rotary(query_hat * gain_query, cosine_lookup, sine_lookup)
        .astype(jnp.bfloat16)
        .reshape(block_length, sequence_count, KEY_VALUE_HEADS, groups_per_head, HEAD_DIMENSION)
    )
    factor_key = norm_factor(key_raw)
    key_hat = key_raw * factor_key
    key_low = (
        apply_rotary(key_hat * gain_key, cosine_lookup, sine_lookup)
        .astype(jnp.bfloat16)
        .reshape(block_length, sequence_count, KEY_VALUE_HEADS * HEAD_DIMENSION)
    )
    key_all, value_all = (
        lax.all_gather(key_low, "ctx", axis=0, tiled=True),
        lax.all_gather(value_low, "ctx", axis=0, tiled=True),
    )

    def block_keys(offset):
        return lax.dynamic_slice_in_dim(key_all, offset, current_key_block, 0).reshape(
            current_key_block, sequence_count, KEY_VALUE_HEADS, HEAD_DIMENSION
        )

    def block_values(offset):
        return lax.dynamic_slice_in_dim(value_all, offset, current_key_block, 0).reshape(
            current_key_block, sequence_count, KEY_VALUE_HEADS, HEAD_DIMENSION
        )

    def block_scores(offset):
        raw_scores = (
            jnp.einsum(
                "tsgre,usge->sgrtu",
                query_low,
                block_keys(offset),
                preferred_element_type=jnp.float32,
            )
            * score_scaling
        )
        key_index = offset + jnp.arange(current_key_block, dtype=jnp.int32)
        allowed = (key_index[None, None, :] >= earliest[:, :, None]) & (
            key_index[None, None, :] <= query_index[None, :, None]
        )
        return (raw_scores, allowed[:, None, None])

    statistic_layout = (sequence_count, KEY_VALUE_HEADS, groups_per_head, block_length)

    def max_step(running, offset):
        raw_scores, allowed = block_scores(offset)
        masked = jnp.where(allowed, raw_scores, -1e30)
        new_max = jnp.maximum(running[0], jnp.max(masked, axis=-1))
        new_total = running[1] * jnp.exp(running[0] - new_max) + jnp.sum(
            jnp.where(allowed, jnp.exp(masked - new_max[..., None]), 0.0), axis=-1
        )
        return ((new_max, new_total), None)

    start_stats = (
        jnp.full(statistic_layout, -1e30, jnp.float32),
        jnp.zeros(statistic_layout, jnp.float32),
    )
    (row_max, row_total), unused = lax.scan(max_step, start_stats, block_offsets)
    log_total = row_max + jnp.log(row_total)

    def value_step(summed, offset):
        raw_scores, allowed = block_scores(offset)
        prob_low = jnp.where(allowed, jnp.exp(raw_scores - log_total[..., None]), 0.0).astype(
            jnp.bfloat16
        )
        return (
            summed
            + jnp.einsum(
                "sgrtu,usge->tsgre",
                prob_low,
                block_values(offset),
                preferred_element_type=jnp.float32,
            ),
            None,
        )

    attn_sum, unused = lax.scan(
        value_step,
        jnp.zeros(
            (block_length, sequence_count, KEY_VALUE_HEADS, groups_per_head, HEAD_DIMENSION),
            jnp.float32,
        ),
        block_offsets,
    )
    attn_low = attn_sum.reshape(total_rows, QUERY_HEADS * HEAD_DIMENSION).astype(jnp.bfloat16)
    middle = inputs + dot_transposed(attn_low, attn_full[5])
    mlp_gain = attn_full[1].astype(jnp.float32)
    factor_two = norm_factor(middle)
    normed_two = middle * factor_two
    hidden_two = (normed_two * mlp_gain).astype(jnp.bfloat16)
    grad_low = out_grad.reshape(total_rows, model_width)
    mlp_full = (
        lax.all_gather(gate_proj, ("dp", "ctx"), axis=0, tiled=True),
        lax.all_gather(up_proj, ("dp", "ctx"), axis=0, tiled=True),
        lax.all_gather(down_proj, ("dp", "ctx"), axis=0, tiled=True),
    )
    gate_weight = mlp_full[0]
    up_weight = mlp_full[1]
    down_weight = mlp_full[2]
    gate_pre = jnp.dot(hidden_two, gate_weight, preferred_element_type=jnp.float32)
    up_pre = jnp.dot(hidden_two, up_weight, preferred_element_type=jnp.float32)
    gate_sig = jax.nn.sigmoid(gate_pre)
    gate_act = gate_pre * gate_sig
    hidden_low = (gate_act * up_pre).astype(jnp.bfloat16)
    branch_terms = dot_transposed(hidden_low, down_weight)
    layer_out = (
        (middle + branch_terms)
        .astype(jnp.bfloat16)
        .reshape(block_length, sequence_count, model_width)
    )
    mlp_back = (
        lax.all_gather(gate_proj, ("dp", "ctx"), axis=0, tiled=True),
        lax.all_gather(up_proj, ("dp", "ctx"), axis=0, tiled=True),
        lax.all_gather(down_proj, ("dp", "ctx"), axis=0, tiled=True),
    )
    gate_back = mlp_back[0]
    up_back = mlp_back[1]
    down_back = mlp_back[2]
    grad_hidden = jnp.dot(grad_low, down_back, preferred_element_type=jnp.float32)
    grad_gate = (grad_hidden * up_pre * gate_sig * (1.0 + gate_pre * (1.0 - gate_sig))).astype(
        jnp.bfloat16
    )
    grad_up = (grad_hidden * gate_act).astype(jnp.bfloat16)
    grad_terms = dot_transposed(grad_gate, gate_back) + dot_transposed(grad_up, up_back)
    mlp_sums = (
        lax.psum_scatter(
            row_contract(hidden_two, grad_gate), ("dp", "ctx"), scatter_dimension=0, tiled=True
        ),
        lax.psum_scatter(
            row_contract(hidden_two, grad_up), ("dp", "ctx"), scatter_dimension=0, tiled=True
        ),
        lax.psum_scatter(
            row_contract(grad_low, hidden_low), ("dp", "ctx"), scatter_dimension=0, tiled=True
        ),
    )
    mlp_gain_term = jnp.sum(normed_two * grad_terms, axis=0)
    grad_middle = grad_low.astype(jnp.float32) + norm_back(
        middle, factor_two, grad_terms * mlp_gain
    )
    grad_mid_low = grad_middle.astype(jnp.bfloat16)
    attn_back = (
        lax.all_gather(attn_norm, ("dp", "ctx"), axis=0, tiled=True),
        lax.all_gather(mlp_norm, ("dp", "ctx"), axis=0, tiled=True),
        lax.all_gather(query_proj, ("dp", "ctx"), axis=0, tiled=True),
        lax.all_gather(key_projected, ("dp", "ctx"), axis=0, tiled=True),
        lax.all_gather(value_projected, ("dp", "ctx"), axis=0, tiled=True),
        lax.all_gather(out_proj, ("dp", "ctx"), axis=0, tiled=True),
    )
    out_proj_term = row_contract(grad_mid_low, attn_low)
    grad_attn = (
        jnp.dot(grad_mid_low, attn_back[5], preferred_element_type=jnp.float32)
        .astype(jnp.bfloat16)
        .reshape(block_length, sequence_count, KEY_VALUE_HEADS, groups_per_head, HEAD_DIMENSION)
    )
    row_delta = jnp.transpose(
        jnp.sum(grad_attn.astype(jnp.float32) * attn_sum, axis=-1), (1, 2, 3, 0)
    )

    def reverse_increment(grad_query, offset):
        raw_scores, allowed = block_scores(offset)
        prob_full = jnp.where(allowed, jnp.exp(raw_scores - log_total[..., None]), 0.0)
        grad_probs = jnp.einsum(
            "tsgre,usge->sgrtu", grad_attn, block_values(offset), preferred_element_type=jnp.float32
        )
        grad_scores = (prob_full * (grad_probs - row_delta[..., None])).astype(jnp.bfloat16)
        key_gradients = jnp.einsum(
            "sgrtu,tsgre->usge", grad_scores, query_low, preferred_element_type=jnp.float32
        )
        value_gradients = jnp.einsum(
            "sgrtu,tsgre->usge",
            prob_full.astype(jnp.bfloat16),
            grad_attn,
            preferred_element_type=jnp.float32,
        )
        grad_next = grad_query + jnp.einsum(
            "sgrtu,usge->tsgre", grad_scores, block_keys(offset), preferred_element_type=jnp.float32
        )
        return (grad_next, (key_gradients, value_gradients))

    grad_query, (key_gradients, value_gradients) = lax.scan(
        reverse_increment,
        jnp.zeros(
            (block_length, sequence_count, KEY_VALUE_HEADS, groups_per_head, HEAD_DIMENSION),
            jnp.float32,
        ),
        block_offsets,
    )
    summed_key_gradient, summed_value_gradient = (
        lax.psum_scatter(
            (
                key_gradients.reshape(total_keys, sequence_count, KEY_VALUE_HEADS * HEAD_DIMENSION)
                * score_scaling
            ).astype(jnp.bfloat16),
            "ctx",
            scatter_dimension=0,
            tiled=True,
        ).astype(jnp.float32),
        lax.psum_scatter(
            value_gradients.reshape(
                total_keys, sequence_count, KEY_VALUE_HEADS * HEAD_DIMENSION
            ).astype(jnp.bfloat16),
            "ctx",
            scatter_dimension=0,
            tiled=True,
        ).astype(jnp.float32),
    )
    grad_query_rot = apply_rotary(
        grad_query.reshape(block_length, sequence_count, QUERY_HEADS, HEAD_DIMENSION)
        * score_scaling,
        cosine_lookup,
        -sine_lookup,
    )
    grad_key_rot = apply_rotary(
        summed_key_gradient.reshape(block_length, sequence_count, KEY_VALUE_HEADS, HEAD_DIMENSION),
        cosine_lookup,
        -sine_lookup,
    )
    head_sums = lax.psum(
        jnp.stack(
            [
                jnp.sum(query_hat * grad_query_rot, axis=(0, 1, 2)),
                jnp.sum(key_hat * grad_key_rot, axis=(0, 1, 2)),
            ]
        ),
        ("dp", "ctx"),
    )
    grad_query_raw = (
        norm_back(query_raw, factor_query, grad_query_rot * gain_query)
        .astype(jnp.bfloat16)
        .reshape(total_rows, QUERY_HEADS * HEAD_DIMENSION)
    )
    grad_key_raw = (
        norm_back(key_raw, factor_key, grad_key_rot * gain_key)
        .astype(jnp.bfloat16)
        .reshape(total_rows, KEY_VALUE_HEADS * HEAD_DIMENSION)
    )
    value_gradient_reduced = summed_value_gradient.astype(jnp.bfloat16).reshape(
        total_rows, KEY_VALUE_HEADS * HEAD_DIMENSION
    )
    grad_one = (
        dot_transposed(grad_query_raw, attn_back[2])
        + dot_transposed(grad_key_raw, attn_back[3])
        + dot_transposed(value_gradient_reduced, attn_back[4])
    )
    attn_sums = (
        lax.psum_scatter(
            jnp.sum(normed_one * grad_one, axis=0), ("dp", "ctx"), scatter_dimension=0, tiled=True
        ),
        lax.psum_scatter(mlp_gain_term, ("dp", "ctx"), scatter_dimension=0, tiled=True),
        lax.psum_scatter(
            row_contract(first_hidden_state, grad_query_raw),
            ("dp", "ctx"),
            scatter_dimension=0,
            tiled=True,
        ),
        lax.psum_scatter(
            row_contract(first_hidden_state, grad_key_raw),
            ("dp", "ctx"),
            scatter_dimension=0,
            tiled=True,
        ),
        lax.psum_scatter(
            row_contract(first_hidden_state, value_gradient_reduced),
            ("dp", "ctx"),
            scatter_dimension=0,
            tiled=True,
        ),
        lax.psum_scatter(out_proj_term, ("dp", "ctx"), scatter_dimension=0, tiled=True),
    )
    input_grad = (
        grad_middle + norm_back(inputs, factor_one, grad_one * attn_back[0].astype(jnp.float32))
    ).reshape(block_length, sequence_count, model_width)
    return (
        layer_out,
        input_grad,
        attn_sums[0],
        attn_sums[2],
        attn_sums[3],
        attn_sums[4],
        head_sums,
        attn_sums[5],
        attn_sums[1],
        mlp_sums[0],
        mlp_sums[1],
        mlp_sums[2],
    )


def solution(mesh):
    in_specs = (
        P("ctx", "dp", None),
        P("ctx", "dp"),
        P(("dp", "ctx")),
        P(("dp", "ctx"), None),
        P(("dp", "ctx"), None),
        P(("dp", "ctx"), None),
        P(),
        P(("dp", "ctx"), None),
        P(("dp", "ctx")),
        P(("dp", "ctx"), None),
        P(("dp", "ctx"), None),
        P(("dp", "ctx"), None),
        P("ctx", "dp", None),
    )
    out_specs = (
        P("ctx", "dp", None),
        P("ctx", "dp", None),
        P(("dp", "ctx")),
        P(("dp", "ctx"), None),
        P(("dp", "ctx"), None),
        P(("dp", "ctx"), None),
        P(),
        P(("dp", "ctx"), None),
        P(("dp", "ctx")),
        P(("dp", "ctx"), None),
        P(("dp", "ctx"), None),
        P(("dp", "ctx"), None),
    )
    return jax.shard_map(
        per_device, mesh=mesh, in_specs=in_specs, out_specs=out_specs, check_vma=False
    )
```

profile of v0, /device:TPU:0, one launch (start us, length us, event | category | flops | bytes accessed | tf_op | source)
XLA Modules:
  0.0 3104.4 jit_solution(10293009836627419932)
XLA Ops:
  11.2 42.1 %all-reduce.5 = (bf16[2048]{0:T(1024)(128)(2,1)S(1)}, bf16[2048]{0:T(1024)(128)(2,1)S(1)}) all-reduce(bf16[2048]{0:T(1024)(128)(2,1)S(1)} %dynamic-update-slice, bf16[2048]{0:T(1024)(128)(2,1)S(1)} %dynamic-update-slice.1), channel_id=1, replica_groups=mesh['dp'=4,'ctx'=8] {'dp','ctx'}, use_global_device_ids=true, to_apply=%add | all-reduce | flops 4096 | bytes 16384
  88.8 50.8 %all-gather.10.cloned.1.call-done = bf16[2048,1024]{1,0:T(8,128)(2,1)} async-done(((bf16[64,1024]{1,0:T(8,128)(2,1)}), bf16[2048,1024]{1,0:T(8,128)(2,1)}) %all-gather.10.cloned.1.call-update) | async-done | bytes 4194320 | tf_op jit(solution)/shard_map/all_gather | solution.py:88
  149.0 69.6 %all-gather.18.cloned.1.call-done = bf16[2048,2048]{1,0:T(8,128)(2,1)} async-done(((bf16[64,2048]{1,0:T(8,128)(2,1)}), bf16[2048,2048]{1,0:T(8,128)(2,1)}) %all-gather.18.cloned.1.call-update) | async-done | bytes 8388624 | tf_op jit(solution)/shard_map/all_gather | solution.py:86
  239.1 28.0 all-gather.16.cloned.1.call-done
  267.0 31.3 %while.39 = (s32[]{:T(128)}, f32[2,8,2,128]{3,2,1,0:T(2,128)S(1)}, f32[2,8,2,128]{3,2,1,0:T(2,128)S(1)}, s32[2]{0:T(128)S(1)}, s32[2,128]{1,0:T(2,128)S(1)}, /*i...) while((s32[]{:T(128)}, f32[2,8,2,128]{3,2,1,0:T(2,128)S(1)}, ...), condition=%wide.region_6.7_spmd.clone, body=%wide.region_3.6_spmd.clone.sunk | while | flops 553996928 | bytes 24862904 | solution.py:170
  315.1 31.1 %while.40 = (s32[]{:T(128)}, f32[128,2,8,2,128]{0,4,3,2,1:T(8,128)}, s32[2]{0:T(128)S(1)}, bf16[1024,2,1024]{0,2,1:T(8,128)(2,1)}, s32[2,128]{1,0:T(2,128)S(1)},...) while((s32[]{:T(128)}, ...), condition=%wide.region_8.9_spmd.clone, body=%wide.region_7.8_spmd.clone.sunk | while | flops 1083507328 | bytes 18243776 | solution.py:189
  355.3 38.3 %all-gather.20.cloned.1.call-done = bf16[2048,2048]{1,0:T(8,128)(2,1)} async-done(((bf16[64,2048]{1,0:T(8,128)(2,1)}), bf16[2048,2048]{1,0:T(8,128)(2,1)}) %all-gather.20.cloned.1.call-update) | async-done | bytes 8388624 | tf_op jit(solution)/shard_map/all_gather | solution.py:89
  401.4 148.5 %all-gather.22.cloned.1.call-done = bf16[2048,6144]{1,0:T(8,128)(2,1)} async-done(((bf16[64,6144]{1,0:T(8,128)(2,1)}), bf16[2048,6144]{1,0:T(8,128)(2,1)}) %all-gather.22.cloned.1.call-update) | async-done | bytes 25165840 | tf_op jit(solution)/shard_map/all_gather | solution.py:205
  564.2 141.6 %all-gather.24.cloned.1.call-done = bf16[2048,6144]{1,0:T(8,128)(2,1)} async-done(((bf16[64,6144]{1,0:T(8,128)(2,1)}), bf16[2048,6144]{1,0:T(8,128)(2,1)}) %all-gather.24.cloned.1.call-update) | async-done | bytes 25165840 | tf_op jit(solution)/shard_map/all_gather | solution.py:206
  720.2 141.5 %all-gather.26.cloned.1.call-done = bf16[2048,6144]{1,0:T(8,128)(2,1)} async-done(((bf16[64,6144]{1,0:T(8,128)(2,1)}), bf16[2048,6144]{1,0:T(8,128)(2,1)}) %all-gather.26.cloned.1.call-update) | async-done | bytes 25165840 | tf_op jit(solution)/shard_map/all_gather | solution.py:207
  861.7 22.4 multiply_convert_fusion.1
  928.4 61.6 %while.41 = (s32[]{:T(128)}, f32[128,2,8,2,128]{0,4,3,2,1:T(8,128)}, f32[2,512,2,8,128]{4,1,3,2,0:T(8,128)}, bf16[2,512,2,8,128]{4,1,3,2,0:T(8,128)(2,1)}, s32[2...) while((s32[]{:T(128)}, ...), condition=%wide.region_13.14_spmd.clone, body=%wide.region_12.13_spmd.clone.sunk | while | flops 2706702848 | bytes 195617200 | solution.py:292
  1023.8 31.2 %reduce-scatter.12.cloned.1.call-done = bf16[128,2,1024]{2,0,1:T(8,128)(2,1)} async-done(((bf16[1024,2,1024]{2,0,1:T(8,128)(2,1)}), bf16[128,2,1024]{2,0,1:T(8,128)(2,1)}) %reduce-scatter.12.cloned.1.call-update) | async-done | bytes 524304 | tf_op jit(solution)/shard_map/reduce_scatter | solution.py:301
  1067.1 38.4 %reduce-scatter.14.cloned.1.call-done = bf16[128,2,1024]{2,0,1:T(8,128)(2,1)} async-done(((bf16[1024,2,1024]{2,0,1:T(8,128)(2,1)}), bf16[128,2,1024]{2,0,1:T(8,128)(2,1)}) %reduce-scatter.14.cloned.1.call-update) | async-done | bytes 524304 | tf_op jit(solution)/shard_map/reduce_scatter | solution.py:310
  1159.5 21.7 fusion.69
  1182.4 21.6 convolution_bitcast_fusion
  1204.0 49.0 %copy.136 = f32[2048,6144]{1,0:T(8,128)} copy(f32[2048,6144]{0,1:T(8,128)} %convolution_bitcast_fusion) | data formatting | bytes 100663296
  1288.6 39.3 %all-reduce.4 = (f32[2048]{0:T(1024)S(1)}, f32[2,128]{1,0:T(2,128)}, f32[2048]{0:T(1024)S(1)}) all-reduce(f32[2048]{0:T(1024)S(1)} %get-tuple-element.416, f32[2,128]{1,0:T(2,128)S(1)} %pad_maximum_fusion.4, f32[2048]{0:T(1024)S(1)} %copy-done.52), channel_id=4, replica_groups=mesh['dp'=4,'ctx'=8] {'dp','ctx'}, use_global_device_ids=true, to_apply=%region_20.21.clone | all-reduce | flops 4352 | bytes 34816
  1329.0 82.1 %reduce-scatter.20.cloned.1.call-done = f32[64,1024]{1,0:T(8,128)} async-done(((f32[2048,1024]{1,0:T(8,128)}), f32[64,1024]{1,0:T(8,128)}) %reduce-scatter.20.cloned.1.call-update) | async-done | bytes 262160 | tf_op jit(solution)/shard_map/reduce_scatter | solution.py:374
  1411.1 188.1 %reduce-scatter.16.cloned.1.call-done = f32[64,2048]{1,0:T(8,128)} async-done(((f32[2048,2048]{1,0:T(8,128)}), f32[64,2048]{1,0:T(8,128)}) %reduce-scatter.16.cloned.1.call-update) | async-done | bytes 524304 | tf_op jit(solution)/shard_map/reduce_scatter | solution.py:362
  1599.2 187.1 %reduce-scatter.22.cloned.1.call-done = f32[64,2048]{1,0:T(8,128)} async-done(((f32[2048,2048]{1,0:T(8,128)}), f32[64,2048]{1,0:T(8,128)}) %reduce-scatter.22.cloned.1.call-update) | async-done | bytes 524304 | tf_op jit(solution)/shard_map/reduce_scatter | solution.py:380
  1786.3 436.2 %reduce-scatter.24.cloned.1.call-done = f32[64,6144]{1,0:T(8,128)} async-done(((f32[2048,6144]{1,0:T(8,128)}), f32[64,6144]{1,0:T(8,128)}) %reduce-scatter.24.cloned.1.call-update) | async-done | bytes 1572880 | tf_op jit(solution)/shard_map/reduce_scatter | solution.py:238
  2222.5 437.5 %reduce-scatter.26.cloned.1.call-done = f32[64,6144]{1,0:T(8,128)} async-done(((f32[2048,6144]{1,0:T(8,128)}), f32[64,6144]{1,0:T(8,128)}) %reduce-scatter.26.cloned.1.call-update) | async-done | bytes 1572880 | tf_op jit(solution)/shard_map/reduce_scatter | solution.py:241
  2660.0 437.4 %reduce-scatter.28.cloned.1.call-done = f32[64,6144]{1,0:T(8,128)} async-done(((f32[2048,6144]{1,0:T(8,128)}), f32[64,6144]{1,0:T(8,128)}) %reduce-scatter.28.cloned.1.call-update) | async-done | bytes 1572880
  (326 shorter events, 423.8 us)
Async XLA Ops:
  7.2 68.7 %all-gather.14.cloned.1.call-start = ((), (), s32[]{:S(2)}) async-start(), calls=%async_computation.11 | async-start | bytes 4325376 | tf_op jit(solution)/shard_map/all_gather | solution.py:87
  7.9 131.7 %all-gather.10.cloned.1.call-start = ((), (), s32[]{:S(2)}) async-start(), calls=%async_computation.9 | async-start | bytes 4325376 | tf_op jit(solution)/shard_map/all_gather | solution.py:88
  8.7 209.9 %all-gather.18.cloned.1.call-start = ((), (), s32[]{:S(2)}) async-start(), calls=%async_computation.13 | async-start | bytes 8650752 | tf_op jit(solution)/shard_map/all_gather | solution.py:86
  9.4 257.6 %all-gather.16.cloned.1.call-start = ((), (), s32[]{:S(2)}) async-start(), calls=%async_computation.12 | async-start | bytes 4718592 | tf_op jit(solution)/shard_map/all_gather | solution.py:125
  53.3 86.3 %copy-start.43 = (f32[2048]{0:T(1024)}, f32[2048]{0:T(1024)S(1)}, u32[]{:S(2)}) copy-start(f32[2048]{0:T(1024)S(1)} %convert_element_type.119) | copy-start | bytes 24580
  54.1 182.7 %copy-start.53 = (f32[128]{0:T(128)}, f32[128]{0:T(128)S(1)}, u32[]{:S(2)}) copy-start(f32[128]{0:T(128)S(1)} %get-tuple-element.513) | copy-start | bytes 1540
  58.2 178.9 %copy-start.31 = (f32[128,2,64]{0,2,1:T(8,128)}, f32[128,2,64]{0,2,1:T(8,128)S(1)}, u32[]{:S(2)}) copy-start(f32[128,2,64]{0,2,1:T(8,128)S(1)} %get-tuple-element.508) | copy-start | bytes 196612
  88.2 226.9 %all-gather.12.cloned.1.call-start = ((), (), s32[]{:S(2)}) async-start(), calls=%async_computation.10 | async-start | bytes 4718592 | tf_op jit(solution)/shard_map/all_gather | solution.py:126
  88.6 54.5 %copy-start.9 = (f32[256,2048]{1,0:T(8,128)}, f32[256,2048]{1,0:T(8,128)S(1)}, u32[]{:S(2)}) copy-start(f32[256,2048]{1,0:T(8,128)S(1)} %reshape.365) | copy-start | bytes 6291460
  144.5 249.1 %all-gather.20.cloned.1.call-start = ((), (), s32[]{:S(2)}) async-start(), calls=%async_computation.14 | async-start | bytes 8650752 | tf_op jit(solution)/shard_map/all_gather | solution.py:89
  145.1 404.8 %all-gather.22.cloned.1.call-start = ((), (), s32[]{:S(2)}) async-start(), calls=%async_computation.15 | async-start | bytes 25952256 | tf_op jit(solution)/shard_map/all_gather | solution.py:205
  145.8 560.0 %all-gather.24.cloned.1.call-start = ((), (), s32[]{:S(2)}) async-start(), calls=%async_computation.16 | async-start | bytes 25952256 | tf_op jit(solution)/shard_map/all_gather | solution.py:206
  146.6 715.1 %all-gather.26.cloned.1.call-start = ((), (), s32[]{:S(2)}) async-start(), calls=%async_computation.17 | async-start | bytes 25952256 | tf_op jit(solution)/shard_map/all_gather | solution.py:207
  147.3 907.7 %reduce-scatter.12.cloned.1.call-start = ((), (), s32[]{:S(2)}) async-start(), calls=%async_computation.18 | async-start | bytes 4718592 | tf_op jit(solution)/shard_map/reduce_scatter | solution.py:301
  401.4 304.4 %copy-start.14 = (bf16[256,2048]{1,0:T(8,128)(2,1)}, bf16[256,2048]{1,0:T(8,128)(2,1)S(1)}, u32[]{:S(2)}) copy-start(bf16[256,2048]{1,0:T(8,128)(2,1)S(1)} %multiply_convert_fusion.4) | copy-start | bytes 3145732
  564.2 297.5 %copy-start.16 = (bf16[256,2048]{1,0:T(8,128)(2,1)S(1)}, bf16[256,2048]{1,0:T(8,128)(2,1)}, u32[]{:S(2)}) copy-start(bf16[256,2048]{1,0:T(8,128)(2,1)} %reshape.368) | copy-start | bytes 3145732
  1006.7 98.8 %reduce-scatter.14.cloned.1.call-start = ((), (), s32[]{:S(2)}) async-start(), calls=%async_computation.19 | async-start | bytes 4718592 | tf_op jit(solution)/shard_map/reduce_scatter | solution.py:310
  1021.0 308.1 %reduce-scatter.18.cloned.1.call-start = ((), (), s32[]{:S(2)}) async-start(), calls=%async_computation.21 | async-start | bytes 8650752 | tf_op jit(solution)/shard_map/reduce_scatter | solution.py:368
  1066.9 344.2 %reduce-scatter.20.cloned.1.call-start = ((), (), s32[]{:S(2)}) async-start(), calls=%async_computation.22 | async-start | bytes 8650752 | tf_op jit(solution)/shard_map/reduce_scatter | solution.py:374
  1111.3 487.9 %reduce-scatter.16.cloned.1.call-start = ((), (), s32[]{:S(2)}) async-start(), calls=%async_computation.20 | async-start | bytes 17301504 | tf_op jit(solution)/shard_map/reduce_scatter | solution.py:362
  1126.1 660.2 %reduce-scatter.22.cloned.1.call-start = ((), (), s32[]{:S(2)}) async-start(), calls=%async_computation.23 | async-start | bytes 17301504 | tf_op jit(solution)/shard_map/reduce_scatter | solution.py:380
  1136.2 1086.4 %reduce-scatter.24.cloned.1.call-start = ((), (), s32[]{:S(2)}) async-start(), calls=%async_computation.24 | async-start | bytes 51904512 | tf_op jit(solution)/shard_map/reduce_scatter | solution.py:238
  1159.0 1501.0 %reduce-scatter.26.cloned.1.call-start = ((), (), s32[]{:S(2)}) async-start(), calls=%async_computation.25 | async-start | bytes 51904512 | tf_op jit(solution)/shard_map/reduce_scatter | solution.py:241
  1181.2 1916.2 %reduce-scatter.28.cloned.1.call-start = ((), (), s32[]{:S(2)}) async-start(), calls=%async_computation.26 | async-start | bytes 51904512
  (60 other events, 580.1 us)
Sparse Core Ops, SparseCore 0:
  11.0 64.8 all-gather.13
  78.9 60.6 all-gather.9
  142.6 75.9 all-gather.17
  220.6 46.3 all-gather.15
  269.0 46.0 all-gather.11
  317.9 75.6 all-gather.19
  396.6 153.2 all-gather.21
  552.9 152.8 all-gather.23
  708.8 152.8 all-gather.25
  1006.8 48.1 reduce-scatter.11
  1057.3 48.1 reduce-scatter.13
  1108.2 149.5 reduce-scatter.17
  1260.7 150.4 reduce-scatter.19
  1413.8 185.3 reduce-scatter.15
  1601.9 184.3 reduce-scatter.21
  1793.2 429.3 reduce-scatter.23
  2229.4 430.5 reduce-scatter.25
  2666.9 430.4 reduce-scatter.27
where the time goes:
time: 3110 us; the launch traced here: 3100 us
  waiting for transfers between devices  2490 us (80%)
  matrix products  276 us (9%)
  local copies, waits for them, and re-layouts  178 us (6%)
  blocking collectives  81.5 us (3%)
  other arithmetic  46.1 us (1%)
    unnamed x19, waiting for transfers between devices  442 us
    reduce_scatter x1, waiting for transfers between devices, per_device(): lax.psum_scatter(row_contract(hidden_two, grad_up), ('dp', 'ctx'), scatte...  437 us
    reduce_scatter x1, waiting for transfers between devices, per_device(): lax.psum_scatter(row_contract(hidden_two, grad_gate), ('dp', 'ctx'), scat...  436 us
    reduce_scatter x1, waiting for transfers between devices, per_device(): lax.psum_scatter(row_contract(first_hidden_state, grad_query_raw), ('dp',...  188 us
    reduce_scatter x1, waiting for transfers between devices, per_device(): lax.psum_scatter(out_proj_term, ('dp', 'ctx'), scatter_dimension=0, tiled...  187 us
    all_gather x1, waiting for transfers between devices, per_device(): lax.all_gather(gate_proj, ('dp', 'ctx'), axis=0, tiled=True)  149 us
    all_gather x1, waiting for transfers between devices, per_device(): lax.all_gather(up_proj, ('dp', 'ctx'), axis=0, tiled=True)  142 us
    all_gather x1, waiting for transfers between devices, per_device(): lax.all_gather(down_proj, ('dp', 'ctx'), axis=0, tiled=True)  141 us
  transfers between devices with their start and end apart: 18, of which 17 were waited for; matrix products, arithmetic and copies ran while one was open for 11% of the time, Pallas kernels for 0%

commit v1 on v0

v1 whole, which is shorter than its diff:
```python
import functools

import jax
import jax.numpy as jnp
from jax import lax
from jax.experimental import pallas as pl
from jax.experimental.pallas import tpu as pltpu
from jax.sharding import Mesh
from jax.sharding import PartitionSpec as P

QUERY_HEADS = 16
KEY_VALUE_HEADS = 8
HEAD_DIMENSION = 128
GROUP = QUERY_HEADS // KEY_VALUE_HEADS
HEAD_SET = (GROUP + 2) * HEAD_DIMENSION

epsilon = 1e-06
theta_base = 1000000.0
score_scaling = HEAD_DIMENSION ** (-0.5)
F32 = jnp.float32
BF16 = jnp.bfloat16


def norm_factor(matrix):
    return lax.rsqrt(jnp.mean(matrix * matrix, axis=-1, keepdims=True) + epsilon)


def norm_back(matrix, factor, upstream):
    return factor * upstream - matrix * (factor * factor * factor) * jnp.mean(
        upstream * matrix, axis=-1, keepdims=True
    )


def dot(a, b, ca=1, cb=0):
    return lax.dot_general(a, b, (((ca,), (cb,)), ((), ())), preferred_element_type=F32)


def rotate(x, cos, sin):
    return x * cos + pltpu.roll(x, HEAD_DIMENSION // 2, 1) * sin


def head_slice(i):
    return slice(i * HEAD_DIMENSION, (i + 1) * HEAD_DIMENSION)


def normed_rotated(raw, gain, cos, sin):
    return rotate(raw * norm_factor(raw) * gain, cos, sin).astype(BF16)


def probabilities(keys, queries, first_query, earliest):
    scores = dot(keys, queries, 1, 1) * score_scaling
    key_index = lax.broadcasted_iota(jnp.int32, scores.shape, 0)
    query_index = lax.broadcasted_iota(jnp.int32, scores.shape, 1) + first_query
    allowed = (key_index <= query_index) & (key_index >= earliest)
    masked = jnp.where(allowed, scores, -1e30)
    shifted = jnp.exp(masked - jnp.max(masked, axis=0, keepdims=True))
    return shifted * (1.0 / jnp.sum(shifted, axis=0, keepdims=True))


def forward_kernel(block, qkv_ref, gain_ref, cos_ref, sin_ref, early_ref, out_ref):
    length = qkv_ref.shape[0]
    gains = gain_ref[...]
    cos, sin = cos_ref[...], sin_ref[...]
    keys = normed_rotated(qkv_ref[:, head_slice(GROUP)], gains[1:2], cos, sin)
    values_t = qkv_ref[:, head_slice(GROUP + 1)].T.astype(BF16)
    for i in range(length // block):
        rows = slice(i * block, (i + 1) * block)
        seen = (i + 1) * block
        for g in range(GROUP):
            queries = normed_rotated(qkv_ref[rows, head_slice(g)], gains[0:1], cos[rows], sin[rows])
            probs = probabilities(keys[:seen], queries, i * block, early_ref[0:1, rows]).astype(BF16)
            mixed = dot(values_t[:, :seen], probs)
            out_ref[rows, head_slice(g)] = mixed.T.astype(BF16)


def backward_kernel(
    block, qkv_ref, dout_ref, gain_ref, cos_ref, sin_ref, early_ref, dqkv_ref, dgain_ref, dkey_ref, dvalue_ref
):
    length = qkv_ref.shape[0]
    gains = gain_ref[...]
    cos, sin = cos_ref[...], sin_ref[...]
    key_raw = qkv_ref[:, head_slice(GROUP)]
    keys = normed_rotated(key_raw, gains[1:2], cos, sin)
    keys_t = keys.astype(F32).T.astype(BF16)
    values = qkv_ref[:, head_slice(GROUP + 1)].astype(BF16)
    dkey_ref[...] = jnp.zeros_like(dkey_ref)
    dvalue_ref[...] = jnp.zeros_like(dvalue_ref)
    query_gain_sum = jnp.zeros((1, HEAD_DIMENSION), F32)
    for i in range(length // block):
        rows = slice(i * block, (i + 1) * block)
        seen = (i + 1) * block
        for g in range(GROUP):
            query_raw = qkv_ref[rows, head_slice(g)]
            queries = normed_rotated(query_raw, gains[0:1], cos[rows], sin[rows])
            dout = dout_ref[rows, head_slice(g)]
            probs = probabilities(keys[:seen], queries, i * block, early_ref[0:1, rows])
            dprobs = dot(values[:seen], dout, 1, 1)
            delta = jnp.sum(probs * dprobs, axis=0, keepdims=True)
            dscores = (probs * (dprobs - delta)).astype(BF16)
            dkey_ref[:seen] += dot(dscores, queries)
            dvalue_ref[:seen] += dot(probs.astype(BF16), dout)
            dquery = dot(keys_t[:, :seen], dscores).T * score_scaling
            dquery = rotate(dquery, cos[rows], -sin[rows])
            factor = norm_factor(query_raw)
            query_gain_sum += jnp.sum(query_raw * factor * dquery, axis=0, keepdims=True)
            dqkv_ref[rows, head_slice(g)] = norm_back(query_raw, factor, dquery * gains[0:1]).astype(BF16)
    dkey = rotate(dkey_ref[...] * score_scaling, cos, -sin)
    factor = norm_factor(key_raw)
    dgain_ref[0, 0:1, :] = query_gain_sum
    dgain_ref[0, 1:2, :] = jnp.sum(key_raw * factor * dkey, axis=0, keepdims=True)
    dgain_ref[0, 2:, :] = jnp.zeros((6, HEAD_DIMENSION), F32)
    dqkv_ref[:, head_slice(GROUP)] = norm_back(key_raw, factor, dkey * gains[1:2]).astype(BF16)
    dqkv_ref[:, head_slice(GROUP + 1)] = dvalue_ref[...].astype(BF16)


def per_head_specs(length):
    whole = lambda shape: pl.BlockSpec(shape, lambda n: (0,) * len(shape))
    return [
        whole((2, HEAD_DIMENSION)),
        whole((length, HEAD_DIMENSION)),
        whole((length, HEAD_DIMENSION)),
        whole((8, length)),
    ]


def columns_spec(length, width):
    return pl.BlockSpec((length, width), lambda n: (0, n))


def attention_forward(qkv, gains, cos, sin, earliest):
    length, width = qkv.shape
    heads = width // HEAD_SET
    return pl.pallas_call(
        functools.partial(forward_kernel, 256),
        grid=(heads,),
        in_specs=[columns_spec(length, HEAD_SET)] + per_head_specs(length),
        out_specs=columns_spec(length, GROUP * HEAD_DIMENSION),
        out_shape=jax.ShapeDtypeStruct((length, heads * GROUP * HEAD_DIMENSION), BF16),
        compiler_params=pltpu.CompilerParams(vmem_limit_bytes=48 << 20),
        cost_estimate=pl.CostEstimate(
            flops=heads * GROUP * 2 * length * length * HEAD_DIMENSION * 2,
            bytes_accessed=length * width * 6,
            transcendentals=heads * GROUP * length * length // 2,
        ),
    )(qkv, gains, cos, sin, earliest)


def attention_backward(qkv, dout, gains, cos, sin, earliest):
    length, width = qkv.shape
    heads = width // HEAD_SET
    return pl.pallas_call(
        functools.partial(backward_kernel, 256),
        grid=(heads,),
        in_specs=[columns_spec(length, HEAD_SET), columns_spec(length, GROUP * HEAD_DIMENSION)]
        + per_head_specs(length),
        out_specs=[
            columns_spec(length, HEAD_SET),
            pl.BlockSpec((1, 8, HEAD_DIMENSION), lambda n: (n, 0, 0)),
        ],
        out_shape=[
            jax.ShapeDtypeStruct((length, width), BF16),
            jax.ShapeDtypeStruct((heads, 8, HEAD_DIMENSION), F32),
        ],
        scratch_shapes=[pltpu.VMEM((length, HEAD_DIMENSION), F32)] * 2,
        compiler_params=pltpu.CompilerParams(vmem_limit_bytes=48 << 20),
        cost_estimate=pl.CostEstimate(
            flops=heads * GROUP * 2 * length * length * HEAD_DIMENSION * 5,
            bytes_accessed=length * width * 8,
            transcendentals=heads * GROUP * length * length // 2,
        ),
    )(qkv, dout, gains, cos, sin, earliest)


def per_device(
    tokens,
    positions,
    attn_norm,
    query_proj,
    key_projected,
    value_projected,
    head_norms,
    out_proj,
    mlp_norm,
    gate_proj,
    up_proj,
    down_proj,
    out_grad,
):
    block, seqs, width = tokens.shape
    rows = block * seqs
    dp = lax.axis_size("dp")
    parts = lax.axis_size("t")
    ctx = 2 * parts
    length = block * ctx
    depth = query_proj.shape[0]
    half = lax.axis_index("h")
    part = lax.axis_index("t")
    everywhere = ("dp", "h", "t")

    def to_sequence(blocks):
        keep = lax.dynamic_index_in_dim(blocks, half, 1, keepdims=False)
        give = lax.dynamic_index_in_dim(blocks, 1 - half, 1, keepdims=False)
        got = lax.ppermute(give, "h", [(0, 1), (1, 0)])
        pair = jnp.where(half == 0, jnp.stack([keep, got]), jnp.stack([got, keep]))
        return lax.all_gather(pair, "t", axis=1, tiled=True).reshape(length, width)

    def to_blocks(partial):
        pair = lax.psum_scatter(
            partial.astype(BF16).reshape(2, length // 2, width), "t", scatter_dimension=1, tiled=True
        )
        keep = lax.dynamic_index_in_dim(pair, half, 0, keepdims=False)
        give = lax.dynamic_index_in_dim(pair, 1 - half, 0, keepdims=False)
        got = lax.ppermute(give, "h", [(0, 1), (1, 0)])
        return jnp.where(half == 0, jnp.stack([keep, got], 1), jnp.stack([got, keep], 1)).reshape(rows, width)

    def gather_dp(x):
        return lax.all_gather(x, "dp", axis=0, tiled=True)

    def scatter_dp(x):
        return lax.psum_scatter(x.astype(BF16), "dp", scatter_dimension=0, tiled=True)

    small = jnp.concatenate(
        [
            attn_norm.astype(F32),
            mlp_norm.astype(F32),
            positions.T.reshape(-1).astype(F32),
        ]
    )
    small_all = lax.all_gather(small, everywhere, axis=0, tiled=False)
    attn_gain = small_all[:, :depth].reshape(1, width)
    mlp_gain = small_all[:, depth : 2 * depth].reshape(1, width)
    own_places = lax.dynamic_slice_in_dim(
        small_all[:, 2 * depth :].reshape(dp, ctx, seqs, block), lax.axis_index("dp"), 1, 0
    )[0]
    places = lax.dynamic_index_in_dim(own_places, half, 1, keepdims=False).reshape(length)

    heads = KEY_VALUE_HEADS // parts
    qkv_set = jnp.concatenate(
        [
            query_proj.reshape(depth, KEY_VALUE_HEADS, GROUP * HEAD_DIMENSION),
            key_projected.reshape(depth, KEY_VALUE_HEADS, HEAD_DIMENSION),
            value_projected.reshape(depth, KEY_VALUE_HEADS, HEAD_DIMENSION),
        ],
        axis=2,
    ).reshape(depth, parts, heads * HEAD_SET)
    mix_width = heads * GROUP * HEAD_DIMENSION
    attn_set = jnp.concatenate([qkv_set, out_proj.reshape(depth, parts, mix_width)], axis=2)
    attn_set = lax.all_to_all(jnp.transpose(attn_set, (1, 0, 2)), "t", 0, 0, tiled=True)
    attn_set = attn_set.reshape(parts * depth, heads * HEAD_SET + mix_width)
    qkv_weight = lax.all_gather(attn_set[:, : heads * HEAD_SET], ("dp", "h"), axis=0, tiled=True)
    out_weight = lax.all_gather(attn_set[:, heads * HEAD_SET :], ("dp", "h"), axis=0, tiled=True)

    hidden = gate_proj.shape[1] // dp

    def ffn_columns(w):
        w = jnp.transpose(w.reshape(depth, dp, hidden), (1, 0, 2))
        w = lax.all_to_all(w, "dp", 0, 0, tiled=True)
        return lax.all_gather(w, ("h", "t"), axis=1, tiled=True).reshape(width, hidden)

    def ffn_owner(g):
        g = lax.psum_scatter(
            g.astype(BF16).reshape(dp, ctx * depth, hidden), ("h", "t"), scatter_dimension=1, tiled=True
        )
        g = lax.all_to_all(g, "dp", 0, 0, tiled=True)
        return jnp.transpose(g, (1, 0, 2)).reshape(depth, dp * hidden).astype(F32)

    sequence = to_sequence(tokens).astype(F32)
    gate_weight, up_weight, down_weight = ffn_columns(gate_proj), ffn_columns(up_proj), ffn_columns(down_proj)
    grad_own = out_grad.reshape(rows, width)
    grad_rows = gather_dp(grad_own)

    gains = head_norms.astype(F32)
    half_width = HEAD_DIMENSION // 2
    frequency = theta_base ** (-(jnp.arange(half_width, dtype=F32) * 2.0 / HEAD_DIMENSION))
    angles = places[:, None] * frequency
    cos, sin = jnp.cos(angles), jnp.sin(angles)
    cos = jnp.concatenate([cos, cos], axis=1)
    sin = jnp.concatenate([-sin, sin], axis=1)
    earliest = jnp.broadcast_to(
        (jnp.arange(length, dtype=jnp.int32) - places.astype(jnp.int32))[None, :], (8, length)
    )
    seq_factor = norm_factor(sequence)
    hidden_one = (sequence * seq_factor * attn_gain).astype(BF16)
    qkv = dot(hidden_one, qkv_weight)
    mixed = attention_forward(qkv, gains, cos, sin, earliest)
    inputs = tokens.astype(F32).reshape(rows, width)
    middle = inputs + to_blocks(dot(mixed, out_weight, 1, 1)).astype(F32)

    factor_two = norm_factor(middle)
    hidden_two = gather_dp((middle * factor_two * mlp_gain).astype(BF16))
    gate_pre = dot(hidden_two, gate_weight)
    up_pre = dot(hidden_two, up_weight)
    gate_sig = jax.nn.sigmoid(gate_pre)
    gate_act = gate_pre * gate_sig
    hidden_low = (gate_act * up_pre).astype(BF16)
    grad_hidden = dot(grad_rows, down_weight)
    grad_gate = (grad_hidden * up_pre * gate_sig * (1.0 + gate_pre * (1.0 - gate_sig))).astype(BF16)
    grad_up = (grad_hidden * gate_act).astype(BF16)
    grad_two = scatter_dp(dot(grad_gate, gate_weight, 1, 1) + dot(grad_up, up_weight, 1, 1)).astype(F32)
    branch = scatter_dp(dot(hidden_low, down_weight, 1, 1)).astype(F32)
    layer_out = (middle + branch).astype(BF16).reshape(block, seqs, width)
    down_grad = ffn_owner(dot(grad_rows, hidden_low, 0, 0))
    gate_grad = ffn_owner(dot(hidden_two, grad_gate, 0, 0))
    up_grad = ffn_owner(dot(hidden_two, grad_up, 0, 0))

    mlp_norm_sum = jnp.sum(middle * factor_two * grad_two, axis=0, keepdims=True)
    grad_middle = grad_own.astype(F32) + norm_back(middle, factor_two, grad_two * mlp_gain)

    grad_mid = to_sequence(grad_middle.astype(BF16).reshape(block, seqs, width))
    grad_mixed = dot(grad_mid, out_weight).astype(BF16)
    out_term = dot(grad_mid, mixed, 0, 0)
    grad_qkv, gain_terms = attention_backward(qkv, grad_mixed, gains, cos, sin, earliest)
    qkv_term = dot(hidden_one, grad_qkv, 0, 0)
    grad_one_part = dot(grad_qkv, qkv_weight, 1, 1)
    attn_norm_sum = jnp.sum(sequence * seq_factor * grad_one_part, axis=0, keepdims=True)
    grad_one = to_blocks(grad_one_part).astype(F32)

    sums = jnp.concatenate(
        [attn_norm_sum, mlp_norm_sum, jnp.sum(gain_terms, axis=0)[:2].reshape(1, -1)], axis=1
    )
    sums = lax.psum(sums, everywhere)[0]
    owner = (lax.axis_index("dp") * ctx + half * parts + part) * depth
    attn_norm_grad = lax.dynamic_slice_in_dim(sums, owner, depth)
    mlp_norm_grad = lax.dynamic_slice_in_dim(sums, width + owner, depth)
    head_norm_grad = sums[2 * width :].reshape(2, HEAD_DIMENSION)

    attn_terms = jnp.concatenate([qkv_term.astype(BF16), out_term.astype(BF16)], axis=1)
    attn_terms = lax.psum_scatter(attn_terms, ("dp", "h"), scatter_dimension=0, tiled=True)
    attn_terms = lax.all_to_all(attn_terms.reshape(parts, depth, -1), "t", 0, 0, tiled=True)
    attn_terms = jnp.transpose(attn_terms, (1, 0, 2)).astype(F32)
    qkv_grad = attn_terms[:, :, : heads * HEAD_SET].reshape(depth, KEY_VALUE_HEADS, HEAD_SET)
    split = GROUP * HEAD_DIMENSION
    query_grad = qkv_grad[:, :, :split].reshape(depth, -1)
    key_grad = qkv_grad[:, :, split : split + HEAD_DIMENSION].reshape(depth, -1)
    value_grad = qkv_grad[:, :, split + HEAD_DIMENSION :].reshape(depth, -1)
    out_proj_grad = attn_terms[:, :, heads * HEAD_SET :].reshape(depth, -1)

    input_grad = (grad_middle + norm_back(inputs, norm_factor(inputs), grad_one * attn_gain)).reshape(
        block, seqs, width
    )
    return (
        layer_out,
        input_grad,
        attn_norm_grad,
        query_grad,
        key_grad,
        value_grad,
        head_norm_grad,
        out_proj_grad,
        mlp_norm_grad,
        gate_grad,
        up_grad,
        down_grad,
    )


def solution(mesh):
    dp, ctx = mesh.shape["dp"], mesh.shape["ctx"]
    fine = Mesh(mesh.devices.reshape(dp, 2, ctx // 2), ("dp", "h", "t"))
    acts = P(("h", "t"), "dp", None)
    rows = P(("dp", "h", "t"), None)
    gain = P(("dp", "h", "t"))
    in_specs = (
        acts,
        P(("h", "t"), "dp"),
        gain,
        rows,
        rows,
        rows,
        P(),
        rows,
        gain,
        rows,
        rows,
        rows,
        acts,
    )
    out_specs = (acts, acts, gain, rows, rows, rows, P(), rows, gain, rows, rows, rows)
    return jax.shard_map(per_device, mesh=fine, in_specs=in_specs, out_specs=out_specs, check_vma=False)
```

time: 3110 us -> 1280 us (0.41)
  waiting for transfers between devices: 2490 us -> 715 us
  matrix products: 276 us -> 142 us
  blocking collectives: 81.5 us -> 184 us
  local copies, waits for them, and re-layouts: 178 us -> 116 us
  Pallas kernels: 0 us -> 31.5 us
    reduce_scatter x8 -> x7, waiting for transfers between devices: 1400 us -> 311 us  [the longest x2 122 us: ffn_owner(): lax.psum_scatter(g.astype(BF16).reshape(dp, ctx * depth, hidden), ('h', '...]
    unnamed x19 -> x18, waiting for transfers between devices: 442 us -> 54.2 us
    all_gather x9, waiting for transfers between devices: 650 us -> 271 us  [the longest x3 96.1 us: ffn_columns(): lax.all_gather(w, ('h', 't'), axis=1, tiled=True).reshape(width, hidden)]
    dot_general x35 -> x15, matrix products: 276 us -> 142 us  [dot(): lax.dot_general(a, b, (((ca,), (cb,)), ((), ())), preferred_element_type=...]
    unnamed x2 -> x0, blocking collectives: 81.5 us -> none
    ppermute x0 -> x4, waiting for transfers between devices: none -> 72.3 us  [the longest x2 46.1 us: to_sequence(): got = lax.ppermute(give, 'h', [(0, 1), (1, 0)])]
    psum x0 -> x1, blocking collectives: none -> 71.5 us  [per_device(): sums = lax.psum(sums, everywhere)[0]]
    all_to_all x0 -> x5, blocking collectives: none -> 71 us  [the longest x3 38.6 us: ffn_columns(): w = lax.all_to_all(w, 'dp', 0, 0, tiled=True)]
  transfers between devices with their start and end apart: 18 -> 24, of which waited for: 17 -> 18; matrix products, arithmetic and copies ran while one was open for 11% -> 18% of each run, Pallas kernels for 0% -> 2%
where the time goes in v1:
time: 1280 us; the launch traced here: 1270 us
  waiting for transfers between devices  715 us (56%)
  blocking collectives  184 us (14%)
  matrix products  142 us (11%)
  local copies, waits for them, and re-layouts  116 us (9%)
  other arithmetic  38.1 us (3%)
  Pallas kernels  31.5 us (2%)
  starting transfers between devices  28.9 us (2%)
  between operations  17.2 us (1%)
    dot_general x15, matrix products, dot(): lax.dot_general(a, b, (((ca,), (cb,)), ((), ())), preferred_element_type=...  142 us
    reduce_scatter x2, waiting for transfers between devices, ffn_owner(): lax.psum_scatter(g.astype(BF16).reshape(dp, ctx * depth, hidden), ('h', '...  122 us
    all_gather x3, waiting for transfers between devices, ffn_columns(): lax.all_gather(w, ('h', 't'), axis=1, tiled=True).reshape(width, hidden)  96.1 us
    reduce_scatter x2, waiting for transfers between devices, scatter_dp(): lax.psum_scatter(x.astype(BF16), 'dp', scatter_dimension=0, tiled=True)  93.5 us
    all_gather x2, waiting for transfers between devices, gather_dp(): return lax.all_gather(x, 'dp', axis=0, tiled=True)  81.2 us
    psum x1, blocking collectives, per_device(): sums = lax.psum(sums, everywhere)[0]  71.5 us
    all_gather x1, waiting for transfers between devices, per_device(): lax.all_gather(attn_set[:, :heads * HEAD_SET], ('dp', 'h'), axis=0, tiled...  61.8 us
    unnamed x18, waiting for transfers between devices  54.2 us
  transfers between devices with their start and end apart: 24, of which 18 were waited for; matrix products, arithmetic and copies ran while one was open for 18% of the time, Pallas kernels for 2%

profile of v1, /device:TPU:0, one launch (start us, length us, event | category | flops | bytes accessed | tf_op | source)
XLA Modules:
  0.0 1271.8 jit_solution(82712004906639625)
XLA Ops:
  15.4 23.2 %collective-permute-done = bf16[128,2048]{1,0:T(8,128)(2,1)S(1)} collective-permute-done((bf16[128,2048]{1,0:T(8,128)(2,1)S(1)}, bf16[128,2048]{1,0:T(8,128)(2,1)S(1)}, u32[]{:S(2)}, u32[]{:S(2)}) %collective-permute-start) | collective-permute-done | bytes 524320 | tf_op jit(solution)/shard_map/ppermute | solution.py:203
  41.0 17.8 %all_to_all.40 = bf16[4,64,1536]{2,1,0:T(8,128)(2,1)S(1)} all-to-all(bf16[4,64,1536]{2,1,0:T(8,128)(2,1)S(1)} %copy.92), channel_id=1, replica_groups=mesh['dp'=4,'h'=2,'t'=4] {'t'}, dimensions={0} | all-to-all | bytes 1572864 | tf_op jit(solution)/shard_map/all_to_all | solution.py:248
  60.8 41.2 %all-gather.1 = f32[32,1,384]{2,1,0:T(1,128)S(1)} all-gather(f32[1,1,384]{2,1,0:T(1,128)S(1)} %reshape.306), channel_id=2, replica_groups=mesh['dp'=4,'h'=2,'t'=4] {'dp','h','t'}, dimensions={0}, use_global_device_ids=true | all-gather | bytes 50688 | tf_op jit(solution)/shard_map/all_gather | solution.py:229
  110.9 61.8 %all-gather.14.cloned.1.call-done = bf16[2048,1024]{1,0:T(8,128)(2,1)} async-done(((bf16[256,1024]{1,0:T(8,128)(2,1)}), bf16[2048,1024]{1,0:T(8,128)(2,1)}) %all-gather.14.cloned.1.call-update) | async-done | bytes 4194320 | tf_op jit(solution)/shard_map/all_gather | solution.py:250
  196.0 32.3 %all-gather.16.cloned.1.call-done = bf16[2048,512]{1,0:T(8,128)(2,1)} async-done(((bf16[256,512]{1,0:T(8,128)(2,1)}), bf16[2048,512]{1,0:T(8,128)(2,1)}) %all-gather.16.cloned.1.call-update) | async-done | bytes 2097168 | tf_op jit(solution)/shard_map/all_gather | solution.py:251
  236.1 14.8 %all_to_all.41 = bf16[4,64,1536]{2,1,0:T(8,128)(2,1)S(1)} all-to-all(bf16[4,64,1536]{2,1,0:T(8,128)(2,1)S(1)} %copy.95), channel_id=1, replica_groups=mesh['dp'=4,'h'=2,'t'=4] {'dp'}, dimensions={0} | all-to-all | bytes 1572864 | tf_op jit(solution)/shard_map/all_to_all | solution.py:257
  285.2 16.5 %reduce-scatter.8.cloned.1.call-done = bf16[2,128,2048]{2,1,0:T(8,128)(2,1)} async-done(((bf16[2,512,2048]{2,1,0:T(8,128)(2,1)}), bf16[2,128,2048]{2,1,0:T(8,128)(2,1)}) %reduce-scatter.8.cloned.1.call-update) | async-done | bytes 1048592 | tf_op jit(solution)/shard_map/reduce_scatter | solution.py:208
  317.8 26.2 %collective-permute-done.1 = bf16[128,2048]{1,0:T(8,128)(2,1)} collective-permute-done((bf16[128,2048]{1,0:T(8,128)(2,1)}, bf16[128,2048]{1,0:T(8,128)(2,1)}, u32[]{:S(2)}, u32[]{:S(2)}) %collective-permute-start.1) | collective-permute-done | bytes 524320 | tf_op jit(solution)/shard_map/ppermute | solution.py:213
  367.4 37.8 %all-gather.22.cloned.1.call-done = bf16[4,512,1536]{2,0,1:T(4,128)(2,1)} async-done(((bf16[4,64,1536]{2,0,1:T(4,128)(2,1)}), bf16[4,512,1536]{2,0,1:T(4,128)(2,1)}) %all-gather.22.cloned.1.call-update) | async-done | bytes 6291472 | tf_op jit(solution)/shard_map/all_gather | solution.py:258
  411.8 58.2 %all-gather.24.cloned.1.call-done = bf16[4,512,1536]{2,0,1:T(4,128)(2,1)} async-done(((bf16[4,64,1536]{2,0,1:T(4,128)(2,1)}), bf16[4,512,1536]{2,0,1:T(4,128)(2,1)}) %all-gather.24.cloned.1.call-update) | async-done | bytes 6291472 | tf_op jit(solution)/shard_map/all_gather | solution.py:258
  476.7 47.1 %all-gather.18.cloned.1.call-done = bf16[1024,2048]{1,0:T(8,128)(2,1)} async-done(((bf16[256,2048]{1,0:T(8,128)(2,1)}), bf16[1024,2048]{1,0:T(8,128)(2,1)}) %all-gather.18.cloned.1.call-update) | async-done | bytes 4194320 | tf_op jit(solution)/shard_map/all_gather | solution.py:217
  544.4 34.0 %all-gather.26.cloned.1.call-done = bf16[1024,2048]{1,0:T(8,128)(2,1)} async-done(((bf16[256,2048]{1,0:T(8,128)(2,1)}), bf16[1024,2048]{1,0:T(8,128)(2,1)}) %all-gather.26.cloned.1.call-update) | async-done | bytes 4194320 | tf_op jit(solution)/shard_map/all_gather | solution.py:217
  578.4 15.8 %multiply_convert_fusion.1 = (bf16[1024,1536]{1,0:T(8,128)(2,1)S(1)}, bf16[1024,1536]{1,0:T(8,128)(2,1)S(1)}, bf16[1024,1536]{1,0:T(8,128)(2,1)}) fusion(f32[1024,1536]{1,0:T(8,128)} %fusion.17, f32[1024,1536]{1,0:T(8,128)} %fusion.18, bf16[1024,2048]{1,0:T(8,128)(2,1)} %all-gather.26.cloned.1.call-done, bf16[2048,1536]{1,0:T(8,128)(2,1)} %bitcast.134), kind=kOutput, calls=%fused_computation.10 | convolution fusion | flops 6466043904 | bytes 32505856 | tf_op jit(solution)/shard_map/dot_general | solution.py:35
  616.8 52.6 %reduce-scatter.12.cloned.1.call-done = bf16[256,2048]{1,0:T(8,128)(2,1)} async-done(((bf16[1024,2048]{1,0:T(8,128)(2,1)}), bf16[256,2048]{1,0:T(8,128)(2,1)}) %reduce-scatter.12.cloned.1.call-update) | async-done | bytes 1048592 | tf_op jit(solution)/shard_map/reduce_scatter | solution.py:220
  681.5 23.0 %collective-permute-done.2 = bf16[128,2048]{1,0:T(8,128)(2,1)S(1)} collective-permute-done((bf16[128,2048]{1,0:T(8,128)(2,1)S(1)}, bf16[128,2048]{1,0:T(8,128)(2,1)S(1)}, u32[]{:S(2)}, u32[]{:S(2)}) %collective-permute-start.2) | collective-permute-done | bytes 524320 | tf_op jit(solution)/shard_map/ppermute | solution.py:203
  771.5 18.9 %shard_map.221 = (bf16[1024,1024]{1,0:T(8,128)(2,1)S(1)}, f32[2,8,128]{2,1,0:T(8,128)S(1)}) custom-call(f32[1024,1024]{1,0:T(8,128)} %fusion.16.qkv_ref, bf16[1024,512]{1,0:T(8,128)(2,1)S(1)} %convolution_convert_fusion.7.dout_ref, f32[2,128]{1,0:T(2,128)S(1)} %copy-done.3, f32[1024,128]{1,0:T(8,128)S(1)} %get-tuple-element.51.cos_ref, ...), custom_call_target="tpu_custom_call" | custom-call | flops 5368709120 | bytes 8388608 | tf_op jit(solution)/shard_map/pallas_call | solution.py:151
  824.5 53.9 %all-reduce.3.cloned.1.call-done = bf16[4,512,1536]{2,0,1:T(4,128)(2,1)} async-done(((bf16[4,512,1536]{2,0,1:T(4,128)(2,1)}), bf16[4,512,1536]{2,0,1:T(4,128)(2,1)}) %all-reduce.3.cloned.1.call-update) | async-done | bytes 6291472
  879.9 14.6 %all_to_all.44 = bf16[4,64,1536]{2,1,0:T(8,128)(2,1)S(1)} all-to-all(bf16[4,64,1536]{2,1,0:T(8,128)(2,1)S(1)} %copy.115), channel_id=1, replica_groups=mesh['dp'=4,'h'=2,'t'=4] {'dp'}, dimensions={0} | all-to-all | bytes 1572864 | tf_op jit(solution)/shard_map/all_to_all | solution.py:264
  894.4 55.8 %reduce-scatter.18.cloned.1.call-done = bf16[4,64,1536]{2,1,0:T(8,128)(2,1)} async-done(((bf16[4,512,1536]{2,1,0:T(8,128)(2,1)}), bf16[4,64,1536]{2,1,0:T(8,128)(2,1)}) %reduce-scatter.18.cloned.1.call-update) | async-done | bytes 786448 | tf_op jit(solution)/shard_map/reduce_scatter | solution.py:261
  953.9 66.6 %reduce-scatter.20.cloned.1.call-done = bf16[4,64,1536]{2,1,0:T(8,128)(2,1)} async-done(((bf16[4,512,1536]{2,1,0:T(8,128)(2,1)}), bf16[4,64,1536]{2,1,0:T(8,128)(2,1)}) %reduce-scatter.20.cloned.1.call-update) | async-done | bytes 786448 | tf_op jit(solution)/shard_map/reduce_scatter | solution.py:261
  1034.8 29.1 %reduce-scatter.14.cloned.1.call-done = bf16[2,128,2048]{2,1,0:T(8,128)(2,1)} async-done(((bf16[2,512,2048]{2,1,0:T(8,128)(2,1)}), bf16[2,128,2048]{2,1,0:T(8,128)(2,1)}) %reduce-scatter.14.cloned.1.call-update) | async-done | bytes 1048592 | tf_op jit(solution)/shard_map/reduce_scatter | solution.py:208
  1067.7 71.5 %psum.7 = f32[1,4352]{1,0:T(1,128)S(1)} all-reduce(f32[1,4352]{1,0:T(1,128)S(1)} %pad_maximum_fusion.4), channel_id=1, replica_groups=mesh['dp'=4,'h'=2,'t'=4] {'dp','h','t'}, use_global_device_ids=true, to_apply=%region_12.13 | all-reduce | flops 4352 | bytes 34816 | tf_op jit(solution)/shard_map/psum | solution.py:321
  1141.7 49.1 %reduce-scatter.16.cloned.1.call-done = bf16[256,1536]{0,1:T(8,128)(2,1)} async-done(((bf16[2048,1536]{0,1:T(8,128)(2,1)}), bf16[256,1536]{0,1:T(8,128)(2,1)}) %reduce-scatter.16.cloned.1.call-update) | async-done | bytes 786448 | tf_op jit(solution)/shard_map/reduce_scatter | solution.py:328
  1204.5 40.9 %reduce-scatter.10.cloned.1.call-done = bf16[256,2048]{1,0:T(8,128)(2,1)} async-done(((bf16[1024,2048]{1,0:T(8,128)(2,1)}), bf16[256,2048]{1,0:T(8,128)(2,1)}) %reduce-scatter.10.cloned.1.call-update) | async-done | bytes 1048592 | tf_op jit(solution)/shard_map/reduce_scatter | solution.py:220
  (251 shorter events, 351.8 us)
Async XLA Ops:
  8.0 96.4 %all-gather.12.cloned.1.call-start = ((), (), s32[]{:S(2)}) async-start(), calls=%async_computation.15 | async-start | bytes 5242880 | tf_op jit(solution)/shard_map/all_gather | solution.py:205
  11.3 27.3 %collective-permute-start = (bf16[128,2048]{1,0:T(8,128)(2,1)S(1)}, bf16[128,2048]{1,0:T(8,128)(2,1)S(1)}, u32[]{:S(2)}, u32[]{:S(2)}) collective-permute-start(bf16[128,2048]{1,0:T(8,128)(2,1)S(1)} %get-tuple-element.42), channel_id=1, source_target_pairs={{0,4},{4,0},{1,5},{5,1},{2,6},{6,2},{3,7},{7,3},{8,12},{12,8},{9,1... | collective-permute-start | bytes 1572872 | tf_op jit(solution)/shard_map/ppermute | solution.py:203
  39.7 133.0 %all-gather.14.cloned.1.call-start = ((), (), s32[]{:S(2)}) async-start(), calls=%async_computation.16 | async-start | bytes 4718592 | tf_op jit(solution)/shard_map/all_gather | solution.py:250
  59.8 168.5 %all-gather.16.cloned.1.call-start = ((), (), s32[]{:S(2)}) async-start(), calls=%async_computation.17 | async-start | bytes 2359296 | tf_op jit(solution)/shard_map/all_gather | solution.py:251
  60.6 241.1 %reduce-scatter.8.cloned.1.call-start = ((), (), s32[]{:S(2)}) async-start(), calls=%async_computation.18 | async-start | bytes 5242880 | tf_op jit(solution)/shard_map/reduce_scatter | solution.py:208
  234.3 126.5 %all-gather.20.cloned.1.call-start = ((), (), s32[]{:S(2)}) async-start(), calls=%async_computation.20 | async-start | bytes 7077888 | tf_op jit(solution)/shard_map/all_gather | solution.py:258
  252.4 152.9 %all-gather.22.cloned.1.call-start = ((), (), s32[]{:S(2)}) async-start(), calls=%async_computation.21 | async-start | bytes 7077888 | tf_op jit(solution)/shard_map/all_gather | solution.py:258
  269.0 201.1 %all-gather.24.cloned.1.call-start = ((), (), s32[]{:S(2)}) async-start(), calls=%async_computation.22 | async-start | bytes 7077888 | tf_op jit(solution)/shard_map/all_gather | solution.py:258
  284.7 239.1 %all-gather.18.cloned.1.call-start = ((), (), s32[]{:S(2)}) async-start(), calls=%async_computation.19 | async-start | bytes 5242880 | tf_op jit(solution)/shard_map/all_gather | solution.py:217
  304.0 39.9 %collective-permute-start.1 = (bf16[128,2048]{1,0:T(8,128)(2,1)}, bf16[128,2048]{1,0:T(8,128)(2,1)}, u32[]{:S(2)}, u32[]{:S(2)}) collective-permute-start(bf16[128,2048]{1,0:T(8,128)(2,1)} %get-tuple-element.39), channel_id=1, source_target_pairs={{0,4},{4,0},{1,5},{5,1},{2,6},{6,2},{3,7},{7,3},{8,12},{12,8},{9,1... | collective-permute-start | bytes 1572872 | tf_op jit(solution)/shard_map/ppermute | solution.py:213
  357.7 220.7 %all-gather.26.cloned.1.call-start = ((), (), s32[]{:S(2)}) async-start(), calls=%async_computation.24 | async-start | bytes 5242880 | tf_op jit(solution)/shard_map/all_gather | solution.py:217
  360.6 308.7 %reduce-scatter.12.cloned.1.call-start = ((), (), s32[]{:S(2)}) async-start(), calls=%async_computation.25 | async-start | bytes 5242880 | tf_op jit(solution)/shard_map/reduce_scatter | solution.py:220
  616.7 148.7 %all-gather.28.cloned.1.call-start = ((), (), s32[]{:S(2)}) async-start(), calls=%async_computation.26 | async-start | bytes 5242880 | tf_op jit(solution)/shard_map/all_gather | solution.py:205
  678.7 25.8 %collective-permute-start.2 = (bf16[128,2048]{1,0:T(8,128)(2,1)S(1)}, bf16[128,2048]{1,0:T(8,128)(2,1)S(1)}, u32[]{:S(2)}, u32[]{:S(2)}) collective-permute-start(bf16[128,2048]{1,0:T(8,128)(2,1)S(1)} %bitcast.160), channel_id=1, source_target_pairs={{0,4},{4,0},{1,5},{5,1},{2,6},{6,2},{3,7},{7,3},{8,12},{12,8},{9,1... | collective-permute-start | bytes 1572872 | tf_op jit(solution)/shard_map/ppermute | solution.py:203
  705.7 172.7 %all-reduce.3.cloned.1.call-start = ((), (), s32[]{:S(2)}) async-start(), calls=%async_computation.31 | async-start | bytes 12582912
  741.5 208.7 %reduce-scatter.18.cloned.1.call-start = ((), (), s32[]{:S(2)}) async-start(), calls=%async_computation.29 | async-start | bytes 7077888 | tf_op jit(solution)/shard_map/reduce_scatter | solution.py:261
  753.7 266.8 %reduce-scatter.20.cloned.1.call-start = ((), (), s32[]{:S(2)}) async-start(), calls=%async_computation.30 | async-start | bytes 7077888 | tf_op jit(solution)/shard_map/reduce_scatter | solution.py:261
  765.3 298.6 %reduce-scatter.14.cloned.1.call-start = ((), (), s32[]{:S(2)}) async-start(), calls=%async_computation.27 | async-start | bytes 5242880 | tf_op jit(solution)/shard_map/reduce_scatter | solution.py:208
  796.7 394.1 %reduce-scatter.16.cloned.1.call-start = ((), (), s32[]{:S(2)}) async-start(), calls=%async_computation.28 | async-start | bytes 7077888 | tf_op jit(solution)/shard_map/reduce_scatter | solution.py:328
  811.4 434.0 %reduce-scatter.10.cloned.1.call-start = ((), (), s32[]{:S(2)}) async-start(), calls=%async_computation.23 | async-start | bytes 5242880 | tf_op jit(solution)/shard_map/reduce_scatter | solution.py:220
  950.2 70.3 %all-to-all-start.5 = ((bf16[4,64,1536]{2,1,0:T(8,128)(2,1)}), bf16[4,64,1536]{2,1,0:T(8,128)(2,1)S(1)}, u32[]{:S(2)}, u32[]{:S(2)}) async-start(bf16[4,64,1536]{2,1,0:T(8,128)(2,1)} %reduce-scatter.18.cloned.1.call-done), calls=%async_computation.11 | async-start | bytes 1572864 | tf_op jit(solution)/shard_map/all_to_all | solution.py:264
  1020.5 12.8 %all-to-all-start.6 = ((bf16[4,64,1536]{2,1,0:T(8,128)(2,1)}), bf16[4,64,1536]{2,1,0:T(8,128)(2,1)S(1)}, u32[]{:S(2)}, u32[]{:S(2)}) async-start(bf16[4,64,1536]{2,1,0:T(8,128)(2,1)} %reduce-scatter.20.cloned.1.call-done), calls=%async_computation.13 | async-start | bytes 1572864 | tf_op jit(solution)/shard_map/all_to_all | solution.py:264
  1065.2 75.1 %collective-permute-start.3 = (bf16[128,2048]{1,0:T(8,128)(2,1)S(1)}, bf16[128,2048]{1,0:T(8,128)(2,1)S(1)}, u32[]{:S(2)}, u32[]{:S(2)}) collective-permute-start(bf16[128,2048]{1,0:T(8,128)(2,1)S(1)} %get-tuple-element.34), channel_id=1, source_target_pairs={{0,4},{4,0},{1,5},{5,1},{2,6},{6,2},{3,7},{7,3},{8,12},{12,8},{9,1... | collective-permute-start | bytes 1572872 | tf_op jit(solution)/shard_map/ppermute | solution.py:213
  1193.1 62.9 %all-to-all-start.4 = ((bf16[4,64,1536]{2,1,0:T(8,128)(2,1)}), bf16[4,64,1536]{2,1,0:T(8,128)(2,1)}, u32[]{:S(2)}, u32[]{:S(2)}) async-start(bf16[4,64,1536]{2,1,0:T(8,128)(2,1)} %bitcast.32), calls=%async_computation.9 | async-start | bytes 1572864 | tf_op jit(solution)/shard_map/all_to_all | solution.py:329
  (38 other events, 1231.8 us)
Sparse Core Ops, SparseCore 0:
  39.8 49.4 all-gather.11
  92.1 80.5 all-gather.13
  175.5 52.6 all-gather.15
  234.4 67.3 reduce-scatter.7
  705.8 43.4 all-gather.27
Sparse Core Ops, SparseCore 1:
  252.5 82.4 all-gather.19
  337.0 68.2 all-gather.21
  406.8 63.2 all-gather.23
  472.6 51.2 all-gather.17
  525.9 52.5 all-gather.25
  616.8 52.5 reduce-scatter.11
  741.6 136.7 all-reduce.2
  880.5 69.7 reduce-scatter.17
  952.4 68.0 reduce-scatter.19
  1022.8 41.1 reduce-scatter.13
  1068.3 122.4 reduce-scatter.15
  1193.8 51.5 reduce-scatter.9

commit v2 on v1

v2 whole, which is shorter than its diff:
```python
import functools

import jax
import jax.numpy as jnp
from jax import lax
from jax.experimental import pallas as pl
from jax.experimental.pallas import tpu as pltpu
from jax.sharding import Mesh
from jax.sharding import PartitionSpec as P

QUERY_HEADS = 16
KEY_VALUE_HEADS = 8
HEAD_DIMENSION = 128
GROUP = QUERY_HEADS // KEY_VALUE_HEADS
HEAD_SET = (GROUP + 2) * HEAD_DIMENSION

epsilon = 1e-06
theta_base = 1000000.0
score_scaling = HEAD_DIMENSION ** (-0.5)
F32 = jnp.float32
BF16 = jnp.bfloat16


def norm_factor(matrix):
    return lax.rsqrt(jnp.mean(matrix * matrix, axis=-1, keepdims=True) + epsilon)


def norm_back(matrix, factor, upstream):
    return factor * upstream - matrix * (factor * factor * factor) * jnp.mean(
        upstream * matrix, axis=-1, keepdims=True
    )


def dot(a, b, ca=1, cb=0):
    return lax.dot_general(a, b, (((ca,), (cb,)), ((), ())), preferred_element_type=F32)


F_AFTER_W = True
PRE_LATE = True
CHEAP = pl.CostEstimate(flops=1 << 20, bytes_accessed=1 << 16, transcendentals=0)


def rows_kernel(contract, a_ref, b_ref, *out_refs):
    out = dot(a_ref[...], b_ref[...], 1, contract).astype(out_refs[0].dtype)
    step = out_refs[0].shape[0]
    for k, out_ref in enumerate(out_refs):
        out_ref[...] = out[k * step : (k + 1) * step]


def rows_product(a, b, contract, tile, dtype, pieces=1):
    rows, depth = a.shape
    columns = b.shape[1 - contract]
    tile = min(tile, columns)
    out = pl.pallas_call(
        functools.partial(rows_kernel, contract),
        grid=(columns // tile,),
        in_specs=[
            pl.BlockSpec((rows, depth), lambda j: (0, 0)),
            pl.BlockSpec((depth, tile), lambda j: (0, j))
            if contract == 0
            else pl.BlockSpec((tile, depth), lambda j: (j, 0)),
        ],
        out_specs=[pl.BlockSpec((rows // pieces, tile), lambda j: (0, j))] * pieces,
        out_shape=[jax.ShapeDtypeStruct((rows // pieces, columns), dtype)] * pieces,
        compiler_params=pltpu.CompilerParams(vmem_limit_bytes=48 << 20),
        cost_estimate=CHEAP,
    )(a, b)
    return out if pieces > 1 else out[0]


def term_kernel(a_ref, b_ref, out_ref):
    out_ref[...] = dot(a_ref[...], b_ref[...], 0, 0).astype(BF16).reshape(out_ref.shape)


def term_product(a, b, groups, blocks):
    rows, width = a.shape
    columns = b.shape[1]
    depth = width // (groups * blocks)
    return pl.pallas_call(
        term_kernel,
        grid=(groups,),
        in_specs=[
            pl.BlockSpec((rows, blocks * depth), lambda i: (0, i)),
            pl.BlockSpec((rows, columns), lambda i: (0, 0)),
        ],
        out_specs=pl.BlockSpec((blocks, 1, depth, columns), lambda i: (0, i, 0, 0)),
        out_shape=jax.ShapeDtypeStruct((blocks, groups, depth, columns), BF16),
        compiler_params=pltpu.CompilerParams(vmem_limit_bytes=56 << 20),
        cost_estimate=CHEAP,
    )(a, b).reshape(width, columns)


def pieces_kernel(me_ref, a_ref, b_ref, *refs):
    norm_ref, out_refs = (refs[0], refs[1:]) if refs[0].shape[0] == 8 else (None, refs)
    wide = b_ref.shape[1]
    part = dot(a_ref[...], b_ref[...], 0, 0).astype(BF16)
    for s, out_ref in enumerate(out_refs):

        @pl.when(pl.program_id(0) == s)
        def _():
            out_ref[:, :wide] = part
            if norm_ref is not None:
                sums = norm_ref[...].T
                rest = jnp.zeros((sums.shape[0], HEAD_DIMENSION - 8), F32)
                out_ref[:, wide:] = jnp.concatenate([sums, rest], axis=1).astype(BF16)


def term_pieces(a, b, me, count, norms=None):
    rows, width = a.shape
    columns = b.shape[1]
    step = width // count
    extra = 0 if norms is None else HEAD_DIMENSION
    in_specs = [
        pl.BlockSpec((rows, step), lambda i, me: (0, me[0] ^ i)),
        pl.BlockSpec((rows, columns), lambda i, me: (0, 0)),
    ]
    if norms is not None:
        in_specs.append(pl.BlockSpec((8, step), lambda i, me: (0, me[0] ^ i)))
    return pl.pallas_call(
        pieces_kernel,
        grid_spec=pltpu.PrefetchScalarGridSpec(
            num_scalar_prefetch=1,
            grid=(count,),
            in_specs=in_specs,
            out_specs=[pl.BlockSpec((step, columns + extra), lambda i, me: (0, 0))] * count,
        ),
        out_shape=[jax.ShapeDtypeStruct((step, columns + extra), BF16)] * count,
        compiler_params=pltpu.CompilerParams(vmem_limit_bytes=56 << 20),
        cost_estimate=CHEAP,
    )(me.reshape(1).astype(jnp.int32), a, b, *([] if norms is None else [norms]))


def input_kernel(grad_ref, weight_ref, normed_ref, other_ref, out_ref, sum_ref):
    part = dot(grad_ref[...], weight_ref[...], 1, 1)
    out_ref[...] = part.astype(BF16)
    sum_ref[...] = jnp.zeros_like(sum_ref)
    sum_ref[0:1] = jnp.sum(normed_ref[...].astype(F32) * part, axis=0, keepdims=True)
    sum_ref[1:2] = other_ref[...]


def input_product(grad, weight, normed, other, tile):
    rows, depth = grad.shape
    columns = weight.shape[0]
    return pl.pallas_call(
        input_kernel,
        grid=(columns // tile,),
        in_specs=[
            pl.BlockSpec((rows, depth), lambda j: (0, 0)),
            pl.BlockSpec((tile, depth), lambda j: (j, 0)),
            pl.BlockSpec((rows, tile), lambda j: (0, j)),
            pl.BlockSpec((1, tile), lambda j: (0, j)),
        ],
        out_specs=[pl.BlockSpec((rows, tile), lambda j: (0, j)), pl.BlockSpec((8, tile), lambda j: (0, j))],
        out_shape=[jax.ShapeDtypeStruct((rows, columns), BF16), jax.ShapeDtypeStruct((8, columns), F32)],
        compiler_params=pltpu.CompilerParams(vmem_limit_bytes=48 << 20),
        cost_estimate=CHEAP,
    )(grad, weight, normed, other)


def whole(kernel, shapes, me, *arrays):
    vmem = pl.BlockSpec(memory_space=pltpu.VMEM)
    return pl.pallas_call(
        kernel,
        in_specs=[pl.BlockSpec(memory_space=pltpu.SMEM)] + [vmem] * len(arrays),
        out_specs=[vmem] * len(shapes),
        out_shape=shapes,
        compiler_params=pltpu.CompilerParams(vmem_limit_bytes=48 << 20),
        cost_estimate=CHEAP,
    )(me.reshape(1).astype(jnp.int32), *arrays)


def lanes(index, size):
    return pl.ds(pl.multiple_of(index * size, HEAD_DIMENSION), size)


def attn_split_kernel(heads, me_ref, gain_ref, q_ref, k_ref, v_ref, o_ref, *out_refs):
    pair = GROUP * HEAD_DIMENSION
    gain = gain_ref[...]

    def scaled(ref, index, size):
        return (ref[:, lanes(index, size)].astype(F32) * gain).astype(BF16)

    for s, out_ref in enumerate(out_refs):
        part = me_ref[0] ^ s
        for n in range(heads):
            head, at = part * heads + n, n * HEAD_SET
            out_ref[:, at : at + pair] = scaled(q_ref, head, pair)
            out_ref[:, at + pair : at + pair + HEAD_DIMENSION] = scaled(k_ref, head, HEAD_DIMENSION)
            out_ref[:, at + pair + HEAD_DIMENSION : at + HEAD_SET] = scaled(v_ref, head, HEAD_DIMENSION)
        out_ref[:, heads * HEAD_SET :] = o_ref[:, lanes(part, heads * pair)]


def attn_join_kernel(heads, me_ref, gain_ref, *refs):
    count = len(refs) - 5
    q_ref, k_ref, v_ref, o_ref, norm_ref = refs[count:]
    pair = GROUP * HEAD_DIMENSION
    gain = gain_ref[...]
    norms = jnp.zeros(norm_ref.shape, F32)
    for s, got_ref in enumerate(refs[:count]):
        part = me_ref[0] ^ s
        for n in range(heads):
            head, at = part * heads + n, n * HEAD_SET
            q_ref[:, lanes(head, pair)] = got_ref[:, at : at + pair].astype(F32) * gain
            k_ref[:, lanes(head, HEAD_DIMENSION)] = (
                got_ref[:, at + pair : at + pair + HEAD_DIMENSION].astype(F32) * gain
            )
            v_ref[:, lanes(head, HEAD_DIMENSION)] = (
                got_ref[:, at + pair + HEAD_DIMENSION : at + HEAD_SET].astype(F32) * gain
            )
        norms += got_ref[:, heads * HEAD_SET : heads * HEAD_SET + HEAD_DIMENSION].astype(F32)
        o_ref[:, lanes(part, heads * pair)] = got_ref[:, heads * HEAD_SET + HEAD_DIMENSION :].astype(F32)
    norm_ref[...] = norms


def ffn_split_kernel(tiles, me_ref, gain_ref, gate_ref, up_ref, down_ref, *out_refs):
    gain = gain_ref[...]
    hidden = out_refs[0].shape[1] // 3
    tile = hidden // tiles
    for s, out_ref in enumerate(out_refs):
        part = me_ref[0] ^ s
        for n in range(tiles):
            for k, ref in enumerate((gate_ref, up_ref)):
                at = (2 * n + k) * tile
                out_ref[:, at : at + tile] = (ref[:, lanes(part * tiles + n, tile)].astype(F32) * gain).astype(
                    BF16
                )
        out_ref[:, 2 * hidden :] = down_ref[:, lanes(part, hidden)]


def ffn_join_kernel(tiles, me_ref, gain_ref, *refs):
    count = len(refs) - 3
    gate_ref, up_ref, down_ref = refs[count:]
    gain = gain_ref[...]
    hidden = refs[0].shape[1] // 3
    tile = hidden // tiles
    for s, got_ref in enumerate(refs[:count]):
        part = me_ref[0] ^ s
        for n in range(tiles):
            for k, ref in enumerate((gate_ref, up_ref)):
                at = (2 * n + k) * tile
                ref[:, lanes(part * tiles + n, tile)] = got_ref[:, at : at + tile].astype(F32) * gain
        down_ref[:, lanes(part, hidden)] = got_ref[:, 2 * hidden :].astype(F32)


def rows_join_kernel(me_ref, *refs):
    first_ref, second_ref = refs[-2:]
    depth = refs[0].shape[0]
    wide = first_ref.shape[1]
    for s, got_ref in enumerate(refs[:-2]):
        rows = pl.ds(pl.multiple_of((me_ref[0] ^ s) * depth, depth), depth)
        first_ref[rows] = got_ref[:, :wide]
        second_ref[rows] = got_ref[:, wide:]


def rows_join(got, wide, me):
    depth, width = got[0].shape
    return whole(
        rows_join_kernel,
        [jax.ShapeDtypeStruct((len(got) * depth, n), BF16) for n in (wide, width - wide)],
        me,
        *got,
    )


def rotate(x, cos, sin):
    return x * cos + pltpu.roll(x, HEAD_DIMENSION // 2, 1) * sin


def head_slice(i):
    return slice(i * HEAD_DIMENSION, (i + 1) * HEAD_DIMENSION)


def normed_rotated(raw, gain, cos, sin):
    return rotate(raw * norm_factor(raw) * gain, cos, sin).astype(BF16)


def probabilities(keys, queries, first_query, earliest):
    scores = dot(keys, queries, 1, 1) * score_scaling
    key_index = lax.broadcasted_iota(jnp.int32, scores.shape, 0)
    query_index = lax.broadcasted_iota(jnp.int32, scores.shape, 1) + first_query
    allowed = (key_index <= query_index) & (key_index >= earliest)
    masked = jnp.where(allowed, scores, -1e30)
    shifted = jnp.exp(masked - jnp.max(masked, axis=0, keepdims=True))
    return shifted * (1.0 / jnp.sum(shifted, axis=0, keepdims=True))


def forward_kernel(block, qkv_ref, gain_ref, cos_ref, sin_ref, early_ref, out_ref):
    length = qkv_ref.shape[0]
    gains = gain_ref[...]
    cos, sin = cos_ref[...], sin_ref[...]
    keys = normed_rotated(qkv_ref[:, head_slice(GROUP)], gains[1:2], cos, sin)
    values_t = qkv_ref[:, head_slice(GROUP + 1)].T.astype(BF16)
    for i in range(length // block):
        rows = slice(i * block, (i + 1) * block)
        seen = (i + 1) * block
        for g in range(GROUP):
            queries = normed_rotated(qkv_ref[rows, head_slice(g)], gains[0:1], cos[rows], sin[rows])
            probs = probabilities(keys[:seen], queries, i * block, early_ref[0:1, rows]).astype(BF16)
            mixed = dot(values_t[:, :seen], probs)
            out_ref[rows, head_slice(g)] = mixed.T.astype(BF16)


def backward_kernel(
    block, qkv_ref, dout_ref, gain_ref, cos_ref, sin_ref, early_ref, dqkv_ref, dgain_ref, dkey_ref, dvalue_ref
):
    length = qkv_ref.shape[0]
    gains = gain_ref[...]
    cos, sin = cos_ref[...], sin_ref[...]
    key_raw = qkv_ref[:, head_slice(GROUP)]
    keys = normed_rotated(key_raw, gains[1:2], cos, sin)
    keys_t = keys.astype(F32).T.astype(BF16)
    values = qkv_ref[:, head_slice(GROUP + 1)].astype(BF16)
    dkey_ref[...] = jnp.zeros_like(dkey_ref)
    dvalue_ref[...] = jnp.zeros_like(dvalue_ref)
    query_gain_sum = jnp.zeros((1, HEAD_DIMENSION), F32)
    for i in range(length // block):
        rows = slice(i * block, (i + 1) * block)
        seen = (i + 1) * block
        for g in range(GROUP):
            query_raw = qkv_ref[rows, head_slice(g)]
            queries = normed_rotated(query_raw, gains[0:1], cos[rows], sin[rows])
            dout = dout_ref[rows, head_slice(g)]
            probs = probabilities(keys[:seen], queries, i * block, early_ref[0:1, rows])
            dprobs = dot(values[:seen], dout, 1, 1)
            delta = jnp.sum(probs * dprobs, axis=0, keepdims=True)
            dscores = (probs * (dprobs - delta)).astype(BF16)
            dkey_ref[:seen] += dot(dscores, queries)
            dvalue_ref[:seen] += dot(probs.astype(BF16), dout)
            dquery = dot(keys_t[:, :seen], dscores).T * score_scaling
            dquery = rotate(dquery, cos[rows], -sin[rows])
            factor = norm_factor(query_raw)
            query_gain_sum += jnp.sum(query_raw * factor * dquery, axis=0, keepdims=True)
            dqkv_ref[rows, head_slice(g)] = norm_back(query_raw, factor, dquery * gains[0:1]).astype(BF16)
    dkey = rotate(dkey_ref[...] * score_scaling, cos, -sin)
    factor = norm_factor(key_raw)
    dgain_ref[0, 0:1, :] = query_gain_sum
    dgain_ref[0, 1:2, :] = jnp.sum(key_raw * factor * dkey, axis=0, keepdims=True)
    dgain_ref[0, 2:, :] = jnp.zeros((6, HEAD_DIMENSION), F32)
    dqkv_ref[:, head_slice(GROUP)] = norm_back(key_raw, factor, dkey * gains[1:2]).astype(BF16)
    dqkv_ref[:, head_slice(GROUP + 1)] = dvalue_ref[...].astype(BF16)


def per_head_specs(length):
    whole = lambda shape: pl.BlockSpec(shape, lambda n: (0,) * len(shape))
    return [
        whole((2, HEAD_DIMENSION)),
        whole((length, HEAD_DIMENSION)),
        whole((length, HEAD_DIMENSION)),
        whole((8, length)),
    ]


def columns_spec(length, width):
    return pl.BlockSpec((length, width), lambda n: (0, n))


def attention_forward(qkv, gains, cos, sin, earliest):
    length, width = qkv.shape
    heads = width // HEAD_SET
    return pl.pallas_call(
        functools.partial(forward_kernel, 256),
        grid=(heads,),
        in_specs=[columns_spec(length, HEAD_SET)] + per_head_specs(length),
        out_specs=columns_spec(length, GROUP * HEAD_DIMENSION),
        out_shape=jax.ShapeDtypeStruct((length, heads * GROUP * HEAD_DIMENSION), BF16),
        compiler_params=pltpu.CompilerParams(vmem_limit_bytes=48 << 20),
        cost_estimate=CHEAP,
    )(qkv, gains, cos, sin, earliest)


def attention_backward(qkv, dout, gains, cos, sin, earliest):
    length, width = qkv.shape
    heads = width // HEAD_SET
    return pl.pallas_call(
        functools.partial(backward_kernel, 256),
        grid=(heads,),
        in_specs=[columns_spec(length, HEAD_SET), columns_spec(length, GROUP * HEAD_DIMENSION)]
        + per_head_specs(length),
        out_specs=[
            columns_spec(length, HEAD_SET),
            pl.BlockSpec((1, 8, HEAD_DIMENSION), lambda n: (n, 0, 0)),
        ],
        out_shape=[
            jax.ShapeDtypeStruct((length, width), BF16),
            jax.ShapeDtypeStruct((heads, 8, HEAD_DIMENSION), F32),
        ],
        scratch_shapes=[pltpu.VMEM((length, HEAD_DIMENSION), F32)] * 2,
        compiler_params=pltpu.CompilerParams(vmem_limit_bytes=48 << 20),
        cost_estimate=CHEAP,
    )(qkv, dout, gains, cos, sin, earliest)


def hidden_kernel(pre_ref, grad_ref, down_ref, hidden_ref, dpre_ref):
    tile = hidden_ref.shape[1]
    grad_hidden = dot(grad_ref[...], down_ref[...])
    step = 128
    for start in range(0, hidden_ref.shape[0], step):
        rows = slice(start, start + step)
        gate, up, grad = pre_ref[rows, :tile], pre_ref[rows, tile:], grad_hidden[rows]
        sig = 1.0 / (1.0 + jnp.exp(-gate))
        act = gate * sig
        hidden_ref[rows] = (act * up).astype(BF16)
        dpre_ref[rows, :tile] = (grad * up * sig * (1.0 + gate * (1.0 - sig))).astype(BF16)
        dpre_ref[rows, tile:] = (grad * act).astype(BF16)


def hidden_layer(pre, grad, down, tiles):
    rows, width = grad.shape
    tile = down.shape[1] // tiles
    step = min(rows, 1024)
    return pl.pallas_call(
        hidden_kernel,
        grid=(tiles, rows // step),
        in_specs=[
            pl.BlockSpec((step, 2 * tile), lambda j, i: (i, j)),
            pl.BlockSpec((step, width), lambda j, i: (i, 0)),
            pl.BlockSpec((width, tile), lambda j, i: (0, j)),
        ],
        out_specs=[
            pl.BlockSpec((step, tile), lambda j, i: (i, j)),
            pl.BlockSpec((step, 2 * tile), lambda j, i: (i, j)),
        ],
        out_shape=[
            jax.ShapeDtypeStruct((rows, tile * tiles), BF16),
            jax.ShapeDtypeStruct((rows, 2 * tile * tiles), BF16),
        ],
        compiler_params=pltpu.CompilerParams(vmem_limit_bytes=56 << 20),
        cost_estimate=CHEAP,
    )(pre, grad, down)


def tie(*items):
    return lax.optimization_barrier(items)


def swap(x, axis, bit):
    return lax.ppermute(x, axis, [(i, i ^ bit) for i in range(lax.axis_size(axis))])


def to_sequence(blocks):
    half, part, parts = lax.axis_index("h"), lax.axis_index("t"), lax.axis_size("t")
    block = blocks.shape[1]
    own = lax.dynamic_index_in_dim(blocks, half, 0, keepdims=False)
    got = swap(lax.dynamic_index_in_dim(blocks, 1 - half, 0, keepdims=False), "h", 1)
    placed = []
    for first, start in ((own, 0), (got, parts)):
        held, keys = [first[None]], [start]
        bit = parts // 2
        while bit:
            held.append(swap(jnp.concatenate(held, axis=0), "t", bit))
            keys += [k | bit for k in keys]
            bit //= 2
        flat = [piece[i] for piece in held for i in range(piece.shape[0])]
        placed += [(b, ((half * parts + part) ^ k) * block) for b, k in zip(flat, keys)]
    return placed


def assemble(placed, columns=slice(None), out=None):
    rows = sum(part.shape[0] for part, _ in placed)
    if out is None:
        out = jnp.zeros((rows, placed[0][0][:, columns].shape[1]), placed[0][0].dtype)
    for part, start in placed:
        out = lax.dynamic_update_slice_in_dim(out, part[:, columns], start, 0)
    return out


def to_blocks(partial):
    half, part, parts = lax.axis_index("h"), lax.axis_index("t"), lax.axis_size("t")
    both = partial.reshape(2, parts, -1, partial.shape[1])
    held = [lax.dynamic_index_in_dim(both, part ^ key, 1, keepdims=False) for key in range(parts)]

    def pick(x, h):
        return lax.dynamic_index_in_dim(x, h, 0, keepdims=False)

    bit = 1
    while 2 * bit < parts:
        got = {key: swap(held[key].astype(BF16), "t", bit) for key in reversed(range(parts)) if held[key] is not None and key & bit}
        for key, value in got.items():
            held[key ^ bit] = held[key ^ bit].astype(F32) + value.astype(F32)
            held[key] = None
        bit *= 2
    far = pick(held[0], 1 - half).astype(F32) + swap(pick(held[bit], 1 - half).astype(BF16), "t", bit).astype(F32)
    got = swap(far.astype(BF16), "h", 1).astype(F32)
    own = pick(held[0], half).astype(F32) + swap(pick(held[bit], half).astype(BF16), "t", bit).astype(F32)
    return jnp.where(half == 0, jnp.stack([own, got]), jnp.stack([got, own]))


def swaps(pieces, axis="dp"):
    return [pieces[0]] + list(reversed([swap(pieces[s], axis, s) for s in reversed(range(1, len(pieces)))]))


def gather_h(x):
    return [x, swap(x, "h", 1)]


def place_rows(blocks):
    dp, half = lax.axis_index("dp"), lax.axis_index("h")
    count, (rows, width) = lax.axis_size("dp"), blocks[0][0].shape
    out = jnp.zeros((count * 2 * rows, width), blocks[0][0].dtype)
    for k, parts in enumerate(blocks):
        for s, part in enumerate(parts):
            out = lax.dynamic_update_slice_in_dim(out, part, ((dp ^ s) * 2 + (half ^ k)) * rows, 0)
    return out


def sum_h(got):
    half = lax.axis_index("h")
    total = sum(g.astype(F32) for g in got)
    total = total.reshape(2, total.shape[0] // 2, -1)
    give = lax.dynamic_index_in_dim(total, 1 - half, 0, keepdims=False).astype(BF16)
    return lax.dynamic_index_in_dim(total, half, 0, keepdims=False), give


def total_over(x, axis):
    bit = 1
    while bit < lax.axis_size(axis):
        x = x + swap(x, axis, bit)
        bit *= 2
    return x


def per_device(
    tokens,
    positions,
    attn_norm,
    query_proj,
    key_projected,
    value_projected,
    head_norms,
    out_proj,
    mlp_norm,
    gate_proj,
    up_proj,
    down_proj,
    out_grad,
):
    block, seqs, width = tokens.shape
    rows = block * seqs
    dp = lax.axis_size("dp")
    parts = lax.axis_size("t")
    ctx = 2 * parts
    length = block * ctx
    depth = query_proj.shape[0]
    part = lax.axis_index("t")
    attn_gain = attn_norm.astype(F32)[:, None]
    mlp_gain = mlp_norm.astype(F32)[:, None]

    inputs = jnp.transpose(tokens, (1, 0, 2)).astype(F32)
    factor_one = norm_factor(inputs)
    digits = jnp.stack([positions.T // 16, positions.T % 16], axis=2).astype(BF16)
    digits = jnp.pad(digits, ((0, 0), (0, 0), (0, HEAD_DIMENSION - 2)))
    placed = to_sequence(jnp.concatenate([(inputs * factor_one).astype(BF16), digits], axis=2))
    normed_one = assemble(placed, slice(0, width))
    places = assemble(placed, slice(width, width + HEAD_DIMENSION))[:, :2].astype(jnp.int32)
    places = places[:, 0] * 16 + places[:, 1]

    heads = KEY_VALUE_HEADS // parts
    pair = GROUP * HEAD_DIMENSION
    qkv_width, mix_width = heads * HEAD_SET, heads * pair
    attn_width = qkv_width + mix_width

    dp_index = lax.axis_index("dp")
    attn_set = whole(
        functools.partial(attn_split_kernel, heads),
        [jax.ShapeDtypeStruct((depth, attn_width), BF16)] * parts,
        part,
        attn_gain,
        query_proj,
        key_projected,
        value_projected,
        out_proj,
    )
    attn_set, gate_proj = tie(attn_set, gate_proj)
    qkv_rows, out_rows = rows_join(swaps(attn_set, "t"), qkv_width, part)

    hidden = gate_proj.shape[1] // dp
    tiles = 3
    ffn_set = whole(
        functools.partial(ffn_split_kernel, tiles),
        [jax.ShapeDtypeStruct((depth, 3 * hidden), BF16)] * dp,
        dp_index,
        mlp_gain,
        gate_proj,
        up_proj,
        down_proj,
    )

    qkv_blocks = gather_h(qkv_rows)
    qkv_own = swaps([qkv_blocks[0]] * dp)
    if F_AFTER_W:
        qkv_own, ffn_set = tie(qkv_own, ffn_set)
    ffn_got = swaps(ffn_set)
    qkv_weight = place_rows([qkv_own, swaps([qkv_blocks[1]] * dp)])
    pre_rows, down_rows = rows_join(ffn_got, 2 * hidden, dp_index)
    pre_rows, normed_one = tie(pre_rows, normed_one)

    def ffn_gather(x):
        return lax.all_gather(x, ("h", "t"), axis=0, tiled=False)

    def ordered(w):
        return jnp.transpose(w.reshape(ctx, dp, depth, -1), (1, 0, 2, 3)).reshape(width, -1)

    pre_all = ffn_gather(pre_rows)

    def ffn_scatter(term):
        return lax.psum_scatter(term, ("h", "t"), scatter_dimension=0, tiled=True).reshape(dp, depth, -1)

    gains = head_norms.astype(F32)
    half_width = HEAD_DIMENSION // 2
    frequency = theta_base ** (-(jnp.arange(half_width, dtype=F32) * 2.0 / HEAD_DIMENSION))
    angles = places.astype(F32)[:, None] * frequency
    cos, sin = jnp.cos(angles), jnp.sin(angles)
    cos = jnp.concatenate([cos, cos], axis=1)
    sin = jnp.concatenate([-sin, sin], axis=1)
    earliest = jnp.broadcast_to((jnp.arange(length, dtype=jnp.int32) - places)[None, :], (8, length))
    out_rows, normed_one = tie(out_rows, normed_one)
    out_blocks = gather_h(out_rows)
    qkv = rows_product(normed_one, qkv_weight, 0, 256, F32)
    out_blocks, qkv = tie(out_blocks, qkv)
    out_weight = place_rows([swaps([b] * dp) for b in out_blocks])
    mixed = attention_forward(qkv, gains, cos, sin, earliest)
    grad_own = jnp.transpose(out_grad, (1, 0, 2)).reshape(rows, width)
    out_weight, mixed, grad_own = tie(out_weight, mixed, grad_own)
    grad_rows = swaps([grad_own] * dp)
    mixed_sum = to_blocks(rows_product(mixed, out_weight, 1, 512, BF16))
    middle = (inputs + mixed_sum).reshape(rows, width)
    pre_all, down_rows, middle = tie(pre_all, down_rows, middle)
    pre_weight, down_weight = ordered(pre_all), ordered(ffn_gather(down_rows))

    factor_two = norm_factor(middle)
    own_two = (middle * factor_two).astype(BF16)
    grad_rows, own_two = tie(grad_rows, own_two)
    grad_rows = jnp.concatenate(grad_rows, axis=0)
    normed_two = jnp.concatenate(swaps([own_two] * dp), axis=0)
    pre = rows_product(normed_two, pre_weight, 0, hidden // 2, F32)
    hidden_low, grad_pre = hidden_layer(pre, grad_rows, down_weight, tiles)
    down_term = term_product(grad_rows, hidden_low, dp, ctx)
    down_term, grad_pre = tie(down_term, grad_pre)
    down_sum = ffn_scatter(down_term)
    two_part = rows_product(grad_pre, pre_weight, 1, 512, BF16, dp)
    grad_pre, two_part = tie(grad_pre, two_part)
    two_got = swaps(two_part)
    pre_term = term_product(normed_two, grad_pre, dp, ctx)
    pre_term, two_got = tie(pre_term, two_got)
    grad_two = sum(g.astype(F32) for g in two_got)
    mlp_norm_sum = jnp.sum(middle * factor_two * grad_two, axis=0)
    grad_middle = grad_own.astype(F32) + norm_back(middle, factor_two, grad_two)
    grad_mid_own = grad_middle.astype(BF16).reshape(seqs, block, width)
    grad_mid_own, hidden_low = tie(grad_mid_own, hidden_low)
    branch_got = swaps(rows_product(hidden_low, down_weight, 1, 512, BF16, dp))

    grad_mid = assemble(to_sequence(grad_mid_own), slice(None), normed_two)
    if PRE_LATE:
        grad_mid, pre_term = tie(grad_mid, pre_term)
    pre_sum = ffn_scatter(pre_term)
    grad_mixed = rows_product(grad_mid, out_weight, 0, 256, BF16)
    out_pieces = term_pieces(grad_mid, mixed, dp_index, dp)
    grad_mixed, out_pieces = tie(grad_mixed, out_pieces)
    out_got = swaps(out_pieces)
    grad_qkv, gain_terms = attention_backward(qkv, grad_mixed, gains, cos, sin, earliest)
    grad_one_part, norm_sums = input_product(grad_qkv, qkv_weight, normed_one, mlp_norm_sum[None], 512)

    qkv_pieces = term_pieces(normed_one, grad_qkv, dp_index, dp, norm_sums)
    qkv_pieces, grad_one_part, branch_got, out_got = tie(qkv_pieces, grad_one_part, branch_got, out_got)
    qkv_got = swaps(qkv_pieces)
    branch = sum(g.astype(F32) for g in branch_got)
    layer_out = (middle + branch).astype(BF16)
    out_keep, out_give = sum_h(out_got)
    out_sum = out_keep + swap(out_give, "h", 1).astype(F32)
    grad_one = to_blocks(grad_one_part)
    qkv_keep, qkv_give = sum_h(qkv_got)
    head_norm_grad = total_over(total_over(jnp.sum(gain_terms, axis=0)[:2], "t"), "h")
    qkv_give, out_sum, pre_sum, down_sum = tie(qkv_give, out_sum, pre_sum, down_sum)
    qkv_sum = qkv_keep + swap(qkv_give, "h", 1).astype(F32)
    ffn_sum = jnp.concatenate([pre_sum, down_sum], axis=2)
    ffn_grad = swaps(
        [lax.dynamic_index_in_dim(ffn_sum, dp_index ^ k, 0, keepdims=False) for k in range(dp)]
    )
    gate_grad, up_grad, down_grad = whole(
        functools.partial(ffn_join_kernel, tiles),
        [jax.ShapeDtypeStruct(gate_proj.shape, F32)] * 3,
        dp_index,
        mlp_gain,
        *ffn_grad,
    )
    input_grad = grad_middle.reshape(seqs, block, width) + norm_back(inputs, factor_one, grad_one)

    attn_sum = jnp.concatenate([qkv_sum, out_sum], axis=1).astype(BF16)
    attn_sum, head_norm_grad = tie(attn_sum, head_norm_grad)
    head_norm_grad = total_over(head_norm_grad, "dp")
    attn_grad = swaps(
        [lax.dynamic_slice_in_dim(attn_sum, (part ^ k) * depth, depth, 0) for k in range(parts)], "t"
    )
    query_grad, key_grad, value_grad, out_proj_grad, norm_grads = whole(
        functools.partial(attn_join_kernel, heads),
        [
            jax.ShapeDtypeStruct(x.shape, F32)
            for x in (query_proj, key_projected, value_projected, out_proj, jnp.zeros((depth, HEAD_DIMENSION)))
        ],
        part,
        attn_gain,
        *attn_grad,
    )
    attn_norm_grad = norm_grads[:, 0] / attn_gain[:, 0]
    mlp_norm_grad = norm_grads[:, 1] / mlp_gain[:, 0]

    layer_out = jnp.transpose(layer_out.reshape(seqs, block, width), (1, 0, 2))
    input_grad = jnp.transpose(input_grad, (1, 0, 2))
    return (
        layer_out,
        input_grad,
        attn_norm_grad,
        query_grad,
        key_grad,
        value_grad,
        head_norm_grad,
        out_proj_grad,
        mlp_norm_grad,
        gate_grad,
        up_grad,
        down_grad,
    )


def solution(mesh):
    dp, ctx = mesh.shape["dp"], mesh.shape["ctx"]
    fine = Mesh(mesh.devices.reshape(dp, 2, ctx // 2), ("dp", "h", "t"))
    acts = P(("h", "t"), "dp", None)
    rows = P(("dp", "h", "t"), None)
    gain = P(("dp", "h", "t"))
    in_specs = (
        acts,
        P(("h", "t"), "dp"),
        gain,
        rows,
        rows,
        rows,
        P(),
        rows,
        gain,
        rows,
        rows,
        rows,
        acts,
    )
    out_specs = (acts, acts, gain, rows, rows, rows, P(), rows, gain, rows, rows, rows)
    return jax.shard_map(per_device, mesh=fine, in_specs=in_specs, out_specs=out_specs, check_vma=False)
```

time: 1280 us -> 822 us (0.64)
  waiting for transfers between devices: 715 us -> 438 us
  blocking collectives: 184 us -> 0 us
  matrix products: 142 us -> 0 us
  Pallas kernels: 31.5 us -> 173 us
  starting transfers between devices: 28.9 us -> 70.2 us
  local copies, waits for them, and re-layouts: 116 us -> 80.9 us
    ppermute x4 -> x71, waiting for transfers between devices: 72.3 us -> 437 us  [swap(): lax.ppermute(x, axis, [(i, i ^ bit) for i in range(lax.axis_size(axis))])]
    reduce_scatter x7 -> x2, waiting for transfers between devices: 311 us -> 0.04 us  [ffn_scatter(): lax.psum_scatter(term, ('h', 't'), scatter_dimension=0, tiled=True)]
    all_gather x9 -> x2, waiting for transfers between devices: 271 us -> 0.01 us  [ffn_gather(): return lax.all_gather(x, ('h', 't'), axis=0, tiled=False)]
    pallas_call x0 -> x18, Pallas kernels: none -> 142 us  [the longest x6 64.6 us: rows_product(): pl.pallas_call(functools.partial(rows_kernel, contract), grid=(columns //...]
    dot_general x15 -> x0, matrix products: 142 us -> none  [dot(): lax.dot_general(a, b, (((ca,), (cb,)), ((), ())), preferred_element_type=...]
    psum x1 -> x0, blocking collectives: 71.5 us -> none  [per_device(): sums = lax.psum(sums, everywhere)[0]]
    all_to_all x5 -> x0, blocking collectives: 71 us -> none  [the longest x3 38.6 us: ffn_columns(): w = lax.all_to_all(w, 'dp', 0, 0, tiled=True)]
    unnamed x18 -> x4, waiting for transfers between devices: 54.2 us -> 0.07 us
  transfers between devices with their start and end apart: 24 -> 75, of which waited for: 18 -> 34; matrix products, arithmetic and copies ran while one was open for 18% -> 12% of each run, Pallas kernels for 2% -> 18%
where the time goes in v2:
time: 822 us; the launch traced here: 814 us
  waiting for transfers between devices  438 us (53%)
  Pallas kernels  173 us (21%)
  local copies, waits for them, and re-layouts  80.9 us (10%)
  starting transfers between devices  70.2 us (9%)
  other arithmetic  37 us (5%)
  between operations  15.5 us (2%)
    ppermute x71, waiting for transfers between devices, swap(): lax.ppermute(x, axis, [(i, i ^ bit) for i in range(lax.axis_size(axis))])  437 us
    ppermute x71, starting transfers between devices, swap(): lax.ppermute(x, axis, [(i, i ^ bit) for i in range(lax.axis_size(axis))])  69.4 us
    pallas_call x6, Pallas kernels, rows_product(): pl.pallas_call(functools.partial(rows_kernel, contract), grid=(columns //...  64.6 us
    pallas_call x2, Pallas kernels, term_product(): pl.pallas_call(term_kernel, grid=(groups,), in_specs=[pl.BlockSpec((rows,...  29.5 us
    pallas_call x1, Pallas kernels, attention_backward(): pl.pallas_call(functools.partial(backward_kernel, 256), grid=(heads,), in...  18.8 us
    pallas_call x2, Pallas kernels, term_pieces(): pl.pallas_call(pieces_kernel, grid_spec=pltpu.PrefetchScalarGridSpec(num_...  17.1 us
  transfers between devices with their start and end apart: 75, of which 34 were waited for; matrix products, arithmetic and copies ran while one was open for 12% of the time, Pallas kernels for 18%

profile of v2, /device:TPU:0, one launch (start us, length us, event | category | flops | bytes accessed | tf_op | source)
XLA Modules:
  0.0 814.3 jit_solution(3455534264113825631)
XLA Ops:
  20.0 24.7 %collective-permute-done.1.refs_2_ = bf16[64,1536]{1,0:T(8,128)(2,1)S(1)} collective-permute-done((bf16[64,1536]{1,0:T(8,128)(2,1)S(1)}, bf16[64,1536]{1,0:T(8,128)(2,1)S(1)}, u32[]{:S(2)}, u32[]{:S(2)}) %collective-permute-start.1) | collective-permute-done | bytes 196640 | tf_op jit(solution)/shard_map/ppermute | solution.py:437
  62.3 12.3 %collective-permute-done.4 = bf16[256,1024]{1,0:T(8,128)(2,1)} collective-permute-done((bf16[256,1024]{1,0:T(8,128)(2,1)S(1)}, bf16[256,1024]{1,0:T(8,128)(2,1)}, u32[]{:S(2)}, u32[]{:S(2)}) %collective-permute-start.4) | collective-permute-done | bytes 524320 | tf_op jit(solution)/shard_map/ppermute | solution.py:437
  90.8 12.7 %collective-permute-done.7.refs_2_ = bf16[64,4608]{1,0:T(8,128)(2,1)S(1)} collective-permute-done((bf16[64,4608]{1,0:T(8,128)(2,1)S(1)}, bf16[64,4608]{1,0:T(8,128)(2,1)S(1)}, u32[]{:S(2)}, u32[]{:S(2)}) %collective-permute-start.7) | collective-permute-done | bytes 589856 | tf_op jit(solution)/shard_map/ppermute | solution.py:437
  119.2 56.3 %collective-permute-done.15 = bf16[256,1024]{1,0:T(8,128)(2,1)} collective-permute-done((bf16[256,1024]{1,0:T(8,128)(2,1)S(1)}, bf16[256,1024]{1,0:T(8,128)(2,1)}, u32[]{:S(2)}, u32[]{:S(2)}) %collective-permute-start.15) | collective-permute-done | bytes 524320 | tf_op jit(solution)/shard_map/ppermute | solution.py:437
  210.7 17.5 %collective-permute-done.14 = bf16[256,512]{1,0:T(8,128)(2,1)S(1)} collective-permute-done((bf16[256,512]{1,0:T(8,128)(2,1)S(1)}, bf16[256,512]{1,0:T(8,128)(2,1)S(1)}, u32[]{:S(2)}, u32[]{:S(2)}) %collective-permute-start.14) | collective-permute-done | bytes 262176 | tf_op jit(solution)/shard_map/ppermute | solution.py:437
  234.4 12.6 %shard_map.225.a_ref.b_ref = bf16[1024,512]{1,0:T(8,128)(2,1)S(1)} custom-call(f32[1024,1024]{1,0:T(8,128)} %copy-done, f32[2,128]{1,0:T(2,128)S(1)} %convert_element_type.192.gain_ref, f32[1024,128]{1,0:T(8,128)S(1)} %get-tuple-element.343.cos_ref, f32[1024,128]{1,0:T(8,128)S(1)} %get-tuple-element.344.sin_ref, s32[8,1024]{1,0:T(8,128)S(1)} %broadcast_in_dim.48.early_ref), custom_call_target="tpu_custom_call" | custom-call | flops 1048576 | bytes 65536 | tf_op jit(solution)/shard_map/pallas_call | solution.py:360
  296.1 24.1 %collective-permute-done.29 = bf16[128,2048]{1,0:T(8,128)(2,1)} collective-permute-done((bf16[128,2048]{1,0:T(8,128)(2,1)}, bf16[128,2048]{1,0:T(8,128)(2,1)}, u32[]{:S(2)}, u32[]{:S(2)}) %collective-permute-start.29) | collective-permute-done | bytes 524320 | tf_op jit(solution)/shard_map/ppermute | solution.py:437
  329.4 20.7 %collective-permute-done.30 = bf16[256,2048]{1,0:T(8,128)(2,1)S(1)} collective-permute-done((bf16[256,2048]{1,0:T(8,128)(2,1)}, bf16[256,2048]{1,0:T(8,128)(2,1)S(1)}, u32[]{:S(2)}, u32[]{:S(2)}) %collective-permute-start.30) | collective-permute-done | bytes 1048608 | tf_op jit(solution)/shard_map/ppermute | solution.py:437
  350.0 21.6 %collective-permute-done.31 = bf16[256,2048]{1,0:T(8,128)(2,1)S(1)} collective-permute-done((bf16[256,2048]{1,0:T(8,128)(2,1)}, bf16[256,2048]{1,0:T(8,128)(2,1)S(1)}, u32[]{:S(2)}, u32[]{:S(2)}) %collective-permute-start.31) | collective-permute-done | bytes 1048608 | tf_op jit(solution)/shard_map/ppermute | solution.py:437
  378.2 11.0 %copy.116 = bf16[4,8,64,3072]{3,2,1,0:T(8,128)(2,1)} copy(bf16[4,8,64,3072]{3,2,0,1:T(8,128)(2,1)} %bitcast.215) | data formatting | bytes 25165824 | tf_op jit(solution)/shard_map/transpose | solution.py:601
  398.8 21.5 %collective-permute-done.34 = bf16[256,2048]{1,0:T(8,128)(2,1)S(1)} collective-permute-done((bf16[256,2048]{1,0:T(8,128)(2,1)S(1)}, bf16[256,2048]{1,0:T(8,128)(2,1)S(1)}, u32[]{:S(2)}, u32[]{:S(2)}) %collective-permute-start.34) | collective-permute-done | bytes 1048608 | tf_op jit(solution)/shard_map/ppermute | solution.py:437
  422.4 18.5 %shard_map.227.pre_ref = f32[1024,3072]{1,0:T(8,128)} custom-call(bf16[1024,2048]{1,0:T(8,128)(2,1)} %constant_dynamic-update-slice_fusion.a_ref, bf16[2048,3072]{1,0:T(8,128)(2,1)} %bitcast.201), custom_call_target="tpu_custom_call" | custom-call | flops 1048576 | bytes 65536 | tf_op jit(solution)/shard_map/pallas_call | solution.py:54
  447.0 16.3 %shard_map.228 = (bf16[1024,1536]{1,0:T(8,128)(2,1)}, bf16[1024,3072]{1,0:T(8,128)(2,1)}) custom-call(f32[1024,3072]{1,0:T(8,128)} %shard_map.227.pre_ref, bf16[1024,2048]{1,0:T(8,128)(2,1)} %constant_dynamic-update-slice_fusion.4.grad_ref.a_ref, bf16[2048,1536]{1,0:T(8,128)(2,1)} %bitcast.208), custom_call_target="tpu_custom_call" | custom-call | flops 1048576 | bytes 65536 | tf_op jit(solution)/shard_map/pallas_call | solution.py:411
  474.2 17.8 %shard_map.230 = (bf16[256,2048]{1,0:T(8,128)(2,1)S(1)}, bf16[256,2048]{1,0:T(8,128)(2,1)S(1)}, bf16[256,2048]{1,0:T(8,128)(2,1)S(1)}, bf16[256,2048]{1,0:T(8,128)(2,1)S(1)}) custom-call(bf16[1024,3072]{1,0:T(8,128)(2,1)} %get-tuple-element.175.a_ref.b_ref, bf16[2048,3072]{1,0:T(8,128)(2,1)} %bitcast.202), custom_call_target="tpu_custom_call" | custom-call | flops 1048576 | bytes 65536 | tf_op jit(solution)/shard_map/pallas_call | solution.py:54
  495.6 18.7 %shard_map.231 = bf16[8,4,64,3072]{3,2,1,0:T(8,128)(2,1)} custom-call(bf16[1024,2048]{1,0:T(8,128)(2,1)} %constant_dynamic-update-slice_fusion.a_ref, bf16[1024,3072]{1,0:T(8,128)(2,1)} %get-tuple-element.175.a_ref.b_ref), custom_call_target="tpu_custom_call" | custom-call | flops 1048576 | bytes 65536 | tf_op jit(solution)/shard_map/pallas_call | solution.py:79
  518.2 17.9 %collective-permute-done.37 = bf16[256,2048]{1,0:T(8,128)(2,1)} collective-permute-done((bf16[256,2048]{1,0:T(8,128)(2,1)S(1)}, bf16[256,2048]{1,0:T(8,128)(2,1)}, u32[]{:S(2)}, u32[]{:S(2)}) %collective-permute-start.37) | collective-permute-done | bytes 1048608 | tf_op jit(solution)/shard_map/ppermute | solution.py:437
  548.0 15.6 %collective-permute-done.39 = bf16[1,128,2048]{2,1,0:T(8,128)(2,1)S(1)} collective-permute-done((bf16[1,128,2048]{2,1,0:T(8,128)(2,1)S(1)}, bf16[1,128,2048]{2,1,0:T(8,128)(2,1)S(1)}, u32[]{:S(2)}, u32[]{:S(2)}) %collective-permute-start.39) | collective-permute-done | bytes 524320 | tf_op jit(solution)/shard_map/ppermute | solution.py:437
  566.8 11.2 %collective-permute-done.42 = bf16[1,128,2048]{2,1,0:T(8,128)(2,1)S(1)} collective-permute-done((bf16[1,128,2048]{2,1,0:T(8,128)(2,1)S(1)}, bf16[1,128,2048]{2,1,0:T(8,128)(2,1)S(1)}, u32[]{:S(2)}, u32[]{:S(2)}) %collective-permute-start.42) | collective-permute-done | bytes 524320 | tf_op jit(solution)/shard_map/ppermute | solution.py:437
  609.6 18.8 %shard_map.234 = (bf16[1024,1024]{1,0:T(8,128)(2,1)S(1)}, f32[2,8,128]{2,1,0:T(8,128)S(1)}) custom-call(f32[1024,1024]{1,0:T(8,128)} %copy-done, bf16[1024,512]{1,0:T(8,128)(2,1)S(1)} %shard_map.232.dout_ref, f32[2,128]{1,0:T(2,128)S(1)} %convert_element_type.192.gain_ref, f32[1024,128]{1,0:T(8,128)S(1)} %copy-done.4, f32[1024,128]{1,0:T(8,128)S(1)} %copy-done.6, ...), custom_call_target="tpu_custom_call" | custom-call | flops 1048576 | bytes 65536 | tf_op jit(solution)/shard_map/pallas_call | solution.py:374
  677.3 18.6 %collective-permute-done.58 = bf16[256,512]{1,0:T(8,128)(2,1)S(1)} collective-permute-done((bf16[256,512]{1,0:T(8,128)(2,1)S(1)}, bf16[256,512]{1,0:T(8,128)(2,1)S(1)}, u32[]{:S(2)}, u32[]{:S(2)}) %collective-permute-start.58) | collective-permute-done | bytes 262176 | tf_op jit(solution)/shard_map/ppermute | solution.py:437
  700.7 23.8 %collective-permute-done.52 = bf16[128,2048]{1,0:T(8,128)(2,1)S(1)} collective-permute-done((bf16[128,2048]{1,0:T(8,128)(2,1)S(1)}, bf16[128,2048]{1,0:T(8,128)(2,1)S(1)}, u32[]{:S(2)}, u32[]{:S(2)}) %collective-permute-start.52) | collective-permute-done | bytes 524320 | tf_op jit(solution)/shard_map/ppermute | solution.py:437
  724.5 12.6 %collective-permute-done.53 = bf16[128,2048]{1,0:T(8,128)(2,1)S(1)} collective-permute-done((bf16[128,2048]{1,0:T(8,128)(2,1)S(1)}, bf16[128,2048]{1,0:T(8,128)(2,1)S(1)}, u32[]{:S(2)}, u32[]{:S(2)}) %collective-permute-start.53) | collective-permute-done | bytes 524320 | tf_op jit(solution)/shard_map/ppermute | solution.py:437
  740.9 21.4 %collective-permute-done.54 = bf16[128,2048]{1,0:T(8,128)(2,1)S(1)} collective-permute-done((bf16[128,2048]{1,0:T(8,128)(2,1)S(1)}, bf16[128,2048]{1,0:T(8,128)(2,1)S(1)}, u32[]{:S(2)}, u32[]{:S(2)}) %collective-permute-start.54) | collective-permute-done | bytes 524320 | tf_op jit(solution)/shard_map/ppermute | solution.py:437
  768.6 23.7 %collective-permute-done.59 = bf16[256,1152]{1,0:T(8,128)(2,1)S(1)} collective-permute-done((bf16[256,1152]{1,0:T(8,128)(2,1)S(1)}, bf16[256,1152]{1,0:T(8,128)(2,1)S(1)}, u32[]{:S(2)}, u32[]{:S(2)}) %collective-permute-start.59) | collective-permute-done | bytes 589856 | tf_op jit(solution)/shard_map/ppermute | solution.py:437
  (382 shorter events, 328.8 us)
Async XLA Ops:
  7.2 316.1 %all-gather.5.cloned.1.call-start = ((), (), s32[]{:S(2)}) async-start(), calls=%async_computation.4 | async-start | bytes 14155776 | tf_op jit(solution)/shard_map/all_gather | solution.py:598
  12.1 38.8 %collective-permute-start.9 = (bf16[1,128,2176]{2,1,0:T(8,128)(2,1)S(1)}, bf16[1,128,2176]{2,1,0:T(8,128)(2,1)S(1)}, u32[]{:S(2)}, u32[]{:S(2)}) collective-permute-start(bf16[1,128,2176]{2,1,0:T(8,128)(2,1)S(1)} %get-tuple-element.323), channel_id=1, source_target_pairs={{0,2},{1,3},{2,0},{3,1},{4,6},{5,7},{6,4},{7,5},{8,10},{9,11},{10,... | collective-permute-start | bytes 1671176 | tf_op jit(solution)/shard_map/ppermute | solution.py:437
  15.6 31.6 %collective-permute-start.2 = (bf16[64,1536]{1,0:T(8,128)(2,1)S(1)}, bf16[64,1536]{1,0:T(8,128)(2,1)S(1)}, u32[]{:S(2)}, u32[]{:S(2)}) collective-permute-start(bf16[64,1536]{1,0:T(8,128)(2,1)S(1)} %get-tuple-element.132), channel_id=1, source_target_pairs={{0,3},{1,2},{2,1},{3,0},{4,7},{5,6},{6,5},{7,4},{8,11},{9,10},{10,... | collective-permute-start | bytes 589832 | tf_op jit(solution)/shard_map/ppermute | solution.py:437
  17.4 38.1 %collective-permute-start.11 = (bf16[128,2176]{1,0:T(8,128)(2,1)}, bf16[128,2176]{1,0:T(8,128)(2,1)}, u32[]{:S(2)}, u32[]{:S(2)}) collective-permute-start(bf16[128,2176]{1,0:T(8,128)(2,1)} %get-tuple-element.322), channel_id=1, source_target_pairs={{0,4},{4,0},{1,5},{5,1},{2,6},{6,2},{3,7},{7,3},{8,12},{12,8},{9,1... | collective-permute-start | bytes 1671176 | tf_op jit(solution)/shard_map/ppermute | solution.py:437
  52.0 53.0 %collective-permute-start.10 = (bf16[2,128,2176]{2,1,0:T(8,128)(2,1)}, bf16[2,128,2176]{2,1,0:T(8,128)(2,1)}, u32[]{:S(2)}, u32[]{:S(2)}) collective-permute-start(bf16[2,128,2176]{2,1,0:T(8,128)(2,1)} %pad_maximum_fusion), channel_id=1, source_target_pairs={{0,1},{1,0},{2,3},{3,2},{4,5},{5,4},{6,7},{7,6},{8,9},{9,8},{10,11... | collective-permute-start | bytes 3342344 | tf_op jit(solution)/shard_map/ppermute | solution.py:437
  80.2 31.6 %collective-permute-start.13 = (bf16[2,128,2176]{2,1,0:T(8,128)(2,1)S(1)}, bf16[2,128,2176]{2,1,0:T(8,128)(2,1)S(1)}, u32[]{:S(2)}, u32[]{:S(2)}) collective-permute-start(bf16[2,128,2176]{2,1,0:T(8,128)(2,1)S(1)} %pad_maximum_fusion.1), channel_id=1, source_target_pairs={{0,1},{1,0},{2,3},{3,2},{4,5},{5,4},{6,7},{7,6},{8,9},{9,8},{10,11... | collective-permute-start | bytes 3342344 | tf_op jit(solution)/shard_map/ppermute | solution.py:437
  113.7 327.2 %all-gather.7.cloned.1.call-start = ((), (), s32[]{:S(2)}) async-start(), calls=%async_computation.5 | async-start | bytes 7077888 | tf_op jit(solution)/shard_map/all_gather | solution.py:598
  113.8 61.7 %collective-permute-start.15 = (bf16[256,1024]{1,0:T(8,128)(2,1)S(1)}, bf16[256,1024]{1,0:T(8,128)(2,1)}, u32[]{:S(2)}, u32[]{:S(2)}) collective-permute-start(bf16[256,1024]{1,0:T(8,128)(2,1)S(1)} %get-tuple-element.150), channel_id=1, source_target_pairs={{0,4},{4,0},{1,5},{5,1},{2,6},{6,2},{3,7},{7,3},{8,12},{12,8},{9,1... | collective-permute-start | bytes 1572872 | tf_op jit(solution)/shard_map/ppermute | solution.py:437
  323.3 439.7 %reduce-scatter.5.cloned.1.call-start = ((), (), s32[]{:S(2)}) async-start(), calls=%async_computation.3 | async-start | bytes 7077888 | tf_op jit(solution)/shard_map/reduce_scatter | solution.py:606
  323.9 47.7 %collective-permute-start.31 = (bf16[256,2048]{1,0:T(8,128)(2,1)}, bf16[256,2048]{1,0:T(8,128)(2,1)S(1)}, u32[]{:S(2)}, u32[]{:S(2)}) collective-permute-start(bf16[256,2048]{1,0:T(8,128)(2,1)} %bitcast.217), channel_id=1, source_target_pairs={{0,16},{8,24},{16,0},{24,8},{1,17},{9,25},{17,1},{25,9},{2,18},{10... | collective-permute-start | bytes 3145736 | tf_op jit(solution)/shard_map/ppermute | solution.py:437
  325.6 46.0 %collective-permute-start.32 = (bf16[256,2048]{1,0:T(8,128)(2,1)}, bf16[256,2048]{1,0:T(8,128)(2,1)S(1)}, u32[]{:S(2)}, u32[]{:S(2)}) collective-permute-start(bf16[256,2048]{1,0:T(8,128)(2,1)} %bitcast.218), channel_id=1, source_target_pairs={{0,24},{8,16},{16,8},{24,0},{1,25},{9,17},{17,9},{25,1},{2,26},{10... | collective-permute-start | bytes 3145736 | tf_op jit(solution)/shard_map/ppermute | solution.py:437
  374.3 46.0 %collective-permute-start.34 = (bf16[256,2048]{1,0:T(8,128)(2,1)S(1)}, bf16[256,2048]{1,0:T(8,128)(2,1)S(1)}, u32[]{:S(2)}, u32[]{:S(2)}) collective-permute-start(bf16[256,2048]{1,0:T(8,128)(2,1)S(1)} %multiply_convert_fusion), channel_id=1, source_target_pairs={{0,16},{8,24},{16,0},{24,8},{1,17},{9,25},{17,1},{25,9},{2,18},{10... | collective-permute-start | bytes 3145736 | tf_op jit(solution)/shard_map/ppermute | solution.py:437
  374.6 46.7 %collective-permute-start.35 = (bf16[256,2048]{1,0:T(8,128)(2,1)S(1)}, bf16[256,2048]{1,0:T(8,128)(2,1)S(1)}, u32[]{:S(2)}, u32[]{:S(2)}) collective-permute-start(bf16[256,2048]{1,0:T(8,128)(2,1)S(1)} %multiply_convert_fusion), channel_id=1, source_target_pairs={{0,24},{8,16},{16,8},{24,0},{1,25},{9,17},{17,9},{25,1},{2,26},{10... | collective-permute-start | bytes 3145736 | tf_op jit(solution)/shard_map/ppermute | solution.py:437
  474.0 289.0 %reduce-scatter.3.cloned.1.call-start = ((), (), s32[]{:S(2)}) async-start(), calls=%async_computation.2 | async-start | bytes 14155776 | tf_op jit(solution)/shard_map/reduce_scatter | solution.py:606
  492.6 43.5 %collective-permute-start.37 = (bf16[256,2048]{1,0:T(8,128)(2,1)S(1)}, bf16[256,2048]{1,0:T(8,128)(2,1)}, u32[]{:S(2)}, u32[]{:S(2)}) collective-permute-start(bf16[256,2048]{1,0:T(8,128)(2,1)S(1)} %get-tuple-element.178), channel_id=1, source_target_pairs={{0,16},{8,24},{16,0},{24,8},{1,17},{9,25},{17,1},{25,9},{2,18},{10... | collective-permute-start | bytes 3145736 | tf_op jit(solution)/shard_map/ppermute | solution.py:437
  494.3 41.8 %collective-permute-start.38 = (bf16[256,2048]{1,0:T(8,128)(2,1)S(1)}, bf16[256,2048]{1,0:T(8,128)(2,1)}, u32[]{:S(2)}, u32[]{:S(2)}) collective-permute-start(bf16[256,2048]{1,0:T(8,128)(2,1)S(1)} %get-tuple-element.179), channel_id=1, source_target_pairs={{0,24},{8,16},{16,8},{24,0},{1,25},{9,17},{17,9},{25,1},{2,26},{10... | collective-permute-start | bytes 3145736 | tf_op jit(solution)/shard_map/ppermute | solution.py:437
  594.2 40.7 %collective-permute-start.44 = (bf16[256,2048]{1,0:T(8,128)(2,1)}, bf16[256,2048]{1,0:T(8,128)(2,1)}, u32[]{:S(2)}, u32[]{:S(2)}) collective-permute-start(bf16[256,2048]{1,0:T(8,128)(2,1)} %get-tuple-element.201), channel_id=1, source_target_pairs={{0,8},{8,0},{16,24},{24,16},{1,9},{9,1},{17,25},{25,17},{2,10},{10... | collective-permute-start | bytes 3145736 | tf_op jit(solution)/shard_map/ppermute | solution.py:437
  595.9 64.6 %collective-permute-start.45 = (bf16[256,2048]{1,0:T(8,128)(2,1)}, bf16[256,2048]{1,0:T(8,128)(2,1)}, u32[]{:S(2)}, u32[]{:S(2)}) collective-permute-start(bf16[256,2048]{1,0:T(8,128)(2,1)} %get-tuple-element.202), channel_id=1, source_target_pairs={{0,16},{8,24},{16,0},{24,8},{1,17},{9,25},{17,1},{25,9},{2,18},{10... | collective-permute-start | bytes 3145736 | tf_op jit(solution)/shard_map/ppermute | solution.py:437
  597.7 62.9 %collective-permute-start.46 = (bf16[256,2048]{1,0:T(8,128)(2,1)}, bf16[256,2048]{1,0:T(8,128)(2,1)}, u32[]{:S(2)}, u32[]{:S(2)}) collective-permute-start(bf16[256,2048]{1,0:T(8,128)(2,1)} %get-tuple-element.203), channel_id=1, source_target_pairs={{0,24},{8,16},{16,8},{24,0},{1,25},{9,17},{17,9},{25,1},{2,26},{10... | collective-permute-start | bytes 3145736 | tf_op jit(solution)/shard_map/ppermute | solution.py:437
  670.3 69.2 %collective-permute-start.55 = (bf16[512,1152]{1,0:T(8,128)(2,1)S(1)}, bf16[512,1152]{1,0:T(8,128)(2,1)S(1)}, u32[]{:S(2)}, u32[]{:S(2)}) collective-permute-start(bf16[512,1152]{1,0:T(8,128)(2,1)S(1)} %copy-done.40), channel_id=1, source_target_pairs={{0,8},{8,0},{16,24},{24,16},{1,9},{9,1},{17,25},{25,17},{2,10},{10... | collective-permute-start | bytes 3538952 | tf_op jit(solution)/shard_map/ppermute | solution.py:437
  671.3 68.2 %collective-permute-start.56 = (bf16[512,1152]{1,0:T(8,128)(2,1)S(1)}, bf16[512,1152]{1,0:T(8,128)(2,1)S(1)}, u32[]{:S(2)}, u32[]{:S(2)}) collective-permute-start(bf16[512,1152]{1,0:T(8,128)(2,1)S(1)} %copy-done.39), channel_id=1, source_target_pairs={{0,16},{8,24},{16,0},{24,8},{1,17},{9,25},{17,1},{25,9},{2,18},{10... | collective-permute-start | bytes 3538952 | tf_op jit(solution)/shard_map/ppermute | solution.py:437
  695.9 43.6 %collective-permute-start.57 = (bf16[512,1152]{1,0:T(8,128)(2,1)S(1)}, bf16[512,1152]{1,0:T(8,128)(2,1)S(1)}, u32[]{:S(2)}, u32[]{:S(2)}) collective-permute-start(bf16[512,1152]{1,0:T(8,128)(2,1)S(1)} %copy-done.38), channel_id=1, source_target_pairs={{0,24},{8,16},{16,8},{24,0},{1,25},{9,17},{17,9},{25,1},{2,26},{10... | collective-permute-start | bytes 3538952 | tf_op jit(solution)/shard_map/ppermute | solution.py:437
  698.3 38.8 %collective-permute-start.53 = (bf16[128,2048]{1,0:T(8,128)(2,1)S(1)}, bf16[128,2048]{1,0:T(8,128)(2,1)S(1)}, u32[]{:S(2)}, u32[]{:S(2)}) collective-permute-start(bf16[128,2048]{1,0:T(8,128)(2,1)S(1)} %get-tuple-element.326), channel_id=1, source_target_pairs={{0,2},{1,3},{2,0},{3,1},{4,6},{5,7},{6,4},{7,5},{8,10},{9,11},{10,... | collective-permute-start | bytes 1572872 | tf_op jit(solution)/shard_map/ppermute | solution.py:437
  768.3 33.7 %collective-permute-start.70 = (bf16[64,4608]{1,0:T(8,128)(2,1)S(1)}, bf16[64,4608]{1,0:T(8,128)(2,1)S(1)}, u32[]{:S(2)}, u32[]{:S(2)}) collective-permute-start(bf16[64,4608]{1,0:T(8,128)(2,1)S(1)} %get-tuple-element.312), channel_id=1, source_target_pairs={{0,24},{8,16},{16,8},{24,0},{1,25},{9,17},{17,9},{25,1},{2,26},{10... | collective-permute-start | bytes 1769480 | tf_op jit(solution)/shard_map/ppermute | solution.py:437
  (95 other events, 1496.8 us)
Sparse Core Ops, SparseCore 0:
  113.8 139.1 all-gather.4
  323.4 63.7 all-gather.6
  474.1 69.3 reduce-scatter.4
  583.4 149.7 reduce-scatter.2

commit v3 on v2

--- a/solution.py
+++ b/solution.py
@@ -35,7 +35,6 @@
     return lax.dot_general(a, b, (((ca,), (cb,)), ((), ())), preferred_element_type=F32)
 
 
-F_AFTER_W = True
 PRE_LATE = True
 CHEAP = pl.CostEstimate(flops=1 << 20, bytes_accessed=1 << 16, transcendentals=0)
 
@@ -66,6 +65,118 @@
         cost_estimate=CHEAP,
     )(a, b)
     return out if pieces > 1 else out[0]
+
+
+def blocks_kernel(where_ref, a_ref, *refs):
+    w_refs, out_ref = refs[:-1], refs[-1]
+    depth = w_refs[0].shape[0]
+    total = None
+    for k, w_ref in enumerate(w_refs):
+        start = pl.multiple_of(where_ref[k] * depth, HEAD_DIMENSION)
+        part = dot(a_ref[:, pl.ds(start, depth)], w_ref[...])
+        total = part if total is None else total + part
+    out_ref[...] = total
+
+
+def blocks_product(a, w_blocks, where, tile):
+    rows, depth = a.shape
+    columns = w_blocks[0].shape[1]
+    return pl.pallas_call(
+        blocks_kernel,
+        grid_spec=pltpu.PrefetchScalarGridSpec(
+            num_scalar_prefetch=1,
+            grid=(columns // tile,),
+            in_specs=[pl.BlockSpec((rows, depth), lambda j, where: (0, 0))]
+            + [pl.BlockSpec((w.shape[0], tile), lambda j, where: (0, j)) for w in w_blocks],
+            out_specs=pl.BlockSpec((rows, tile), lambda j, where: (0, j)),
+        ),
+        out_shape=jax.ShapeDtypeStruct((rows, columns), F32),
+        compiler_params=pltpu.CompilerParams(vmem_limit_bytes=48 << 20),
+        cost_estimate=CHEAP,
+    )(where, a, *w_blocks)
+
+
+def blocks_back_kernel(where_ref, a_ref, *refs):
+    w_refs, out_ref = refs[:-1], refs[-1]
+    depth = w_refs[0].shape[0]
+    for k, w_ref in enumerate(w_refs):
+        start = pl.multiple_of(where_ref[k] * depth, HEAD_DIMENSION)
+        out_ref[:, pl.ds(start, depth)] = dot(a_ref[...], w_ref[...], 1, 1).astype(BF16)
+
+
+def blocks_back(a, w_blocks, where, pieces):
+    rows, depth = a.shape
+    columns = sum(w.shape[0] for w in w_blocks)
+    return pl.pallas_call(
+        blocks_back_kernel,
+        grid_spec=pltpu.PrefetchScalarGridSpec(
+            num_scalar_prefetch=1,
+            grid=(pieces,),
+            in_specs=[pl.BlockSpec((rows // pieces, depth), lambda j, where: (j, 0))]
+            + [pl.BlockSpec(w.shape, lambda j, where: (0, 0)) for w in w_blocks],
+            out_specs=pl.BlockSpec((rows // pieces, columns), lambda j, where: (j, 0)),
+        ),
+        out_shape=jax.ShapeDtypeStruct((rows, columns), BF16),
+        compiler_params=pltpu.CompilerParams(vmem_limit_bytes=48 << 20),
+        cost_estimate=CHEAP,
+    )(where, a, *w_blocks)
+
+
+def stacked_kernel(a_ref, w_ref, out_ref):
+    out_ref[...] = stacked_dot(a_ref, w_ref).astype(out_ref.dtype)
+
+
+def stacked_dot(a_ref, w_ref):
+    blocks, groups, depth, columns = w_ref.shape
+    step = blocks * depth
+    total = None
+    for d in range(groups):
+        part = dot(a_ref[:, d * step : (d + 1) * step], w_ref[:, d].reshape(step, columns))
+        total = part if total is None else total + part
+    return total
+
+
+def stacked_product(a, w, tile):
+    rows, depth = a.shape
+    columns = w.shape[3]
+    return pl.pallas_call(
+        stacked_kernel,
+        grid=(columns // tile,),
+        in_specs=[
+            pl.BlockSpec((rows, depth), lambda j: (0, 0)),
+            pl.BlockSpec(w.shape[:3] + (tile,), lambda j: (0, 0, 0, j)),
+        ],
+        out_specs=pl.BlockSpec((rows, tile), lambda j: (0, j)),
+        out_shape=jax.ShapeDtypeStruct((rows, columns), F32),
+        compiler_params=pltpu.CompilerParams(vmem_limit_bytes=56 << 20),
+        cost_estimate=CHEAP,
+    )(a, w)
+
+
+def stacked_back_kernel(a_ref, w_ref, *out_refs):
+    blocks, _, depth, columns = w_ref.shape
+    out = dot(a_ref[...], w_ref[:, 0].reshape(blocks * depth, columns), 1, 1).astype(BF16)
+    step = out_refs[0].shape[0]
+    for k, out_ref in enumerate(out_refs):
+        out_ref[...] = out[k * step : (k + 1) * step]
+
+
+def stacked_back(a, w, pieces):
+    rows, depth = a.shape
+    blocks, groups, n, columns = w.shape
+    step = blocks * n
+    return pl.pallas_call(
+        stacked_back_kernel,
+        grid=(groups,),
+        in_specs=[
+            pl.BlockSpec((rows, depth), lambda j: (0, 0)),
+            pl.BlockSpec((blocks, 1, n, columns), lambda j: (0, j, 0, 0)),
+        ],
+        out_specs=[pl.BlockSpec((rows // pieces, step), lambda j: (0, j))] * pieces,
+        out_shape=[jax.ShapeDtypeStruct((rows // pieces, groups * step), BF16)] * pieces,
+        compiler_params=pltpu.CompilerParams(vmem_limit_bytes=56 << 20),
+        cost_estimate=CHEAP,
+    )(a, w)
 
 
 def term_kernel(a_ref, b_ref, out_ref):
@@ -228,18 +339,18 @@
 
 
 def ffn_join_kernel(tiles, me_ref, gain_ref, *refs):
-    count = len(refs) - 3
-    gate_ref, up_ref, down_ref = refs[count:]
+    count = (len(refs) - 3) // 2
+    gate_ref, up_ref, down_ref = refs[2 * count :]
     gain = gain_ref[...]
-    hidden = refs[0].shape[1] // 3
+    hidden = refs[0].shape[1] // 2
     tile = hidden // tiles
-    for s, got_ref in enumerate(refs[:count]):
+    for s, (got_ref, down_got_ref) in enumerate(zip(refs[:count], refs[count:])):
         part = me_ref[0] ^ s
         for n in range(tiles):
             for k, ref in enumerate((gate_ref, up_ref)):
                 at = (2 * n + k) * tile
                 ref[:, lanes(part * tiles + n, tile)] = got_ref[:, at : at + tile].astype(F32) * gain
-        down_ref[:, lanes(part, hidden)] = got_ref[:, 2 * hidden :].astype(F32)
+        down_ref[:, lanes(part, hidden)] = down_got_ref[...].astype(F32)
 
 
 def rows_join_kernel(me_ref, *refs):
@@ -392,7 +503,7 @@
 
 def hidden_kernel(pre_ref, grad_ref, down_ref, hidden_ref, dpre_ref):
     tile = hidden_ref.shape[1]
-    grad_hidden = dot(grad_ref[...], down_ref[...])
+    grad_hidden = stacked_dot(grad_ref, down_ref)
     step = 128
     for start in range(0, hidden_ref.shape[0], step):
         rows = slice(start, start + step)
@@ -406,7 +517,7 @@
 
 def hidden_layer(pre, grad, down, tiles):
     rows, width = grad.shape
-    tile = down.shape[1] // tiles
+    tile = down.shape[3] // tiles
     step = min(rows, 1024)
     return pl.pallas_call(
         hidden_kernel,
@@ -414,7 +525,7 @@
         in_specs=[
             pl.BlockSpec((step, 2 * tile), lambda j, i: (i, j)),
             pl.BlockSpec((step, width), lambda j, i: (i, 0)),
-            pl.BlockSpec((width, tile), lambda j, i: (0, j)),
+            pl.BlockSpec(down.shape[:3] + (tile,), lambda j, i: (0, 0, 0, j)),
         ],
         out_specs=[
             pl.BlockSpec((step, tile), lambda j, i: (i, j)),
@@ -437,34 +548,60 @@
     return lax.ppermute(x, axis, [(i, i ^ bit) for i in range(lax.axis_size(axis))])
 
 
-def to_sequence(blocks):
+def sequence_steps(blocks, together):
     half, part, parts = lax.axis_index("h"), lax.axis_index("t"), lax.axis_size("t")
     block = blocks.shape[1]
-    own = lax.dynamic_index_in_dim(blocks, half, 0, keepdims=False)
-    got = swap(lax.dynamic_index_in_dim(blocks, 1 - half, 0, keepdims=False), "h", 1)
+    own = lax.dynamic_index_in_dim(blocks, half, 0, keepdims=True)
+    got = swap(lax.dynamic_index_in_dim(blocks, 1 - half, 0, keepdims=True), "h", 1)
+    if not together:
+        own_first, got = tie(swap(own, "t", parts // 2), got)
+    got = yield got
+    if together:
+        starts = [(jnp.concatenate([own, got], axis=0), [0, parts])]
+    else:
+        starts = [(own, [0]), (got, [parts])]
     placed = []
-    for first, start in ((own, 0), (got, parts)):
-        held, keys = [first[None]], [start]
+    for first, keys in starts:
+        held = [first]
         bit = parts // 2
         while bit:
-            held.append(swap(jnp.concatenate(held, axis=0), "t", bit))
-            keys += [k | bit for k in keys]
+            if together:
+                for piece in list(held):
+                    got = yield swap(piece, "t", bit)
+                    held.append(got)
+            else:
+                if first is own and len(held) == 1:
+                    got = yield own_first
+                else:
+                    got = yield swap(jnp.concatenate(held, axis=0) if len(held) > 1 else first, "t", bit)
+                held.append(got)
+            keys = keys + [k | bit for k in keys]
             bit //= 2
         flat = [piece[i] for piece in held for i in range(piece.shape[0])]
         placed += [(b, ((half * parts + part) ^ k) * block) for b, k in zip(flat, keys)]
     return placed
 
 
+def run_steps(steps, ties):
+    number, arrived = 0, next(steps)
+    while True:
+        try:
+            arrived = steps.send(ties[number](arrived) if number in ties else arrived)
+        except StopIteration as end:
+            return end.value
+        number += 1
+
+
 def assemble(placed, columns=slice(None), out=None):
     rows = sum(part.shape[0] for part, _ in placed)
     if out is None:
-        out = jnp.zeros((rows, placed[0][0][:, columns].shape[1]), placed[0][0].dtype)
+        out = blank((rows, placed[0][0][:, columns].shape[1]), placed[0][0].dtype)
     for part, start in placed:
         out = lax.dynamic_update_slice_in_dim(out, part[:, columns], start, 0)
     return out
 
 
-def to_blocks(partial):
+def to_blocks(partial, early=(), late=()):
     half, part, parts = lax.axis_index("h"), lax.axis_index("t"), lax.axis_size("t")
     both = partial.reshape(2, parts, -1, partial.shape[1])
     held = [lax.dynamic_index_in_dim(both, part ^ key, 1, keepdims=False) for key in range(parts)]
@@ -474,15 +611,19 @@
 
     bit = 1
     while 2 * bit < parts:
-        got = {key: swap(held[key].astype(BF16), "t", bit) for key in reversed(range(parts)) if held[key] is not None and key & bit}
-        for key, value in got.items():
-            held[key ^ bit] = held[key ^ bit].astype(F32) + value.astype(F32)
+        keys = [key for key in range(parts) if held[key] is not None and key & bit]
+        got = swap(jnp.stack([held[key].astype(BF16) for key in keys]), "t", bit)
+        for n, key in enumerate(keys):
+            held[key ^ bit] = held[key ^ bit].astype(F32) + got[n].astype(F32)
             held[key] = None
         bit *= 2
     far = pick(held[0], 1 - half).astype(F32) + swap(pick(held[bit], 1 - half).astype(BF16), "t", bit).astype(F32)
-    got = swap(far.astype(BF16), "h", 1).astype(F32)
-    own = pick(held[0], half).astype(F32) + swap(pick(held[bit], half).astype(BF16), "t", bit).astype(F32)
-    return jnp.where(half == 0, jnp.stack([own, got]), jnp.stack([got, own]))
+    far, near = tie(far.astype(BF16), pick(held[bit], half).astype(BF16))
+    got = swap(far, "h", 1).astype(F32)
+    own = pick(held[0], half).astype(F32) + swap(near, "t", bit).astype(F32)
+    own, early = tie(own, list(early))
+    got, own, late = tie(got, own, list(late(early) if callable(late) else late))
+    return jnp.where(half == 0, jnp.stack([own, got]), jnp.stack([got, own])), early, late
 
 
 def swaps(pieces, axis="dp"):
@@ -493,13 +634,24 @@
     return [x, swap(x, "h", 1)]
 
 
-def place_rows(blocks):
-    dp, half = lax.axis_index("dp"), lax.axis_index("h")
-    count, (rows, width) = lax.axis_size("dp"), blocks[0][0].shape
-    out = jnp.zeros((count * 2 * rows, width), blocks[0][0].dtype)
-    for k, parts in enumerate(blocks):
-        for s, part in enumerate(parts):
-            out = lax.dynamic_update_slice_in_dim(out, part, ((dp ^ s) * 2 + (half ^ k)) * rows, 0)
+def block_places():
+    dp, half, count = lax.axis_index("dp"), lax.axis_index("h"), lax.axis_size("dp")
+    return jnp.stack([(dp ^ s) * 2 + (half ^ k) for k in (0, 1) for s in range(count)]).astype(jnp.int32)
+
+
+def blank(shape, dtype):
+    return pl.pallas_call(
+        lambda out_ref: None,
+        out_specs=pl.BlockSpec(memory_space=pl.ANY),
+        out_shape=jax.ShapeDtypeStruct(shape, dtype),
+    )()
+
+
+def place_rows(blocks, places):
+    rows, width = blocks[0].shape
+    out = blank((len(blocks) * rows, width), blocks[0].dtype)
+    for k, part in enumerate(blocks):
+        out = lax.dynamic_update_slice_in_dim(out, part, places[k] * rows, 0)
     return out
 
 
@@ -549,10 +701,8 @@
     factor_one = norm_factor(inputs)
     digits = jnp.stack([positions.T // 16, positions.T % 16], axis=2).astype(BF16)
     digits = jnp.pad(digits, ((0, 0), (0, 0), (0, HEAD_DIMENSION - 2)))
-    placed = to_sequence(jnp.concatenate([(inputs * factor_one).astype(BF16), digits], axis=2))
-    normed_one = assemble(placed, slice(0, width))
-    places = assemble(placed, slice(width, width + HEAD_DIMENSION))[:, :2].astype(jnp.int32)
-    places = places[:, 0] * 16 + places[:, 1]
+    own_one = jnp.concatenate([(inputs * factor_one).astype(BF16), digits], axis=2)
+    own_one, query_proj, gate_proj = tie(own_one, query_proj, gate_proj)
 
     heads = KEY_VALUE_HEADS // parts
     pair = GROUP * HEAD_DIMENSION
@@ -571,7 +721,6 @@
         out_proj,
     )
     attn_set, gate_proj = tie(attn_set, gate_proj)
-    qkv_rows, out_rows = rows_join(swaps(attn_set, "t"), qkv_width, part)
 
     hidden = gate_proj.shape[1] // dp
     tiles = 3
@@ -585,22 +734,54 @@
         down_proj,
     )
 
-    qkv_blocks = gather_h(qkv_rows)
-    qkv_own = swaps([qkv_blocks[0]] * dp)
-    if F_AFTER_W:
-        qkv_own, ffn_set = tie(qkv_own, ffn_set)
-    ffn_got = swaps(ffn_set)
-    qkv_weight = place_rows([qkv_own, swaps([qkv_blocks[1]] * dp)])
+    def swap_h(x):
+        return swap(x, "h", 1)
+
+    def swap_dp(x, keys):
+        return [swap(x[k] if isinstance(x, (list, tuple)) else x, "dp", k) for k in keys]
+
+    near, far = range(1, dp - 1), range(dp - 1, dp)
+    bits = parts.bit_length() - 1
+    hold = {}
+
+    def first_step(x):
+        x, got, ffn_near = tie(x, swaps(attn_set, "t"), swap_dp(ffn_set, near))
+        qkv_rows, out_rows = rows_join(got, qkv_width, part)
+        hold.update(qkv=qkv_rows, out=out_rows, ffn_near=ffn_near)
+        return x
+
+    def second_step(x):
+        x, qkv_h, ffn_far, qkv_near, out_h = tie(
+            x,
+            swap_h(hold["qkv"]),
+            swap_dp(ffn_set, far),
+            swap_dp(hold["qkv"], near),
+            swap_h(hold["out"]),
+        )
+        hold.update(qkv_h=qkv_h, ffn_far=ffn_far, qkv_near=qkv_near, out_h=out_h)
+        return x
+
+    def third_step(x):
+        x, qkv_far, qkv_h_got = tie(
+            x, swap_dp(hold["qkv"], far), swap_dp(hold["qkv_h"], range(1, dp))
+        )
+        hold.update(qkv_far=qkv_far, qkv_h_got=qkv_h_got)
+        return x
+
+    placed = run_steps(sequence_steps(own_one, True), {0: first_step, 1: second_step, parts - 1: third_step})
+    normed_one = assemble(placed, slice(0, width))
+    places = assemble(placed, slice(width, width + HEAD_DIMENSION))[:, :2].astype(jnp.int32)
+    places = places[:, 0] * 16 + places[:, 1]
+    normed_one, out_rows = tie(normed_one, hold["out"])
+    qkv_blocks = [hold["qkv"], *hold["qkv_near"], *hold["qkv_far"], hold["qkv_h"], *hold["qkv_h_got"]]
+    block_at = block_places()
+    ffn_got = [ffn_set[0], *hold["ffn_near"], *hold["ffn_far"]]
     pre_rows, down_rows = rows_join(ffn_got, 2 * hidden, dp_index)
-    pre_rows, normed_one = tie(pre_rows, normed_one)
 
     def ffn_gather(x):
-        return lax.all_gather(x, ("h", "t"), axis=0, tiled=False)
-
-    def ordered(w):
-        return jnp.transpose(w.reshape(ctx, dp, depth, -1), (1, 0, 2, 3)).reshape(width, -1)
-
-    pre_all = ffn_gather(pre_rows)
+        return lax.all_gather(x, ("h", "t"), axis=0, tiled=False).reshape(ctx, dp, depth, -1)
+
+    pre_weight = ffn_gather(pre_rows)
 
     def ffn_scatter(term):
         return lax.psum_scatter(term, ("h", "t"), scatter_dimension=0, tiled=True).reshape(dp, depth, -1)
@@ -613,84 +794,109 @@
     cos = jnp.concatenate([cos, cos], axis=1)
     sin = jnp.concatenate([-sin, sin], axis=1)
     earliest = jnp.broadcast_to((jnp.arange(length, dtype=jnp.int32) - places)[None, :], (8, length))
-    out_rows, normed_one = tie(out_rows, normed_one)
-    out_blocks = gather_h(out_rows)
-    qkv = rows_product(normed_one, qkv_weight, 0, 256, F32)
-    out_blocks, qkv = tie(out_blocks, qkv)
-    out_weight = place_rows([swaps([b] * dp) for b in out_blocks])
+    out_pair = jnp.concatenate([out_rows, hold["out_h"]], axis=0)
+    qkv = blocks_product(normed_one, qkv_blocks, block_at, 256)
+    grad_own = jnp.transpose(out_grad, (1, 0, 2)).reshape(rows, width)
+    qkv, qkv_blocks, out_near, grad_own = tie(qkv, qkv_blocks, swap_dp(out_pair, near), grad_own)
     mixed = attention_forward(qkv, gains, cos, sin, earliest)
-    grad_own = jnp.transpose(out_grad, (1, 0, 2)).reshape(rows, width)
-    out_weight, mixed, grad_own = tie(out_weight, mixed, grad_own)
-    grad_rows = swaps([grad_own] * dp)
-    mixed_sum = to_blocks(rows_product(mixed, out_weight, 1, 512, BF16))
+    mixed, out_far = tie(mixed, swap_dp(out_pair, far))
+    out_pairs = [out_pair, *out_near, *out_far]
+    out_blocks = [p[: parts * depth] for p in out_pairs] + [p[parts * depth :] for p in out_pairs]
+    mixed_part = blocks_back(mixed, out_blocks, block_at, 2)
+    mixed_part, out_blocks, qkv_blocks, early = tie(
+        mixed_part, out_blocks, qkv_blocks, swap_dp(grad_own, range(1, 2))
+    )
+    qkv_weight, out_weight = place_rows(qkv_blocks, block_at), place_rows(out_blocks, block_at)
+    mixed_sum, _, (late, pre_weight, down_rows, qkv_weight, out_weight) = to_blocks(
+        mixed_part, [], [swap_dp(grad_own, range(2, dp)), pre_weight, down_rows, qkv_weight, out_weight]
+    )
     middle = (inputs + mixed_sum).reshape(rows, width)
-    pre_all, down_rows, middle = tie(pre_all, down_rows, middle)
-    pre_weight, down_weight = ordered(pre_all), ordered(ffn_gather(down_rows))
+    down_weight = ffn_gather(down_rows)
 
     factor_two = norm_factor(middle)
     own_two = (middle * factor_two).astype(BF16)
-    grad_rows, own_two = tie(grad_rows, own_two)
-    grad_rows = jnp.concatenate(grad_rows, axis=0)
-    normed_two = jnp.concatenate(swaps([own_two] * dp), axis=0)
-    pre = rows_product(normed_two, pre_weight, 0, hidden // 2, F32)
+    normed_two = swaps([own_two] * dp)
+    grad_rows = jnp.concatenate([grad_own, *early, *late], axis=0)
+    normed_two = jnp.concatenate(normed_two, axis=0)
+    pre = stacked_product(normed_two, pre_weight, hidden // 2)
     hidden_low, grad_pre = hidden_layer(pre, grad_rows, down_weight, tiles)
     down_term = term_product(grad_rows, hidden_low, dp, ctx)
     down_term, grad_pre = tie(down_term, grad_pre)
     down_sum = ffn_scatter(down_term)
-    two_part = rows_product(grad_pre, pre_weight, 1, 512, BF16, dp)
+    two_part = stacked_back(grad_pre, pre_weight, dp)
     grad_pre, two_part = tie(grad_pre, two_part)
     two_got = swaps(two_part)
     pre_term = term_product(normed_two, grad_pre, dp, ctx)
-    pre_term, two_got = tie(pre_term, two_got)
+    branch_part = stacked_back(hidden_low, down_weight, dp)
+    pre_term, branch_part, two_got = tie(pre_term, branch_part, two_got)
     grad_two = sum(g.astype(F32) for g in two_got)
-    mlp_norm_sum = jnp.sum(middle * factor_two * grad_two, axis=0)
     grad_middle = grad_own.astype(F32) + norm_back(middle, factor_two, grad_two)
     grad_mid_own = grad_middle.astype(BF16).reshape(seqs, block, width)
-    grad_mid_own, hidden_low = tie(grad_mid_own, hidden_low)
-    branch_got = swaps(rows_product(hidden_low, down_weight, 1, 512, BF16, dp))
-
-    grad_mid = assemble(to_sequence(grad_mid_own), slice(None), normed_two)
+    grad_mid_own, grad_two = tie(grad_mid_own, grad_two)
+    mlp_norm_sum = jnp.sum(middle * factor_two * grad_two, axis=0)
+
+    def to_dp(x):
+        return [lax.dynamic_index_in_dim(x, dp_index ^ k, 0, keepdims=False) for k in range(dp)]
+
+    def near_step(x):
+        x, hold["branch_near"] = tie(x, swap_dp(branch_part, near))
+        return x
+
+    def far_step(x):
+        x, hold["branch_far"], hold["mlp_sum"] = tie(x, swap_dp(branch_part, far), mlp_norm_sum)
+        return x
+
+    placed = run_steps(sequence_steps(grad_mid_own, False), {bits + 1: near_step, 2 * bits: far_step})
+    mlp_norm_sum = hold["mlp_sum"]
+    grad_mid = assemble(placed, slice(None), normed_two)
     if PRE_LATE:
         grad_mid, pre_term = tie(grad_mid, pre_term)
     pre_sum = ffn_scatter(pre_term)
     grad_mixed = rows_product(grad_mid, out_weight, 0, 256, BF16)
     out_pieces = term_pieces(grad_mid, mixed, dp_index, dp)
     grad_mixed, out_pieces = tie(grad_mixed, out_pieces)
-    out_got = swaps(out_pieces)
     grad_qkv, gain_terms = attention_backward(qkv, grad_mixed, gains, cos, sin, earliest)
+    grad_qkv, out_got = tie(grad_qkv, swap_dp(out_pieces, range(1, dp)))
+    out_keep, out_give = sum_h([out_pieces[0], *out_got])
+    grad_qkv, out_give, down_give = tie(grad_qkv, out_give, to_dp(down_sum))
     grad_one_part, norm_sums = input_product(grad_qkv, qkv_weight, normed_one, mlp_norm_sum[None], 512)
+    grad_qkv, grad_one_part = tie(grad_qkv, grad_one_part)
 
     qkv_pieces = term_pieces(normed_one, grad_qkv, dp_index, dp, norm_sums)
-    qkv_pieces, grad_one_part, branch_got, out_got = tie(qkv_pieces, grad_one_part, branch_got, out_got)
+    head_sum = total_over(jnp.sum(gain_terms, axis=0)[:2], "dp")
+    qkv_pieces, grad_one_part, out_h_got, head_sum, down_got = tie(
+        qkv_pieces, grad_one_part, swap_h(out_give), head_sum, swaps(down_give)
+    )
+    out_sum = out_keep + out_h_got.astype(F32)
     qkv_got = swaps(qkv_pieces)
-    branch = sum(g.astype(F32) for g in branch_got)
-    layer_out = (middle + branch).astype(BF16)
-    out_keep, out_give = sum_h(out_got)
-    out_sum = out_keep + swap(out_give, "h", 1).astype(F32)
-    grad_one = to_blocks(grad_one_part)
-    qkv_keep, qkv_give = sum_h(qkv_got)
-    head_norm_grad = total_over(total_over(jnp.sum(gain_terms, axis=0)[:2], "t"), "h")
-    qkv_give, out_sum, pre_sum, down_sum = tie(qkv_give, out_sum, pre_sum, down_sum)
-    qkv_sum = qkv_keep + swap(qkv_give, "h", 1).astype(F32)
-    ffn_sum = jnp.concatenate([pre_sum, down_sum], axis=2)
-    ffn_grad = swaps(
-        [lax.dynamic_index_in_dim(ffn_sum, dp_index ^ k, 0, keepdims=False) for k in range(dp)]
+
+    def late_step(early):
+        keep, hold["give"] = sum_h(early[0])
+        return [keep]
+
+    branch_got = [branch_part[0], *hold["branch_near"], *hold["branch_far"]]
+    grad_one, (_, branch_got), (qkv_keep,) = to_blocks(grad_one_part, [qkv_got, branch_got], late_step)
+    qkv_give = hold["give"]
+    layer_out = (middle + sum(g.astype(F32) for g in branch_got)).astype(BF16)
+    qkv_h_got = swap_h(qkv_give)
+    qkv_h_got, head_sum = tie(qkv_h_got, head_sum)
+    head_norm_grad = total_over(total_over(head_sum, "t"), "h")
+    grad_one, pre_give = tie(grad_one, to_dp(pre_sum))
+    pre_grad = swaps(pre_give)
+    qkv_sum = qkv_keep + qkv_h_got.astype(F32)
+    attn_sum = jnp.concatenate([qkv_sum, out_sum], axis=1).astype(BF16)
+    attn_grad = swaps(
+        [lax.dynamic_slice_in_dim(attn_sum, (part ^ k) * depth, depth, 0) for k in range(parts)], "t"
     )
     gate_grad, up_grad, down_grad = whole(
         functools.partial(ffn_join_kernel, tiles),
         [jax.ShapeDtypeStruct(gate_proj.shape, F32)] * 3,
         dp_index,
         mlp_gain,
-        *ffn_grad,
+        *pre_grad,
+        *down_got,
     )
     input_grad = grad_middle.reshape(seqs, block, width) + norm_back(inputs, factor_one, grad_one)
-
-    attn_sum = jnp.concatenate([qkv_sum, out_sum], axis=1).astype(BF16)
-    attn_sum, head_norm_grad = tie(attn_sum, head_norm_grad)
-    head_norm_grad = total_over(head_norm_grad, "dp")
-    attn_grad = swaps(
-        [lax.dynamic_slice_in_dim(attn_sum, (part ^ k) * depth, depth, 0) for k in range(parts)], "t"
-    )
     query_grad, key_grad, value_grad, out_proj_grad, norm_grads = whole(
         functools.partial(attn_join_kernel, heads),
         [

time: 822 us -> 722 us (0.88)
  waiting for transfers between devices: 438 us -> 330 us
  local copies, waits for them, and re-layouts: 80.9 us -> 64.7 us
  starting transfers between devices: 70.2 us -> 85.2 us
    ppermute x71 -> x68, waiting for transfers between devices: 437 us -> 330 us  [swap(): lax.ppermute(x, axis, [(i, i ^ bit) for i in range(lax.axis_size(axis))])]
    pallas_call x0 -> x9, Pallas kernels: none -> 63 us  [the longest x2 29.3 us: stacked_back(): pl.pallas_call(stacked_back_kernel, grid=(groups,), in_specs=[pl.BlockSpe...]
    pallas_call x6 -> x1, Pallas kernels: 64.6 us -> 5.33 us  [rows_product(): pl.pallas_call(functools.partial(rows_kernel, contract), grid=(columns //...]
    ppermute x71 -> x68, starting transfers between devices: 69.4 us -> 85 us  [swap(): lax.ppermute(x, axis, [(i, i ^ bit) for i in range(lax.axis_size(axis))])]
    transpose x1 -> x0, local copies, waits for them, and re-layouts: 11 us -> none  [ordered(): jnp.transpose(w.reshape(ctx, dp, depth, -1), (1, 0, 2, 3))]
    unnamed x96 -> x183, local copies, waits for them, and re-layouts: 12.7 us -> 20.5 us
  transfers between devices with their start and end apart: 75 -> 72, of which waited for: 34 -> 35; matrix products, arithmetic and copies ran while one was open for 12% -> 12% of each run, Pallas kernels for 18% -> 20%
where the time goes in v3:
time: 722 us; the launch traced here: 716 us
  waiting for transfers between devices  330 us (46%)
  Pallas kernels  176 us (24%)
  starting transfers between devices  85.2 us (12%)
  local copies, waits for them, and re-layouts  64.7 us (9%)
  other arithmetic  44.3 us (6%)
  between operations  15.6 us (2%)
    ppermute x68, waiting for transfers between devices, swap(): lax.ppermute(x, axis, [(i, i ^ bit) for i in range(lax.axis_size(axis))])  330 us
    ppermute x68, starting transfers between devices, swap(): lax.ppermute(x, axis, [(i, i ^ bit) for i in range(lax.axis_size(axis))])  85 us
    pallas_call x2, Pallas kernels, term_product(): pl.pallas_call(term_kernel, grid=(groups,), in_specs=[pl.BlockSpec((rows,...  29.4 us
    pallas_call x2, Pallas kernels, stacked_back(): pl.pallas_call(stacked_back_kernel, grid=(groups,), in_specs=[pl.BlockSpe...  29.3 us
    unnamed x183, local copies, waits for them, and re-layouts  20.5 us
    pallas_call x1, Pallas kernels, stacked_product(): pl.pallas_call(stacked_kernel, grid=(columns // tile,), in_specs=[pl.Bloc...  18.9 us
    pallas_call x1, Pallas kernels, attention_backward(): pl.pallas_call(functools.partial(backward_kernel, 256), grid=(heads,), in...  18.7 us
    dynamic_update_slice x24, local copies, waits for them, and re-layouts, assemble(): out = lax.dynamic_update_slice_in_dim(out, part[:, columns], start, 0)  17.1 us
  transfers between devices with their start and end apart: 72, of which 35 were waited for; matrix products, arithmetic and copies ran while one was open for 12% of the time, Pallas kernels for 20%

profile of v3, /device:TPU:0, one launch (start us, length us, event | category | flops | bytes accessed | tf_op | source)
XLA Modules:
  0.0 716.1 jit_solution(4846174471541220316)
XLA Ops:
  30.5 14.6 %collective-permute-done.2.refs_2_ = bf16[64,1536]{1,0:T(8,128)(2,1)S(1)} collective-permute-done((bf16[64,1536]{1,0:T(8,128)(2,1)S(1)}, bf16[64,1536]{1,0:T(8,128)(2,1)S(1)}, u32[]{:S(2)}, u32[]{:S(2)}) %collective-permute-start.2) | collective-permute-done | bytes 196640 | tf_op jit(solution)/shard_map/ppermute | solution.py:548
  59.8 10.3 %collective-permute-done.8.refs_3_ = bf16[64,4608]{1,0:T(8,128)(2,1)S(1)} collective-permute-done((bf16[64,4608]{1,0:T(8,128)(2,1)S(1)}, bf16[64,4608]{1,0:T(8,128)(2,1)S(1)}, u32[]{:S(2)}, u32[]{:S(2)}) %collective-permute-start.8) | collective-permute-done | bytes 589856 | tf_op jit(solution)/shard_map/ppermute | solution.py:548
  73.3 20.3 %collective-permute-done.11.refs_4_ = bf16[256,512]{1,0:T(8,128)(2,1)S(1)} collective-permute-done((bf16[256,512]{1,0:T(8,128)(2,1)S(1)}, bf16[256,512]{1,0:T(8,128)(2,1)S(1)}, u32[]{:S(2)}, u32[]{:S(2)}) %collective-permute-start.11) | collective-permute-done | bytes 262176 | tf_op jit(solution)/shard_map/ppermute | solution.py:548
  119.9 10.3 %collective-permute-done.15.refs_5_ = bf16[256,1024]{1,0:T(8,128)(2,1)S(1)} collective-permute-done((bf16[256,1024]{1,0:T(8,128)(2,1)S(1)}, bf16[256,1024]{1,0:T(8,128)(2,1)S(1)}, u32[]{:S(2)}, u32[]{:S(2)}) %collective-permute-start.15) | collective-permute-done | bytes 524320 | tf_op jit(solution)/shard_map/ppermute | solution.py:548
  145.5 9.5 %shard_map.224.qkv_ref = f32[1024,1024]{1,0:T(8,128)} custom-call(s32[8]{0:T(128)S(1)} %stack.93.where_ref, bf16[1024,2048]{1,0:T(8,128)(2,1)} %slice_dynamic-update-slice_fusion.a_ref.normed_ref, bf16[256,1024]{1,0:T(8,128)(2,1)S(1)} %get-tuple-element.258.refs_0_, bf16[256,1024]{1,0:T(8,128)(2,1)S(1)} %collective-permute-done.9.refs_1_, ...), custom_call_target="tpu_custom_call" | custom-call | flops 1048576 | bytes 65536 | tf_op jit(solution)/shard_map/pallas_call | solution.py:84
  167.0 12.5 %shard_map.226.a_ref.b_ref = bf16[1024,512]{1,0:T(8,128)(2,1)S(1)} custom-call(f32[1024,1024]{1,0:T(8,128)} %shard_map.224.qkv_ref, f32[2,128]{1,0:T(2,128)S(1)} %convert_element_type.208.gain_ref, f32[1024,128]{1,0:T(8,128)S(1)} %get-tuple-element.503.cos_ref, f32[1024,128]{1,0:T(8,128)S(1)} %get-tuple-element.504.sin_ref, ...), custom_call_target="tpu_custom_call" | custom-call | flops 1048576 | bytes 65536 | tf_op jit(solution)/shard_map/pallas_call | solution.py:471
  209.1 15.0 %collective-permute-done.23 = bf16[128,2048]{1,0:T(8,128)(2,1)S(1)} collective-permute-done((bf16[128,2048]{1,0:T(8,128)(2,1)S(1)}, bf16[128,2048]{1,0:T(8,128)(2,1)S(1)}, u32[]{:S(2)}, u32[]{:S(2)}) %collective-permute-start.23) | collective-permute-done | bytes 524320 | tf_op jit(solution)/shard_map/ppermute | solution.py:548
  229.8 17.9 %collective-permute-done.25 = bf16[128,2048]{1,0:T(8,128)(2,1)S(1)} collective-permute-done((bf16[128,2048]{1,0:T(8,128)(2,1)S(1)}, bf16[128,2048]{1,0:T(8,128)(2,1)S(1)}, u32[]{:S(2)}, u32[]{:S(2)}) %collective-permute-start.25) | collective-permute-done | bytes 524320 | tf_op jit(solution)/shard_map/ppermute | solution.py:548
  268.2 15.7 %collective-permute-done.28 = bf16[256,2048]{1,0:T(8,128)(2,1)S(1)} collective-permute-done((bf16[256,2048]{1,0:T(8,128)(2,1)S(1)}, bf16[256,2048]{1,0:T(8,128)(2,1)S(1)}, u32[]{:S(2)}, u32[]{:S(2)}) %collective-permute-start.28) | collective-permute-done | bytes 1048608 | tf_op jit(solution)/shard_map/ppermute | solution.py:548
  284.0 21.6 %collective-permute-done.29 = bf16[256,2048]{1,0:T(8,128)(2,1)S(1)} collective-permute-done((bf16[256,2048]{1,0:T(8,128)(2,1)S(1)}, bf16[256,2048]{1,0:T(8,128)(2,1)S(1)}, u32[]{:S(2)}, u32[]{:S(2)}) %collective-permute-start.29) | collective-permute-done | bytes 1048608 | tf_op jit(solution)/shard_map/ppermute | solution.py:548
  307.9 18.9 %shard_map.231.pre_ref = f32[1024,3072]{1,0:T(8,128)} custom-call(bf16[1024,2048]{1,0:T(8,128)(2,1)} %pad_maximum_fusion.a_ref, bf16[8,4,64,3072]{3,2,1,0:T(8,128)(2,1)} %bitcast.241), custom_call_target="tpu_custom_call" | custom-call | flops 1048576 | bytes 65536 | tf_op jit(solution)/shard_map/pallas_call | solution.py:142
  326.8 16.3 %shard_map.232 = (bf16[1024,1536]{1,0:T(8,128)(2,1)}, bf16[1024,3072]{1,0:T(8,128)(2,1)}) custom-call(f32[1024,3072]{1,0:T(8,128)} %shard_map.231.pre_ref, bf16[1024,2048]{1,0:T(8,128)(2,1)} %constant_dynamic-update-slice_fusion.18.grad_ref.a_ref, bf16[8,4,64,1536]{3,2,1,0:T(8,128)(2,1)} %bitcast.245), custom_call_target="tpu_custom_call" | custom-call | flops 1048576 | bytes 65536 | tf_op jit(solution)/shard_map/pallas_call | solution.py:522
  343.1 10.7 %shard_map.233 = bf16[8,4,64,1536]{3,2,1,0:T(8,128)(2,1)} custom-call(bf16[1024,2048]{1,0:T(8,128)(2,1)} %constant_dynamic-update-slice_fusion.18.grad_ref.a_ref, bf16[1024,1536]{1,0:T(8,128)(2,1)} %get-tuple-element.281.b_ref.a_ref), custom_call_target="tpu_custom_call" | custom-call | flops 1048576 | bytes 65536 | tf_op jit(solution)/shard_map/pallas_call | solution.py:190
  353.9 18.7 %shard_map.234 = (bf16[256,2048]{1,0:T(8,128)(2,1)}, bf16[256,2048]{1,0:T(8,128)(2,1)}, bf16[256,2048]{1,0:T(8,128)(2,1)}, bf16[256,2048]{1,0:T(8,128)(2,1)}) custom-call(bf16[1024,3072]{1,0:T(8,128)(2,1)} %get-tuple-element.288.a_ref.b_ref, bf16[8,4,64,3072]{3,2,1,0:T(8,128)(2,1)} %bitcast.242), custom_call_target="tpu_custom_call" | custom-call | flops 1048576 | bytes 65536 | tf_op jit(solution)/shard_map/pallas_call | solution.py:168
  376.1 10.6 %shard_map.236 = (bf16[256,2048]{1,0:T(8,128)(2,1)}, bf16[256,2048]{1,0:T(8,128)(2,1)}, bf16[256,2048]{1,0:T(8,128)(2,1)}, bf16[256,2048]{1,0:T(8,128)(2,1)}) custom-call(bf16[1024,1536]{1,0:T(8,128)(2,1)} %get-tuple-element.281.b_ref.a_ref, bf16[8,4,64,1536]{3,2,1,0:T(8,128)(2,1)} %bitcast.246), custom_call_target="tpu_custom_call" | custom-call | flops 1048576 | bytes 65536 | tf_op jit(solution)/shard_map/pallas_call | solution.py:168
  386.7 18.7 %shard_map.235 = bf16[8,4,64,3072]{3,2,1,0:T(8,128)(2,1)} custom-call(bf16[1024,2048]{1,0:T(8,128)(2,1)} %pad_maximum_fusion.a_ref, bf16[1024,3072]{1,0:T(8,128)(2,1)} %get-tuple-element.288.a_ref.b_ref), custom_call_target="tpu_custom_call" | custom-call | flops 1048576 | bytes 65536 | tf_op jit(solution)/shard_map/pallas_call | solution.py:190
  405.4 13.8 %collective-permute-done.32 = bf16[256,2048]{1,0:T(8,128)(2,1)} collective-permute-done((bf16[256,2048]{1,0:T(8,128)(2,1)}, bf16[256,2048]{1,0:T(8,128)(2,1)}, u32[]{:S(2)}, u32[]{:S(2)}) %collective-permute-start.32) | collective-permute-done | bytes 1048608 | tf_op jit(solution)/shard_map/ppermute | solution.py:548
  431.9 13.6 %collective-permute-done.34 = bf16[1,128,2048]{2,1,0:T(8,128)(2,1)S(1)} collective-permute-done((bf16[1,128,2048]{2,1,0:T(8,128)(2,1)S(1)}, bf16[1,128,2048]{2,1,0:T(8,128)(2,1)S(1)}, u32[]{:S(2)}, u32[]{:S(2)}) %collective-permute-start.34) | collective-permute-done | bytes 524320 | tf_op jit(solution)/shard_map/ppermute | solution.py:548
  466.4 9.6 %collective-permute-done.41 = bf16[256,2048]{1,0:T(8,128)(2,1)} collective-permute-done((bf16[256,2048]{1,0:T(8,128)(2,1)S(1)}, bf16[256,2048]{1,0:T(8,128)(2,1)}, u32[]{:S(2)}, u32[]{:S(2)}) %collective-permute-start.41) | collective-permute-done | bytes 1048608 | tf_op jit(solution)/shard_map/ppermute | solution.py:548
  495.3 18.7 %shard_map.239 = (bf16[1024,1024]{1,0:T(8,128)(2,1)S(1)}, f32[2,8,128]{2,1,0:T(8,128)S(1)}) custom-call(f32[1024,1024]{1,0:T(8,128)} %shard_map.224.qkv_ref, bf16[1024,512]{1,0:T(8,128)(2,1)S(1)} %copy-done.4, f32[2,128]{1,0:T(2,128)S(1)} %convert_element_type.208.gain_ref, f32[1024,128]{1,0:T(8,128)S(1)} %get-tuple-element.503.cos_ref, ...), custom_call_target="tpu_custom_call" | custom-call | flops 1048576 | bytes 65536 | tf_op jit(solution)/shard_map/pallas_call | solution.py:485
  545.6 10.4 %shard_map.241 = (bf16[512,1152]{1,0:T(8,128)(2,1)}, bf16[512,1152]{1,0:T(8,128)(2,1)}, bf16[512,1152]{1,0:T(8,128)(2,1)}, bf16[512,1152]{1,0:T(8,128)(2,1)}) custom-call(s32[1]{0:T(128)} %bitcast.15.me_ref, bf16[1024,2048]{1,0:T(8,128)(2,1)} %slice_dynamic-update-slice_fusion.a_ref.normed_ref, bf16[1024,1024]{1,0:T(8,128)(2,1)} %copy-done.2, ...), custom_call_target="tpu_custom_call" | custom-call | flops 1048576 | bytes 65536 | tf_op jit(solution)/shard_map/pallas_call | solution.py:230
  562.4 25.6 %collective-permute-done.52 = bf16[128,2048]{1,0:T(8,128)(2,1)S(1)} collective-permute-done((bf16[128,2048]{1,0:T(8,128)(2,1)S(1)}, bf16[128,2048]{1,0:T(8,128)(2,1)S(1)}, u32[]{:S(2)}, u32[]{:S(2)}) %collective-permute-start.52) | collective-permute-done | bytes 524320 | tf_op jit(solution)/shard_map/ppermute | solution.py:548
  592.0 37.6 %collective-permute-done.53 = bf16[128,2048]{1,0:T(8,128)(2,1)} collective-permute-done((bf16[128,2048]{1,0:T(8,128)(2,1)}, bf16[128,2048]{1,0:T(8,128)(2,1)}, u32[]{:S(2)}, u32[]{:S(2)}) %collective-permute-start.53) | collective-permute-done | bytes 524320 | tf_op jit(solution)/shard_map/ppermute | solution.py:548
  643.4 25.1 %collective-permute-done.58 = bf16[256,1152]{1,0:T(8,128)(2,1)S(1)} collective-permute-done((bf16[256,1152]{1,0:T(8,128)(2,1)S(1)}, bf16[256,1152]{1,0:T(8,128)(2,1)S(1)}, u32[]{:S(2)}, u32[]{:S(2)}) %collective-permute-start.58) | collective-permute-done | bytes 589856 | tf_op jit(solution)/shard_map/ppermute | solution.py:548
  (457 shorter events, 304.6 us)
Async XLA Ops:
  7.2 247.2 %all-gather.5.cloned.1.call-start = ((), (), s32[]{:S(2)}) async-start(), calls=%async_computation.4 | async-start | bytes 14155776 | tf_op jit(solution)/shard_map/all_gather | solution.py:782
  19.3 32.5 %collective-permute-start.4 = (bf16[64,4608]{1,0:T(8,128)(2,1)}, bf16[64,4608]{1,0:T(8,128)(2,1)S(1)}, u32[]{:S(2)}, u32[]{:S(2)}) collective-permute-start(bf16[64,4608]{1,0:T(8,128)(2,1)} %get-tuple-element.213), channel_id=1, source_target_pairs={{0,8},{8,0},{16,24},{24,16},{1,9},{9,1},{17,25},{25,17},{2,10},{10... | collective-permute-start | bytes 1769480 | tf_op jit(solution)/shard_map/ppermute | solution.py:548
  52.0 42.3 %collective-permute-start.6 = (bf16[2,128,2176]{2,1,0:T(8,128)(2,1)S(1)}, bf16[2,128,2176]{2,1,0:T(8,128)(2,1)S(1)}, u32[]{:S(2)}, u32[]{:S(2)}) collective-permute-start(bf16[2,128,2176]{2,1,0:T(8,128)(2,1)S(1)} %pad_maximum_fusion.4), channel_id=1, source_target_pairs={{0,2},{1,3},{2,0},{3,1},{4,6},{5,7},{6,4},{7,5},{8,10},{9,11},{10,... | collective-permute-start | bytes 3342344 | tf_op jit(solution)/shard_map/ppermute | solution.py:548
  53.4 40.2 %collective-permute-start.10 = (bf16[256,1024]{1,0:T(8,128)(2,1)S(1)}, bf16[256,1024]{1,0:T(8,128)(2,1)S(1)}, u32[]{:S(2)}, u32[]{:S(2)}) collective-permute-start(bf16[256,1024]{1,0:T(8,128)(2,1)S(1)} %get-tuple-element.258.refs_0_), channel_id=1, source_target_pairs={{0,16},{8,24},{16,0},{24,8},{1,17},{9,25},{17,1},{25,9},{2,18},{10... | collective-permute-start | bytes 1572872 | tf_op jit(solution)/shard_map/ppermute | solution.py:548
  55.0 38.6 %collective-permute-start.7 = (bf16[256,1024]{1,0:T(8,128)(2,1)S(1)}, bf16[256,1024]{1,0:T(8,128)(2,1)S(1)}, u32[]{:S(2)}, u32[]{:S(2)}) collective-permute-start(bf16[256,1024]{1,0:T(8,128)(2,1)S(1)} %get-tuple-element.258.refs_0_), channel_id=1, source_target_pairs={{0,4},{4,0},{1,5},{5,1},{2,6},{6,2},{3,7},{7,3},{8,12},{12,8},{9,1... | collective-permute-start | bytes 1572872 | tf_op jit(solution)/shard_map/ppermute | solution.py:548
  58.3 35.3 %collective-permute-start.9 = (bf16[256,1024]{1,0:T(8,128)(2,1)S(1)}, bf16[256,1024]{1,0:T(8,128)(2,1)S(1)}, u32[]{:S(2)}, u32[]{:S(2)}) collective-permute-start(bf16[256,1024]{1,0:T(8,128)(2,1)S(1)} %get-tuple-element.258.refs_0_), channel_id=1, source_target_pairs={{0,8},{8,0},{16,24},{24,16},{1,9},{9,1},{17,25},{25,17},{2,10},{10... | collective-permute-start | bytes 1572872 | tf_op jit(solution)/shard_map/ppermute | solution.py:548
  99.7 227.1 %all-gather.7.cloned.1.call-start = ((), (), s32[]{:S(2)}) async-start(), calls=%async_computation.5 | async-start | bytes 7077888 | tf_op jit(solution)/shard_map/all_gather | solution.py:782
  142.9 36.7 %collective-permute-start.20 = (bf16[512,512]{1,0:T(8,128)(2,1)S(1)}, bf16[512,512]{1,0:T(8,128)(2,1)S(1)}, u32[]{:S(2)}, u32[]{:S(2)}) collective-permute-start(bf16[512,512]{1,0:T(8,128)(2,1)S(1)} %constant_dynamic-update-slice_fusion.16), channel_id=1, source_target_pairs={{0,24},{8,16},{16,8},{24,0},{1,25},{9,17},{17,9},{25,1},{2,26},{10... | collective-permute-start | bytes 1572872 | tf_op jit(solution)/shard_map/ppermute | solution.py:548
  190.8 63.6 %collective-permute-start.26 = (bf16[256,2048]{1,0:T(8,128)(2,1)}, bf16[256,2048]{1,0:T(8,128)(2,1)}, u32[]{:S(2)}, u32[]{:S(2)}) collective-permute-start(bf16[256,2048]{1,0:T(8,128)(2,1)} %bitcast.250), channel_id=1, source_target_pairs={{0,16},{8,24},{16,0},{24,8},{1,17},{9,25},{17,1},{25,9},{2,18},{10... | collective-permute-start | bytes 3145736 | tf_op jit(solution)/shard_map/ppermute | solution.py:548
  191.4 63.0 %collective-permute-start.27 = (bf16[256,2048]{1,0:T(8,128)(2,1)}, bf16[256,2048]{1,0:T(8,128)(2,1)}, u32[]{:S(2)}, u32[]{:S(2)}) collective-permute-start(bf16[256,2048]{1,0:T(8,128)(2,1)} %bitcast.251), channel_id=1, source_target_pairs={{0,24},{8,16},{16,8},{24,0},{1,25},{9,17},{17,9},{25,1},{2,26},{10... | collective-permute-start | bytes 3145736 | tf_op jit(solution)/shard_map/ppermute | solution.py:548
  254.4 265.5 %reduce-scatter.3.cloned.1.call-start = ((), (), s32[]{:S(2)}) async-start(), calls=%async_computation.2 | async-start | bytes 7077888 | tf_op jit(solution)/shard_map/reduce_scatter | solution.py:787
  259.5 46.0 %collective-permute-start.29 = (bf16[256,2048]{1,0:T(8,128)(2,1)S(1)}, bf16[256,2048]{1,0:T(8,128)(2,1)S(1)}, u32[]{:S(2)}, u32[]{:S(2)}) collective-permute-start(bf16[256,2048]{1,0:T(8,128)(2,1)S(1)} %fusion.13), channel_id=1, source_target_pairs={{0,16},{8,24},{16,0},{24,8},{1,17},{9,25},{17,1},{25,9},{2,18},{10... | collective-permute-start | bytes 3145736 | tf_op jit(solution)/shard_map/ppermute | solution.py:548
  261.0 44.6 %collective-permute-start.30 = (bf16[256,2048]{1,0:T(8,128)(2,1)S(1)}, bf16[256,2048]{1,0:T(8,128)(2,1)S(1)}, u32[]{:S(2)}, u32[]{:S(2)}) collective-permute-start(bf16[256,2048]{1,0:T(8,128)(2,1)S(1)} %fusion.13), channel_id=1, source_target_pairs={{0,24},{8,16},{16,8},{24,0},{1,25},{9,17},{17,9},{25,1},{2,26},{10... | collective-permute-start | bytes 3145736 | tf_op jit(solution)/shard_map/ppermute | solution.py:548
  353.8 330.9 %reduce-scatter.5.cloned.1.call-start = ((), (), s32[]{:S(2)}) async-start(), calls=%async_computation.3 | async-start | bytes 14155776 | tf_op jit(solution)/shard_map/reduce_scatter | solution.py:787
  372.6 32.9 %collective-permute-start.31 = (bf16[256,2048]{1,0:T(8,128)(2,1)}, bf16[256,2048]{1,0:T(8,128)(2,1)}, u32[]{:S(2)}, u32[]{:S(2)}) collective-permute-start(bf16[256,2048]{1,0:T(8,128)(2,1)} %get-tuple-element.294), channel_id=1, source_target_pairs={{0,8},{8,0},{16,24},{24,16},{1,9},{9,1},{17,25},{25,17},{2,10},{10... | collective-permute-start | bytes 3145736 | tf_op jit(solution)/shard_map/ppermute | solution.py:548
  373.7 45.5 %collective-permute-start.32 = (bf16[256,2048]{1,0:T(8,128)(2,1)}, bf16[256,2048]{1,0:T(8,128)(2,1)}, u32[]{:S(2)}, u32[]{:S(2)}) collective-permute-start(bf16[256,2048]{1,0:T(8,128)(2,1)} %get-tuple-element.295), channel_id=1, source_target_pairs={{0,16},{8,24},{16,0},{24,8},{1,17},{9,25},{17,1},{25,9},{2,18},{10... | collective-permute-start | bytes 3145736 | tf_op jit(solution)/shard_map/ppermute | solution.py:548
  374.6 44.6 %collective-permute-start.33 = (bf16[256,2048]{1,0:T(8,128)(2,1)}, bf16[256,2048]{1,0:T(8,128)(2,1)}, u32[]{:S(2)}, u32[]{:S(2)}) collective-permute-start(bf16[256,2048]{1,0:T(8,128)(2,1)} %get-tuple-element.296), channel_id=1, source_target_pairs={{0,24},{8,16},{16,8},{24,0},{1,25},{9,17},{17,9},{25,1},{2,26},{10... | collective-permute-start | bytes 3145736 | tf_op jit(solution)/shard_map/ppermute | solution.py:548
  430.1 32.5 %collective-permute-start.38 = (bf16[256,2048]{1,0:T(8,128)(2,1)S(1)}, bf16[256,2048]{1,0:T(8,128)(2,1)S(1)}, u32[]{:S(2)}, u32[]{:S(2)}) collective-permute-start(bf16[256,2048]{1,0:T(8,128)(2,1)S(1)} %copy-done.85), channel_id=1, source_target_pairs={{0,8},{8,0},{16,24},{24,16},{1,9},{9,1},{17,25},{25,17},{2,10},{10... | collective-permute-start | bytes 3145736 | tf_op jit(solution)/shard_map/ppermute | solution.py:548
  521.9 34.2 %collective-permute-start.45 = (bf16[256,512]{1,0:T(8,128)(2,1)}, bf16[256,512]{1,0:T(8,128)(2,1)}, u32[]{:S(2)}, u32[]{:S(2)}) collective-permute-start(bf16[256,512]{1,0:T(8,128)(2,1)} %fusion.24), channel_id=1, source_target_pairs={{0,4},{4,0},{1,5},{5,1},{2,6},{6,2},{3,7},{7,3},{8,12},{12,8},{9,1... | collective-permute-start | bytes 786440 | tf_op jit(solution)/shard_map/ppermute | solution.py:548
  556.6 74.1 %collective-permute-start.54 = (bf16[512,1152]{1,0:T(8,128)(2,1)}, bf16[512,1152]{1,0:T(8,128)(2,1)}, u32[]{:S(2)}, u32[]{:S(2)}) collective-permute-start(bf16[512,1152]{1,0:T(8,128)(2,1)} %get-tuple-element.348), channel_id=1, source_target_pairs={{0,8},{8,0},{16,24},{24,16},{1,9},{9,1},{17,25},{25,17},{2,10},{10... | collective-permute-start | bytes 3538952 | tf_op jit(solution)/shard_map/ppermute | solution.py:548
  557.9 72.8 %collective-permute-start.55 = (bf16[512,1152]{1,0:T(8,128)(2,1)}, bf16[512,1152]{1,0:T(8,128)(2,1)}, u32[]{:S(2)}, u32[]{:S(2)}) collective-permute-start(bf16[512,1152]{1,0:T(8,128)(2,1)} %get-tuple-element.349), channel_id=1, source_target_pairs={{0,16},{8,24},{16,0},{24,8},{1,17},{9,25},{17,1},{25,9},{2,18},{10... | collective-permute-start | bytes 3538952 | tf_op jit(solution)/shard_map/ppermute | solution.py:548
  558.6 72.1 %collective-permute-start.56 = (bf16[512,1152]{1,0:T(8,128)(2,1)}, bf16[512,1152]{1,0:T(8,128)(2,1)}, u32[]{:S(2)}, u32[]{:S(2)}) collective-permute-start(bf16[512,1152]{1,0:T(8,128)(2,1)} %get-tuple-element.350), channel_id=1, source_target_pairs={{0,24},{8,16},{16,8},{24,0},{1,25},{9,17},{17,9},{25,1},{2,26},{10... | collective-permute-start | bytes 3538952 | tf_op jit(solution)/shard_map/ppermute | solution.py:548
  588.9 40.6 %collective-permute-start.53 = (bf16[128,2048]{1,0:T(8,128)(2,1)}, bf16[128,2048]{1,0:T(8,128)(2,1)}, u32[]{:S(2)}, u32[]{:S(2)}) collective-permute-start(bf16[128,2048]{1,0:T(8,128)(2,1)} %get-tuple-element.346), channel_id=1, source_target_pairs={{0,2},{1,3},{2,0},{3,1},{4,6},{5,7},{6,4},{7,5},{8,10},{9,11},{10,... | collective-permute-start | bytes 1572872 | tf_op jit(solution)/shard_map/ppermute | solution.py:548
  588.9 46.0 %collective-permute-start.57 = (bf16[128,2048]{1,0:T(8,128)(2,1)}, bf16[128,2048]{1,0:T(8,128)(2,1)S(1)}, u32[]{:S(2)}, u32[]{:S(2)}) collective-permute-start(bf16[128,2048]{1,0:T(8,128)(2,1)} %fusion.14), channel_id=1, source_target_pairs={{0,4},{4,0},{1,5},{5,1},{2,6},{6,2},{3,7},{7,3},{8,12},{12,8},{9,1... | collective-permute-start | bytes 1572872 | tf_op jit(solution)/shard_map/ppermute | solution.py:548
  (137 other events, 1932.8 us)
Sparse Core Ops, SparseCore 0:
  99.8 117.0 all-gather.4
  254.6 65.8 all-gather.6
  353.9 69.9 reduce-scatter.2
  477.8 170.9 reduce-scatter.4

commit v4 on v3

--- a/solution.py
+++ b/solution.py
@@ -268,16 +268,22 @@
     )(grad, weight, normed, other)
 
 
-def whole(kernel, shapes, me, *arrays):
+def whole(kernel, shapes, me, *arrays, seen=()):
     vmem = pl.BlockSpec(memory_space=pltpu.VMEM)
-    return pl.pallas_call(
-        kernel,
-        in_specs=[pl.BlockSpec(memory_space=pltpu.SMEM)] + [vmem] * len(arrays),
+
+    def body(me_ref, *refs):
+        kernel(me_ref, *refs[: len(arrays)], *refs[len(arrays) + len(seen) :])
+
+    return pl.pallas_call(
+        body,
+        in_specs=[pl.BlockSpec(memory_space=pltpu.SMEM)]
+        + [vmem] * len(arrays)
+        + [pl.BlockSpec(memory_space=pl.ANY)] * len(seen),
         out_specs=[vmem] * len(shapes),
         out_shape=shapes,
         compiler_params=pltpu.CompilerParams(vmem_limit_bytes=48 << 20),
         cost_estimate=CHEAP,
-    )(me.reshape(1).astype(jnp.int32), *arrays)
+    )(me.reshape(1).astype(jnp.int32), *arrays, *seen)
 
 
 def lanes(index, size):
@@ -548,11 +554,15 @@
     return lax.ppermute(x, axis, [(i, i ^ bit) for i in range(lax.axis_size(axis))])
 
 
-def sequence_steps(blocks, together):
+def own_and_other(blocks):
+    half = lax.axis_index("h")
+    return [lax.dynamic_index_in_dim(blocks, k, 0, keepdims=True) for k in (half, 1 - half)]
+
+
+def sequence_steps(own, give, together):
     half, part, parts = lax.axis_index("h"), lax.axis_index("t"), lax.axis_size("t")
-    block = blocks.shape[1]
-    own = lax.dynamic_index_in_dim(blocks, half, 0, keepdims=True)
-    got = swap(lax.dynamic_index_in_dim(blocks, 1 - half, 0, keepdims=True), "h", 1)
+    block = own.shape[1]
+    got = swap(give, "h", 1)
     if not together:
         own_first, got = tie(swap(own, "t", parts // 2), got)
     got = yield got
@@ -601,7 +611,7 @@
     return out
 
 
-def to_blocks(partial, early=(), late=()):
+def to_blocks(partial, late=(), on_first=None, on_last=None):
     half, part, parts = lax.axis_index("h"), lax.axis_index("t"), lax.axis_size("t")
     both = partial.reshape(2, parts, -1, partial.shape[1])
     held = [lax.dynamic_index_in_dim(both, part ^ key, 1, keepdims=False) for key in range(parts)]
@@ -617,13 +627,17 @@
             held[key ^ bit] = held[key ^ bit].astype(F32) + got[n].astype(F32)
             held[key] = None
         bit *= 2
-    far = pick(held[0], 1 - half).astype(F32) + swap(pick(held[bit], 1 - half).astype(BF16), "t", bit).astype(F32)
+    first = swap(pick(held[bit], 1 - half).astype(BF16), "t", bit)
+    if on_first is not None:
+        on_first(first)
+    far = pick(held[0], 1 - half).astype(F32) + first.astype(F32)
     far, near = tie(far.astype(BF16), pick(held[bit], half).astype(BF16))
-    got = swap(far, "h", 1).astype(F32)
+    got = swap(far, "h", 1)
+    if on_last is not None:
+        got = on_last(got)
     own = pick(held[0], half).astype(F32) + swap(near, "t", bit).astype(F32)
-    own, early = tie(own, list(early))
-    got, own, late = tie(got, own, list(late(early) if callable(late) else late))
-    return jnp.where(half == 0, jnp.stack([own, got]), jnp.stack([got, own])), early, late
+    got, own, late = tie(got.astype(F32), own, list(late))
+    return jnp.where(half == 0, jnp.stack([own, got]), jnp.stack([got, own])), late
 
 
 def swaps(pieces, axis="dp"):
@@ -702,7 +716,7 @@
     digits = jnp.stack([positions.T // 16, positions.T % 16], axis=2).astype(BF16)
     digits = jnp.pad(digits, ((0, 0), (0, 0), (0, HEAD_DIMENSION - 2)))
     own_one = jnp.concatenate([(inputs * factor_one).astype(BF16), digits], axis=2)
-    own_one, query_proj, gate_proj = tie(own_one, query_proj, gate_proj)
+    own_one, query_proj, gate_proj = tie(own_and_other(own_one), query_proj, gate_proj)
 
     heads = KEY_VALUE_HEADS // parts
     pair = GROUP * HEAD_DIMENSION
@@ -751,29 +765,26 @@
         return x
 
     def second_step(x):
-        x, qkv_h, ffn_far, qkv_near, out_h = tie(
+        x, qkv_h, ffn_far, qkv_got, out_h = tie(
             x,
             swap_h(hold["qkv"]),
             swap_dp(ffn_set, far),
-            swap_dp(hold["qkv"], near),
+            swap_dp(hold["qkv"], range(1, dp)),
             swap_h(hold["out"]),
         )
-        hold.update(qkv_h=qkv_h, ffn_far=ffn_far, qkv_near=qkv_near, out_h=out_h)
+        hold.update(qkv_h=qkv_h, ffn_far=ffn_far, qkv_got=qkv_got, out_h=out_h)
         return x
 
     def third_step(x):
-        x, qkv_far, qkv_h_got = tie(
-            x, swap_dp(hold["qkv"], far), swap_dp(hold["qkv_h"], range(1, dp))
-        )
-        hold.update(qkv_far=qkv_far, qkv_h_got=qkv_h_got)
+        x, hold["qkv_h_got"] = tie(x, swap_dp(hold["qkv_h"], range(1, dp)))
         return x
 
-    placed = run_steps(sequence_steps(own_one, True), {0: first_step, 1: second_step, parts - 1: third_step})
+    placed = run_steps(sequence_steps(*own_one, True), {0: first_step, 1: second_step, parts - 1: third_step})
     normed_one = assemble(placed, slice(0, width))
     places = assemble(placed, slice(width, width + HEAD_DIMENSION))[:, :2].astype(jnp.int32)
     places = places[:, 0] * 16 + places[:, 1]
     normed_one, out_rows = tie(normed_one, hold["out"])
-    qkv_blocks = [hold["qkv"], *hold["qkv_near"], *hold["qkv_far"], hold["qkv_h"], *hold["qkv_h_got"]]
+    qkv_blocks = [hold["qkv"], *hold["qkv_got"], hold["qkv_h"], *hold["qkv_h_got"]]
     block_at = block_places()
     ffn_got = [ffn_set[0], *hold["ffn_near"], *hold["ffn_far"]]
     pre_rows, down_rows = rows_join(ffn_got, 2 * hidden, dp_index)
@@ -807,8 +818,8 @@
         mixed_part, out_blocks, qkv_blocks, swap_dp(grad_own, range(1, 2))
     )
     qkv_weight, out_weight = place_rows(qkv_blocks, block_at), place_rows(out_blocks, block_at)
-    mixed_sum, _, (late, pre_weight, down_rows, qkv_weight, out_weight) = to_blocks(
-        mixed_part, [], [swap_dp(grad_own, range(2, dp)), pre_weight, down_rows, qkv_weight, out_weight]
+    mixed_sum, (late, pre_weight, down_rows, qkv_weight, out_weight) = to_blocks(
+        mixed_part, [swap_dp(grad_own, range(2, dp)), pre_weight, down_rows, qkv_weight, out_weight]
     )
     middle = (inputs + mixed_sum).reshape(rows, width)
     down_weight = ffn_gather(down_rows)
@@ -842,11 +853,13 @@
         x, hold["branch_near"] = tie(x, swap_dp(branch_part, near))
         return x
 
-    def far_step(x):
-        x, hold["branch_far"], hold["mlp_sum"] = tie(x, swap_dp(branch_part, far), mlp_norm_sum)
+    def last_step(x):
+        x, hold["mlp_sum"] = tie(x, mlp_norm_sum)
         return x
 
-    placed = run_steps(sequence_steps(grad_mid_own, False), {bits + 1: near_step, 2 * bits: far_step})
+    placed = run_steps(
+        sequence_steps(*own_and_other(grad_mid_own), False), {bits + 1: near_step, 2 * bits: last_step}
+    )
     mlp_norm_sum = hold["mlp_sum"]
     grad_mid = assemble(placed, slice(None), normed_two)
     if PRE_LATE:
@@ -854,40 +867,62 @@
     pre_sum = ffn_scatter(pre_term)
     grad_mixed = rows_product(grad_mid, out_weight, 0, 256, BF16)
     out_pieces = term_pieces(grad_mid, mixed, dp_index, dp)
-    grad_mixed, out_pieces = tie(grad_mixed, out_pieces)
+    grad_mixed, out_pieces, hold["branch_far"] = tie(grad_mixed, out_pieces, swap_dp(branch_part, far))
     grad_qkv, gain_terms = attention_backward(qkv, grad_mixed, gains, cos, sin, earliest)
-    grad_qkv, out_got = tie(grad_qkv, swap_dp(out_pieces, range(1, dp)))
+    hops = [
+        (axis, 1 << k) for axis in ("dp", "t", "h") for k in range(lax.axis_size(axis).bit_length() - 1)
+    ]
+    hold["head"] = jnp.sum(gain_terms, axis=0)[:2]
+
+    def hop():
+        axis, bit = hops.pop(0)
+        return swap(hold["head"], axis, bit)
+
+    grad_one_part, norm_sums = input_product(grad_qkv, qkv_weight, normed_one, mlp_norm_sum[None], 512)
+    grad_qkv, grad_one_part, out_got, down_give, head = tie(
+        grad_qkv, grad_one_part, swap_dp(out_pieces, range(1, dp)), to_dp(down_sum), hop()
+    )
+    hold["head"] += head
     out_keep, out_give = sum_h([out_pieces[0], *out_got])
-    grad_qkv, out_give, down_give = tie(grad_qkv, out_give, to_dp(down_sum))
-    grad_one_part, norm_sums = input_product(grad_qkv, qkv_weight, normed_one, mlp_norm_sum[None], 512)
-    grad_qkv, grad_one_part = tie(grad_qkv, grad_one_part)
 
     qkv_pieces = term_pieces(normed_one, grad_qkv, dp_index, dp, norm_sums)
-    head_sum = total_over(jnp.sum(gain_terms, axis=0)[:2], "dp")
-    qkv_pieces, grad_one_part, out_h_got, head_sum, down_got = tie(
-        qkv_pieces, grad_one_part, swap_h(out_give), head_sum, swaps(down_give)
-    )
-    out_sum = out_keep + out_h_got.astype(F32)
+    qkv_pieces, grad_one_part, down_got, head = tie(qkv_pieces, grad_one_part, swaps(down_give), hop())
+    hold["head"] += head
     qkv_got = swaps(qkv_pieces)
-
-    def late_step(early):
-        keep, hold["give"] = sum_h(early[0])
-        return [keep]
-
     branch_got = [branch_part[0], *hold["branch_near"], *hold["branch_far"]]
-    grad_one, (_, branch_got), (qkv_keep,) = to_blocks(grad_one_part, [qkv_got, branch_got], late_step)
-    qkv_give = hold["give"]
-    layer_out = (middle + sum(g.astype(F32) for g in branch_got)).astype(BF16)
-    qkv_h_got = swap_h(qkv_give)
-    qkv_h_got, head_sum = tie(qkv_h_got, head_sum)
-    head_norm_grad = total_over(total_over(head_sum, "t"), "h")
-    grad_one, pre_give = tie(grad_one, to_dp(pre_sum))
-    pre_grad = swaps(pre_give)
-    qkv_sum = qkv_keep + qkv_h_got.astype(F32)
-    attn_sum = jnp.concatenate([qkv_sum, out_sum], axis=1).astype(BF16)
-    attn_grad = swaps(
-        [lax.dynamic_slice_in_dim(attn_sum, (part ^ k) * depth, depth, 0) for k in range(parts)], "t"
-    )
+    seen = []
+
+    def gradients_step(first):
+        got, first, out_h, head, hold["branch"] = tie(qkv_got, first, swap_h(out_give), hop(), branch_got)
+        hold["head"] += head
+        seen.append(first)
+        hold["out_h_got"] = out_h
+        hold["qkv_keep"], hold["qkv_give"] = sum_h(got)
+
+    def last_swap_step(got):
+        qkv_h_got, head = tie(swap_h(hold["qkv_give"]), hop())
+        hold["head"] += head
+        attn_sum = hold["qkv_keep"] + qkv_h_got.astype(F32)
+        out_sum = out_keep + hold["out_h_got"].astype(F32)
+        attn_sum, pre_give = tie(jnp.concatenate([attn_sum, out_sum], axis=1).astype(BF16), to_dp(pre_sum))
+        attn_got = swaps(
+            [lax.dynamic_slice_in_dim(attn_sum, (part ^ k) * depth, depth, 0) for k in range(parts)], "t"
+        )
+        while len(hops) > 1:
+            hold["head"] += hop()
+        hold["pre_got"] = swaps(pre_give)
+        got, hold["attn_got"], head = tie(got, attn_got, hop())
+        hold["head"] += head
+        return got
+
+    grad_one, _ = to_blocks(grad_one_part, [], gradients_step, last_swap_step)
+    attn_grad, pre_grad = hold["attn_got"], hold["pre_got"]
+    head_norm_grad = hold["head"]
+    layer_out = (middle + sum(g.astype(F32) for g in hold["branch"])).astype(BF16)
+    input_grad = grad_middle.reshape(seqs, block, width) + norm_back(inputs, factor_one, grad_one)
+    layer_out = jnp.transpose(layer_out.reshape(seqs, block, width), (1, 0, 2))
+    input_grad = jnp.transpose(input_grad, (1, 0, 2))
+    pre_grad, input_grad, layer_out = tie(pre_grad, input_grad, layer_out)
     gate_grad, up_grad, down_grad = whole(
         functools.partial(ffn_join_kernel, tiles),
         [jax.ShapeDtypeStruct(gate_proj.shape, F32)] * 3,
@@ -896,7 +931,6 @@
         *pre_grad,
         *down_got,
     )
-    input_grad = grad_middle.reshape(seqs, block, width) + norm_back(inputs, factor_one, grad_one)
     query_grad, key_grad, value_grad, out_proj_grad, norm_grads = whole(
         functools.partial(attn_join_kernel, heads),
         [
@@ -906,12 +940,11 @@
         part,
         attn_gain,
         *attn_grad,
+        seen=seen,
     )
     attn_norm_grad = norm_grads[:, 0] / attn_gain[:, 0]
     mlp_norm_grad = norm_grads[:, 1] / mlp_gain[:, 0]
 
-    layer_out = jnp.transpose(layer_out.reshape(seqs, block, width), (1, 0, 2))
-    input_grad = jnp.transpose(input_grad, (1, 0, 2))
     return (
         layer_out,
         input_grad,

time: 722 us -> 693 us (0.960)
  waiting for transfers between devices: 330 us -> 313 us
  starting transfers between devices: 85.2 us -> 76.6 us
    ppermute x68, waiting for transfers between devices: 330 us -> 313 us  [swap(): lax.ppermute(x, axis, [(i, i ^ bit) for i in range(lax.axis_size(axis))])]
    ppermute x68, starting transfers between devices: 85 us -> 76.4 us  [swap(): lax.ppermute(x, axis, [(i, i ^ bit) for i in range(lax.axis_size(axis))])]
    unnamed x183 -> x172, local copies, waits for them, and re-layouts: 20.5 us -> 17.3 us
  transfers between devices with their start and end apart: 72 -> 72, of which waited for: 35 -> 32; matrix products, arithmetic and copies ran while one was open for 12% -> 12% of each run, Pallas kernels for 20% -> 21%
where the time goes in v4:
time: 693 us; the launch traced here: 687 us
  waiting for transfers between devices  313 us (45%)
  Pallas kernels  176 us (25%)
  starting transfers between devices  76.6 us (11%)
  local copies, waits for them, and re-layouts  60.6 us (9%)
  other arithmetic  45.2 us (7%)
  between operations  15.6 us (2%)
    ppermute x68, waiting for transfers between devices, swap(): lax.ppermute(x, axis, [(i, i ^ bit) for i in range(lax.axis_size(axis))])  313 us
    ppermute x68, starting transfers between devices, swap(): lax.ppermute(x, axis, [(i, i ^ bit) for i in range(lax.axis_size(axis))])  76.4 us
    pallas_call x2, Pallas kernels, term_product(): pl.pallas_call(term_kernel, grid=(groups,), in_specs=[pl.BlockSpec((rows,...  29.5 us
    pallas_call x2, Pallas kernels, stacked_back(): pl.pallas_call(stacked_back_kernel, grid=(groups,), in_specs=[pl.BlockSpe...  29.3 us
    pallas_call x1, Pallas kernels, stacked_product(): pl.pallas_call(stacked_kernel, grid=(columns // tile,), in_specs=[pl.Bloc...  18.8 us
    pallas_call x1, Pallas kernels, attention_backward(): pl.pallas_call(functools.partial(backward_kernel, 256), grid=(heads,), in...  18.7 us
    dynamic_update_slice x24, local copies, waits for them, and re-layouts, assemble(): out = lax.dynamic_update_slice_in_dim(out, part[:, columns], start, 0)  17.8 us
    pallas_call x2, Pallas kernels, term_pieces(): pl.pallas_call(pieces_kernel, grid_spec=pltpu.PrefetchScalarGridSpec(num_...  17.4 us
  transfers between devices with their start and end apart: 72, of which 32 were waited for; matrix products, arithmetic and copies ran while one was open for 12% of the time, Pallas kernels for 21%

profile of v4, /device:TPU:0, one launch (start us, length us, event | category | flops | bytes accessed | tf_op | source)
XLA Modules:
  0.0 687.0 jit_solution(8153378570853817860)
XLA Ops:
  27.6 14.3 %collective-permute-done.2.refs_2_ = bf16[64,1536]{1,0:T(8,128)(2,1)S(1)} collective-permute-done((bf16[64,1536]{1,0:T(8,128)(2,1)S(1)}, bf16[64,1536]{1,0:T(8,128)(2,1)S(1)}, u32[]{:S(2)}, u32[]{:S(2)}) %collective-permute-start.2) | collective-permute-done | bytes 196640 | tf_op jit(solution)/shard_map/ppermute | solution.py:554
  57.2 23.5 %collective-permute-done.12.refs_4_ = bf16[256,512]{1,0:T(8,128)(2,1)S(1)} collective-permute-done((bf16[256,512]{1,0:T(8,128)(2,1)S(1)}, bf16[256,512]{1,0:T(8,128)(2,1)S(1)}, u32[]{:S(2)}, u32[]{:S(2)}) %collective-permute-start.12) | collective-permute-done | bytes 262176 | tf_op jit(solution)/shard_map/ppermute | solution.py:554
  119.1 11.0 %collective-permute-done.16.refs_6_ = bf16[256,1024]{1,0:T(8,128)(2,1)S(1)} collective-permute-done((bf16[256,1024]{1,0:T(8,128)(2,1)S(1)}, bf16[256,1024]{1,0:T(8,128)(2,1)S(1)}, u32[]{:S(2)}, u32[]{:S(2)}) %collective-permute-start.16) | collective-permute-done | bytes 524320 | tf_op jit(solution)/shard_map/ppermute | solution.py:554
  159.7 12.5 %shard_map.226.a_ref.b_ref = bf16[1024,512]{1,0:T(8,128)(2,1)S(1)} custom-call(f32[1024,1024]{1,0:T(8,128)} %shard_map.224.qkv_ref, f32[2,128]{1,0:T(2,128)S(1)} %convert_element_type.208.gain_ref, f32[1024,128]{1,0:T(8,128)S(1)} %get-tuple-element.525.cos_ref, f32[1024,128]{1,0:T(8,128)S(1)} %get-tuple-element.526.sin_ref, ...), custom_call_target="tpu_custom_call" | custom-call | flops 1048576 | bytes 65536 | tf_op jit(solution)/shard_map/pallas_call | solution.py:477
  201.8 18.7 %collective-permute-done.23 = bf16[128,2048]{1,0:T(8,128)(2,1)S(1)} collective-permute-done((bf16[128,2048]{1,0:T(8,128)(2,1)S(1)}, bf16[128,2048]{1,0:T(8,128)(2,1)S(1)}, u32[]{:S(2)}, u32[]{:S(2)}) %collective-permute-start.23) | collective-permute-done | bytes 524320 | tf_op jit(solution)/shard_map/ppermute | solution.py:554
  227.0 17.0 %collective-permute-done.24 = bf16[128,2048]{1,0:T(8,128)(2,1)S(1)} collective-permute-done((bf16[128,2048]{1,0:T(8,128)(2,1)S(1)}, bf16[128,2048]{1,0:T(8,128)(2,1)S(1)}, u32[]{:S(2)}, u32[]{:S(2)}) %collective-permute-start.24) | collective-permute-done | bytes 524320 | tf_op jit(solution)/shard_map/ppermute | solution.py:554
  260.9 15.6 %collective-permute-done.28 = bf16[256,2048]{1,0:T(8,128)(2,1)S(1)} collective-permute-done((bf16[256,2048]{1,0:T(8,128)(2,1)S(1)}, bf16[256,2048]{1,0:T(8,128)(2,1)S(1)}, u32[]{:S(2)}, u32[]{:S(2)}) %collective-permute-start.28) | collective-permute-done | bytes 1048608 | tf_op jit(solution)/shard_map/ppermute | solution.py:554
  276.5 22.0 %collective-permute-done.29 = bf16[256,2048]{1,0:T(8,128)(2,1)S(1)} collective-permute-done((bf16[256,2048]{1,0:T(8,128)(2,1)S(1)}, bf16[256,2048]{1,0:T(8,128)(2,1)S(1)}, u32[]{:S(2)}, u32[]{:S(2)}) %collective-permute-start.29) | collective-permute-done | bytes 1048608 | tf_op jit(solution)/shard_map/ppermute | solution.py:554
  300.9 18.8 %shard_map.231.pre_ref = f32[1024,3072]{1,0:T(8,128)} custom-call(bf16[1024,2048]{1,0:T(8,128)(2,1)} %pad_maximum_fusion.a_ref, bf16[8,4,64,3072]{3,2,1,0:T(8,128)(2,1)} %bitcast.243), custom_call_target="tpu_custom_call" | custom-call | flops 1048576 | bytes 65536 | tf_op jit(solution)/shard_map/pallas_call | solution.py:142
  319.7 16.3 %shard_map.232 = (bf16[1024,1536]{1,0:T(8,128)(2,1)}, bf16[1024,3072]{1,0:T(8,128)(2,1)}) custom-call(f32[1024,3072]{1,0:T(8,128)} %shard_map.231.pre_ref, bf16[1024,2048]{1,0:T(8,128)(2,1)} %constant_dynamic-update-slice_fusion.20.grad_ref.a_ref, bf16[8,4,64,1536]{3,2,1,0:T(8,128)(2,1)} %bitcast.247), custom_call_target="tpu_custom_call" | custom-call | flops 1048576 | bytes 65536 | tf_op jit(solution)/shard_map/pallas_call | solution.py:528
  336.0 10.8 %shard_map.233 = bf16[8,4,64,1536]{3,2,1,0:T(8,128)(2,1)} custom-call(bf16[1024,2048]{1,0:T(8,128)(2,1)} %constant_dynamic-update-slice_fusion.20.grad_ref.a_ref, bf16[1024,1536]{1,0:T(8,128)(2,1)} %get-tuple-element.293.b_ref.a_ref), custom_call_target="tpu_custom_call" | custom-call | flops 1048576 | bytes 65536 | tf_op jit(solution)/shard_map/pallas_call | solution.py:190
  346.8 18.7 %shard_map.234 = (bf16[256,2048]{1,0:T(8,128)(2,1)}, bf16[256,2048]{1,0:T(8,128)(2,1)}, bf16[256,2048]{1,0:T(8,128)(2,1)}, bf16[256,2048]{1,0:T(8,128)(2,1)}) custom-call(bf16[1024,3072]{1,0:T(8,128)(2,1)} %get-tuple-element.300.a_ref.b_ref, bf16[8,4,64,3072]{3,2,1,0:T(8,128)(2,1)} %bitcast.244), custom_call_target="tpu_custom_call" | custom-call | flops 1048576 | bytes 65536 | tf_op jit(solution)/shard_map/pallas_call | solution.py:168
  369.0 10.6 %shard_map.236 = (bf16[256,2048]{1,0:T(8,128)(2,1)}, bf16[256,2048]{1,0:T(8,128)(2,1)}, bf16[256,2048]{1,0:T(8,128)(2,1)}, bf16[256,2048]{1,0:T(8,128)(2,1)}) custom-call(bf16[1024,1536]{1,0:T(8,128)(2,1)} %get-tuple-element.293.b_ref.a_ref, bf16[8,4,64,1536]{3,2,1,0:T(8,128)(2,1)} %bitcast.248), custom_call_target="tpu_custom_call" | custom-call | flops 1048576 | bytes 65536 | tf_op jit(solution)/shard_map/pallas_call | solution.py:168
  379.6 18.7 %shard_map.235 = bf16[8,4,64,3072]{3,2,1,0:T(8,128)(2,1)} custom-call(bf16[1024,2048]{1,0:T(8,128)(2,1)} %pad_maximum_fusion.a_ref, bf16[1024,3072]{1,0:T(8,128)(2,1)} %get-tuple-element.300.a_ref.b_ref), custom_call_target="tpu_custom_call" | custom-call | flops 1048576 | bytes 65536 | tf_op jit(solution)/shard_map/pallas_call | solution.py:190
  398.3 14.5 %collective-permute-done.32 = bf16[256,2048]{1,0:T(8,128)(2,1)} collective-permute-done((bf16[256,2048]{1,0:T(8,128)(2,1)}, bf16[256,2048]{1,0:T(8,128)(2,1)}, u32[]{:S(2)}, u32[]{:S(2)}) %collective-permute-start.32) | collective-permute-done | bytes 1048608 | tf_op jit(solution)/shard_map/ppermute | solution.py:554
  425.8 15.2 %collective-permute-done.34 = bf16[1,128,2048]{2,1,0:T(8,128)(2,1)S(1)} collective-permute-done((bf16[1,128,2048]{2,1,0:T(8,128)(2,1)S(1)}, bf16[1,128,2048]{2,1,0:T(8,128)(2,1)S(1)}, u32[]{:S(2)}, u32[]{:S(2)}) %collective-permute-start.34) | collective-permute-done | bytes 524320 | tf_op jit(solution)/shard_map/ppermute | solution.py:554
  445.7 13.1 %collective-permute-done.37 = bf16[1,128,2048]{2,1,0:T(8,128)(2,1)S(1)} collective-permute-done((bf16[1,128,2048]{2,1,0:T(8,128)(2,1)S(1)}, bf16[1,128,2048]{2,1,0:T(8,128)(2,1)S(1)}, u32[]{:S(2)}, u32[]{:S(2)}) %collective-permute-start.37) | collective-permute-done | bytes 524320 | tf_op jit(solution)/shard_map/ppermute | solution.py:554
  477.6 13.4 %collective-permute-done.41 = bf16[256,2048]{1,0:T(8,128)(2,1)} collective-permute-done((bf16[256,2048]{1,0:T(8,128)(2,1)}, bf16[256,2048]{1,0:T(8,128)(2,1)}, u32[]{:S(2)}, u32[]{:S(2)}) %collective-permute-start.41) | collective-permute-done | bytes 1048608 | tf_op jit(solution)/shard_map/ppermute | solution.py:554
  495.7 18.7 %shard_map.239 = (bf16[1024,1024]{1,0:T(8,128)(2,1)S(1)}, f32[2,8,128]{2,1,0:T(8,128)S(1)}) custom-call(f32[1024,1024]{1,0:T(8,128)} %shard_map.224.qkv_ref, bf16[1024,512]{1,0:T(8,128)(2,1)S(1)} %copy-done.4, f32[2,128]{1,0:T(2,128)S(1)} %convert_element_type.208.gain_ref, f32[1024,128]{1,0:T(8,128)S(1)} %get-tuple-element.525.cos_ref, ...), custom_call_target="tpu_custom_call" | custom-call | flops 1048576 | bytes 65536 | tf_op jit(solution)/shard_map/pallas_call | solution.py:491
  529.6 10.4 %shard_map.241 = (bf16[512,1152]{1,0:T(8,128)(2,1)}, bf16[512,1152]{1,0:T(8,128)(2,1)}, bf16[512,1152]{1,0:T(8,128)(2,1)}, bf16[512,1152]{1,0:T(8,128)(2,1)}) custom-call(s32[1]{0:T(128)} %bitcast.me_ref, bf16[1024,2048]{1,0:T(8,128)(2,1)} %slice_dynamic-update-slice_fusion.a_ref.normed_ref, bf16[1024,1024]{1,0:T(8,128)(2,1)} %copy-done.2, f32[8,2048]{1,0:T(8,128)} %copy-done.40), custom_call_target="tpu_custom_call" | custom-call | flops 1048576 | bytes 65536 | tf_op jit(solution)/shard_map/pallas_call | solution.py:230
  556.5 10.3 %collective-permute-done.55 = bf16[256,512]{1,0:T(8,128)(2,1)S(1)} collective-permute-done((bf16[256,512]{1,0:T(8,128)(2,1)S(1)}, bf16[256,512]{1,0:T(8,128)(2,1)S(1)}, u32[]{:S(2)}, u32[]{:S(2)}) %collective-permute-start.55) | collective-permute-done | bytes 262176 | tf_op jit(solution)/shard_map/ppermute | solution.py:554
  574.1 24.4 %collective-permute-done.51 = bf16[512,1152]{1,0:T(8,128)(2,1)S(1)} collective-permute-done((bf16[512,1152]{1,0:T(8,128)(2,1)S(1)}, bf16[512,1152]{1,0:T(8,128)(2,1)S(1)}, u32[]{:S(2)}, u32[]{:S(2)}) %collective-permute-start.51) | collective-permute-done | bytes 1179680 | tf_op jit(solution)/shard_map/ppermute | solution.py:554
  610.2 21.5 %collective-permute-done.58 = f32[2,128]{1,0:T(2,128)S(1)} collective-permute-done((f32[2,128]{1,0:T(2,128)S(1)}, f32[2,128]{1,0:T(2,128)S(1)}, u32[]{:S(2)}, u32[]{:S(2)}) %collective-permute-start.58) | collective-permute-done | bytes 1056 | tf_op jit(solution)/shard_map/ppermute | solution.py:554
  631.7 13.4 %collective-permute-done.57 = bf16[256,1152]{1,0:T(8,128)(2,1)S(1)} collective-permute-done((bf16[256,1152]{1,0:T(8,128)(2,1)S(1)}, bf16[256,1152]{1,0:T(8,128)(2,1)S(1)}, u32[]{:S(2)}, u32[]{:S(2)}) %collective-permute-start.57) | collective-permute-done | bytes 589856 | tf_op jit(solution)/shard_map/ppermute | solution.py:554
  (444 shorter events, 287.8 us)
Async XLA Ops:
  7.2 239.8 %all-gather.5.cloned.1.call-start = ((), (), s32[]{:S(2)}) async-start(), calls=%async_computation.4 | async-start | bytes 14155776 | tf_op jit(solution)/shard_map/all_gather | solution.py:793
  49.4 43.3 %collective-permute-start.6 = (bf16[2,128,2176]{2,1,0:T(8,128)(2,1)S(1)}, bf16[2,128,2176]{2,1,0:T(8,128)(2,1)S(1)}, u32[]{:S(2)}, u32[]{:S(2)}) collective-permute-start(bf16[2,128,2176]{2,1,0:T(8,128)(2,1)S(1)} %constant_dynamic-update-slice_fusion.16), channel_id=1, source_target_pairs={{0,2},{1,3},{2,0},{3,1},{4,6},{5,7},{6,4},{7,5},{8,10},{9,11},{10,... | collective-permute-start | bytes 3342344 | tf_op jit(solution)/shard_map/ppermute | solution.py:554
  55.7 35.3 %collective-permute-start.7 = (bf16[256,1024]{1,0:T(8,128)(2,1)S(1)}, bf16[256,1024]{1,0:T(8,128)(2,1)S(1)}, u32[]{:S(2)}, u32[]{:S(2)}) collective-permute-start(bf16[256,1024]{1,0:T(8,128)(2,1)S(1)} %get-tuple-element.270.refs_0_), channel_id=1, source_target_pairs={{0,4},{4,0},{1,5},{5,1},{2,6},{6,2},{3,7},{7,3},{8,12},{12,8},{9,1... | collective-permute-start | bytes 1572872 | tf_op jit(solution)/shard_map/ppermute | solution.py:554
  96.0 223.7 %all-gather.7.cloned.1.call-start = ((), (), s32[]{:S(2)}) async-start(), calls=%async_computation.5 | async-start | bytes 7077888 | tf_op jit(solution)/shard_map/all_gather | solution.py:793
  134.3 37.9 %collective-permute-start.20 = (bf16[512,512]{1,0:T(8,128)(2,1)S(1)}, bf16[512,512]{1,0:T(8,128)(2,1)S(1)}, u32[]{:S(2)}, u32[]{:S(2)}) collective-permute-start(bf16[512,512]{1,0:T(8,128)(2,1)S(1)} %constant_dynamic-update-slice_fusion.18), channel_id=1, source_target_pairs={{0,24},{8,16},{16,8},{24,0},{1,25},{9,17},{17,9},{25,1},{2,26},{10... | collective-permute-start | bytes 1572872 | tf_op jit(solution)/shard_map/ppermute | solution.py:554
  182.8 64.2 %collective-permute-start.26 = (bf16[256,2048]{1,0:T(8,128)(2,1)}, bf16[256,2048]{1,0:T(8,128)(2,1)}, u32[]{:S(2)}, u32[]{:S(2)}) collective-permute-start(bf16[256,2048]{1,0:T(8,128)(2,1)} %bitcast.252), channel_id=1, source_target_pairs={{0,16},{8,24},{16,0},{24,8},{1,17},{9,25},{17,1},{25,9},{2,18},{10... | collective-permute-start | bytes 3145736 | tf_op jit(solution)/shard_map/ppermute | solution.py:554
  184.4 62.6 %collective-permute-start.27 = (bf16[256,2048]{1,0:T(8,128)(2,1)}, bf16[256,2048]{1,0:T(8,128)(2,1)}, u32[]{:S(2)}, u32[]{:S(2)}) collective-permute-start(bf16[256,2048]{1,0:T(8,128)(2,1)} %bitcast.253), channel_id=1, source_target_pairs={{0,24},{8,16},{16,8},{24,0},{1,25},{9,17},{17,9},{25,1},{2,26},{10... | collective-permute-start | bytes 3145736 | tf_op jit(solution)/shard_map/ppermute | solution.py:554
  247.0 277.4 %reduce-scatter.3.cloned.1.call-start = ((), (), s32[]{:S(2)}) async-start(), calls=%async_computation.2 | async-start | bytes 7077888 | tf_op jit(solution)/shard_map/reduce_scatter | solution.py:798
  251.9 46.7 %collective-permute-start.29 = (bf16[256,2048]{1,0:T(8,128)(2,1)S(1)}, bf16[256,2048]{1,0:T(8,128)(2,1)S(1)}, u32[]{:S(2)}, u32[]{:S(2)}) collective-permute-start(bf16[256,2048]{1,0:T(8,128)(2,1)S(1)} %fusion.13), channel_id=1, source_target_pairs={{0,16},{8,24},{16,0},{24,8},{1,17},{9,25},{17,1},{25,9},{2,18},{10... | collective-permute-start | bytes 3145736 | tf_op jit(solution)/shard_map/ppermute | solution.py:554
  253.4 45.2 %collective-permute-start.30 = (bf16[256,2048]{1,0:T(8,128)(2,1)S(1)}, bf16[256,2048]{1,0:T(8,128)(2,1)S(1)}, u32[]{:S(2)}, u32[]{:S(2)}) collective-permute-start(bf16[256,2048]{1,0:T(8,128)(2,1)S(1)} %fusion.13), channel_id=1, source_target_pairs={{0,24},{8,16},{16,8},{24,0},{1,25},{9,17},{17,9},{25,1},{2,26},{10... | collective-permute-start | bytes 3145736 | tf_op jit(solution)/shard_map/ppermute | solution.py:554
  346.8 298.6 %reduce-scatter.5.cloned.1.call-start = ((), (), s32[]{:S(2)}) async-start(), calls=%async_computation.3 | async-start | bytes 14155776 | tf_op jit(solution)/shard_map/reduce_scatter | solution.py:798
  366.7 46.2 %collective-permute-start.32 = (bf16[256,2048]{1,0:T(8,128)(2,1)}, bf16[256,2048]{1,0:T(8,128)(2,1)}, u32[]{:S(2)}, u32[]{:S(2)}) collective-permute-start(bf16[256,2048]{1,0:T(8,128)(2,1)} %get-tuple-element.307), channel_id=1, source_target_pairs={{0,16},{8,24},{16,0},{24,8},{1,17},{9,25},{17,1},{25,9},{2,18},{10... | collective-permute-start | bytes 3145736 | tf_op jit(solution)/shard_map/ppermute | solution.py:554
  367.6 45.3 %collective-permute-start.33 = (bf16[256,2048]{1,0:T(8,128)(2,1)}, bf16[256,2048]{1,0:T(8,128)(2,1)}, u32[]{:S(2)}, u32[]{:S(2)}) collective-permute-start(bf16[256,2048]{1,0:T(8,128)(2,1)} %get-tuple-element.308), channel_id=1, source_target_pairs={{0,24},{8,16},{16,8},{24,0},{1,25},{9,17},{17,9},{25,1},{2,26},{10... | collective-permute-start | bytes 3145736 | tf_op jit(solution)/shard_map/ppermute | solution.py:554
  423.7 35.1 %collective-permute-start.38 = (bf16[256,2048]{1,0:T(8,128)(2,1)S(1)}, bf16[256,2048]{1,0:T(8,128)(2,1)S(1)}, u32[]{:S(2)}, u32[]{:S(2)}) collective-permute-start(bf16[256,2048]{1,0:T(8,128)(2,1)S(1)} %copy-done.79), channel_id=1, source_target_pairs={{0,8},{8,0},{16,24},{24,16},{1,9},{9,1},{17,25},{25,17},{2,10},{10... | collective-permute-start | bytes 3145736 | tf_op jit(solution)/shard_map/ppermute | solution.py:554
  424.3 34.5 %collective-permute-start.39 = (bf16[256,2048]{1,0:T(8,128)(2,1)S(1)}, bf16[256,2048]{1,0:T(8,128)(2,1)S(1)}, u32[]{:S(2)}, u32[]{:S(2)}) collective-permute-start(bf16[256,2048]{1,0:T(8,128)(2,1)S(1)} %copy-done.78), channel_id=1, source_target_pairs={{0,16},{8,24},{16,0},{24,8},{1,17},{9,25},{17,1},{25,9},{2,18},{10... | collective-permute-start | bytes 3145736 | tf_op jit(solution)/shard_map/ppermute | solution.py:554
  491.0 34.8 %collective-permute-start.42 = (bf16[512,512]{1,0:T(8,128)(2,1)}, bf16[512,512]{1,0:T(8,128)(2,1)}, u32[]{:S(2)}, u32[]{:S(2)}) collective-permute-start(bf16[512,512]{1,0:T(8,128)(2,1)} %get-tuple-element.334), channel_id=1, source_target_pairs={{0,8},{8,0},{16,24},{24,16},{1,9},{9,1},{17,25},{25,17},{2,10},{10... | collective-permute-start | bytes 1572872 | tf_op jit(solution)/shard_map/ppermute | solution.py:554
  491.2 34.6 %collective-permute-start.43 = (bf16[512,512]{1,0:T(8,128)(2,1)}, bf16[512,512]{1,0:T(8,128)(2,1)}, u32[]{:S(2)}, u32[]{:S(2)}) collective-permute-start(bf16[512,512]{1,0:T(8,128)(2,1)} %get-tuple-element.335), channel_id=1, source_target_pairs={{0,16},{8,24},{16,0},{24,8},{1,17},{9,25},{17,1},{25,9},{2,18},{10... | collective-permute-start | bytes 1572872 | tf_op jit(solution)/shard_map/ppermute | solution.py:554
  491.9 33.9 %collective-permute-start.44 = (bf16[512,512]{1,0:T(8,128)(2,1)}, bf16[512,512]{1,0:T(8,128)(2,1)}, u32[]{:S(2)}, u32[]{:S(2)}) collective-permute-start(bf16[512,512]{1,0:T(8,128)(2,1)} %get-tuple-element.336), channel_id=1, source_target_pairs={{0,24},{8,16},{16,8},{24,0},{1,25},{9,17},{17,9},{25,1},{2,26},{10... | collective-permute-start | bytes 1572872 | tf_op jit(solution)/shard_map/ppermute | solution.py:554
  546.1 52.4 %collective-permute-start.51 = (bf16[512,1152]{1,0:T(8,128)(2,1)S(1)}, bf16[512,1152]{1,0:T(8,128)(2,1)S(1)}, u32[]{:S(2)}, u32[]{:S(2)}) collective-permute-start(bf16[512,1152]{1,0:T(8,128)(2,1)S(1)} %copy-done.76), channel_id=1, source_target_pairs={{0,16},{8,24},{16,0},{24,8},{1,17},{9,25},{17,1},{25,9},{2,18},{10... | collective-permute-start | bytes 3538952 | tf_op jit(solution)/shard_map/ppermute | solution.py:554
  549.1 50.2 %collective-permute-start.52 = (bf16[512,1152]{1,0:T(8,128)(2,1)S(1)}, bf16[512,1152]{1,0:T(8,128)(2,1)S(1)}, u32[]{:S(2)}, u32[]{:S(2)}) collective-permute-start(bf16[512,1152]{1,0:T(8,128)(2,1)S(1)} %copy-done.75), channel_id=1, source_target_pairs={{0,24},{8,16},{16,8},{24,0},{1,25},{9,17},{17,9},{25,1},{2,26},{10... | collective-permute-start | bytes 3538952 | tf_op jit(solution)/shard_map/ppermute | solution.py:554
  553.1 46.2 %collective-permute-start.54 = (bf16[128,2048]{1,0:T(8,128)(2,1)S(1)}, bf16[128,2048]{1,0:T(8,128)(2,1)S(1)}, u32[]{:S(2)}, u32[]{:S(2)}) collective-permute-start(bf16[128,2048]{1,0:T(8,128)(2,1)S(1)} %get-tuple-element.499), channel_id=1, source_target_pairs={{0,2},{1,3},{2,0},{3,1},{4,6},{5,7},{6,4},{7,5},{8,10},{9,11},{10,... | collective-permute-start | bytes 1572872 | tf_op jit(solution)/shard_map/ppermute | solution.py:554
  604.2 40.9 %collective-permute-start.57 = (bf16[256,1152]{1,0:T(8,128)(2,1)S(1)}, bf16[256,1152]{1,0:T(8,128)(2,1)S(1)}, u32[]{:S(2)}, u32[]{:S(2)}) collective-permute-start(bf16[256,1152]{1,0:T(8,128)(2,1)S(1)} %fusion.17), channel_id=1, source_target_pairs={{0,4},{4,0},{1,5},{5,1},{2,6},{6,2},{3,7},{7,3},{8,12},{12,8},{9,1... | collective-permute-start | bytes 1769480 | tf_op jit(solution)/shard_map/ppermute | solution.py:554
  607.5 42.3 %collective-permute-start.67 = (bf16[128,2048]{1,0:T(8,128)(2,1)}, bf16[128,2048]{1,0:T(8,128)(2,1)}, u32[]{:S(2)}, u32[]{:S(2)}) collective-permute-start(bf16[128,2048]{1,0:T(8,128)(2,1)} %get-tuple-element.381), channel_id=1, source_target_pairs={{0,2},{1,3},{2,0},{3,1},{4,6},{5,7},{6,4},{7,5},{8,10},{9,11},{10,... | collective-permute-start | bytes 1572872 | tf_op jit(solution)/shard_map/ppermute | solution.py:554
  609.5 45.8 %collective-permute-start.62 = (bf16[128,2048]{1,0:T(8,128)(2,1)}, bf16[128,2048]{1,0:T(8,128)(2,1)}, u32[]{:S(2)}, u32[]{:S(2)}) collective-permute-start(bf16[128,2048]{1,0:T(8,128)(2,1)} %fusion.15), channel_id=1, source_target_pairs={{0,4},{4,0},{1,5},{5,1},{2,6},{6,2},{3,7},{7,3},{8,12},{12,8},{9,1... | collective-permute-start | bytes 1572872 | tf_op jit(solution)/shard_map/ppermute | solution.py:554
  (131 other events, 2007.6 us)
Sparse Core Ops, SparseCore 0:
  96.2 118.5 all-gather.4
  247.2 67.3 all-gather.6
  346.9 70.6 reduce-scatter.2
  464.4 144.1 reduce-scatter.4

commit v5 on v4

--- a/solution.py
+++ b/solution.py
@@ -629,13 +629,14 @@
         bit *= 2
     first = swap(pick(held[bit], 1 - half).astype(BF16), "t", bit)
     if on_first is not None:
-        on_first(first)
+        first = on_first(first)
     far = pick(held[0], 1 - half).astype(F32) + first.astype(F32)
     far, near = tie(far.astype(BF16), pick(held[bit], half).astype(BF16))
     got = swap(far, "h", 1)
+    second = swap(near, "t", bit)
     if on_last is not None:
-        got = on_last(got)
-    own = pick(held[0], half).astype(F32) + swap(near, "t", bit).astype(F32)
+        got, second = on_last(got, second)
+    own = pick(held[0], half).astype(F32) + second.astype(F32)
     got, own, late = tie(got.astype(F32), own, list(late))
     return jnp.where(half == 0, jnp.stack([own, got]), jnp.stack([got, own])), late
 
@@ -807,8 +808,8 @@
     earliest = jnp.broadcast_to((jnp.arange(length, dtype=jnp.int32) - places)[None, :], (8, length))
     out_pair = jnp.concatenate([out_rows, hold["out_h"]], axis=0)
     qkv = blocks_product(normed_one, qkv_blocks, block_at, 256)
+    qkv, qkv_blocks, out_near, out_grad = tie(qkv, qkv_blocks, swap_dp(out_pair, near), out_grad)
     grad_own = jnp.transpose(out_grad, (1, 0, 2)).reshape(rows, width)
-    qkv, qkv_blocks, out_near, grad_own = tie(qkv, qkv_blocks, swap_dp(out_pair, near), grad_own)
     mixed = attention_forward(qkv, gains, cos, sin, earliest)
     mixed, out_far = tie(mixed, swap_dp(out_pair, far))
     out_pairs = [out_pair, *out_near, *out_far]
@@ -817,10 +818,20 @@
     mixed_part, out_blocks, qkv_blocks, early = tie(
         mixed_part, out_blocks, qkv_blocks, swap_dp(grad_own, range(1, 2))
     )
-    qkv_weight, out_weight = place_rows(qkv_blocks, block_at), place_rows(out_blocks, block_at)
-    mixed_sum, (late, pre_weight, down_rows, qkv_weight, out_weight) = to_blocks(
-        mixed_part, [swap_dp(grad_own, range(2, dp)), pre_weight, down_rows, qkv_weight, out_weight]
-    )
+    def weights_step(first):
+        first, qkv_parts, out_parts = tie(first, qkv_blocks, out_blocks)
+        hold["qkv_weight"] = place_rows(qkv_parts, block_at)
+        hold["out_weight"] = place_rows(out_parts, block_at)
+        return first
+
+    def weights_done(got, second):
+        got, hold["qkv_weight"], hold["out_weight"] = tie(got, hold["qkv_weight"], hold["out_weight"])
+        return got, second
+
+    mixed_sum, (late, pre_weight, down_rows) = to_blocks(
+        mixed_part, [swap_dp(grad_own, range(2, dp)), pre_weight, down_rows], weights_step, weights_done
+    )
+    qkv_weight, out_weight = hold["qkv_weight"], hold["out_weight"]
     middle = (inputs + mixed_sum).reshape(rows, width)
     down_weight = ffn_gather(down_rows)
 
@@ -867,8 +878,9 @@
     pre_sum = ffn_scatter(pre_term)
     grad_mixed = rows_product(grad_mid, out_weight, 0, 256, BF16)
     out_pieces = term_pieces(grad_mid, mixed, dp_index, dp)
-    grad_mixed, out_pieces, hold["branch_far"] = tie(grad_mixed, out_pieces, swap_dp(branch_part, far))
+    grad_mixed, out_pieces = tie(grad_mixed, out_pieces)
     grad_qkv, gain_terms = attention_backward(qkv, grad_mixed, gains, cos, sin, earliest)
+    grad_qkv, hold["branch_far"] = tie(grad_qkv, swap_dp(branch_part, far))
     hops = [
         (axis, 1 << k) for axis in ("dp", "t", "h") for k in range(lax.axis_size(axis).bit_length() - 1)
     ]
@@ -893,27 +905,30 @@
     seen = []
 
     def gradients_step(first):
+        arrived = first
         got, first, out_h, head, hold["branch"] = tie(qkv_got, first, swap_h(out_give), hop(), branch_got)
         hold["head"] += head
         seen.append(first)
         hold["out_h_got"] = out_h
         hold["qkv_keep"], hold["qkv_give"] = sum_h(got)
-
-    def last_swap_step(got):
-        qkv_h_got, head = tie(swap_h(hold["qkv_give"]), hop())
+        return arrived
+
+    def last_swap_step(got, second):
+        got, head, second, pre_give = tie(got, hop(), second, to_dp(pre_sum))
+        qkv_h_got, pre_near = tie(swap_h(hold["qkv_give"]), swap_dp(pre_give, near))
         hold["head"] += head
         attn_sum = hold["qkv_keep"] + qkv_h_got.astype(F32)
         out_sum = out_keep + hold["out_h_got"].astype(F32)
-        attn_sum, pre_give = tie(jnp.concatenate([attn_sum, out_sum], axis=1).astype(BF16), to_dp(pre_sum))
+        attn_sum = jnp.concatenate([attn_sum, out_sum], axis=1).astype(BF16)
         attn_got = swaps(
             [lax.dynamic_slice_in_dim(attn_sum, (part ^ k) * depth, depth, 0) for k in range(parts)], "t"
         )
         while len(hops) > 1:
             hold["head"] += hop()
-        hold["pre_got"] = swaps(pre_give)
+        hold["pre_got"] = [pre_give[0], *pre_near, *swap_dp(pre_give, far)]
         got, hold["attn_got"], head = tie(got, attn_got, hop())
         hold["head"] += head
-        return got
+        return got, second
 
     grad_one, _ = to_blocks(grad_one_part, [], gradients_step, last_swap_step)
     attn_grad, pre_grad = hold["attn_got"], hold["pre_got"]

time: 693 us -> 691 us (level)
  local copies, waits for them, and re-layouts: 60.6 us -> 49.5 us
    ppermute x68, waiting for transfers between devices: 313 us -> 284 us  [swap(): lax.ppermute(x, axis, [(i, i ^ bit) for i in range(lax.axis_size(axis))])]
    reduce_scatter x2, waiting for transfers between devices: 0.02 us -> 27.2 us  [ffn_scatter(): lax.psum_scatter(term, ('h', 't'), scatter_dimension=0, tiled=True)]
    dynamic_update_slice x16, local copies, waits for them, and re-layouts: 10.8 us -> 0.52 us  [place_rows(): out = lax.dynamic_update_slice_in_dim(out, part, places[k] * rows, 0)]
    unnamed x172 -> x191, local copies, waits for them, and re-layouts: 17.3 us -> 18.2 us
  transfers between devices with their start and end apart: 72 -> 72, of which waited for: 32 -> 28; matrix products, arithmetic and copies ran while one was open for 12% -> 11% of each run, Pallas kernels for 21% -> 21%
where the time goes in v5:
time: 691 us; the launch traced here: 686 us
  waiting for transfers between devices  311 us (45%)
  Pallas kernels  176 us (25%)
  starting transfers between devices  82.8 us (12%)
  other arithmetic  51.2 us (7%)
  local copies, waits for them, and re-layouts  49.5 us (7%)
  between operations  15.8 us (2%)
    ppermute x68, waiting for transfers between devices, swap(): lax.ppermute(x, axis, [(i, i ^ bit) for i in range(lax.axis_size(axis))])  284 us
    ppermute x68, starting transfers between devices, swap(): lax.ppermute(x, axis, [(i, i ^ bit) for i in range(lax.axis_size(axis))])  82.7 us
    pallas_call x2, Pallas kernels, term_product(): pl.pallas_call(term_kernel, grid=(groups,), in_specs=[pl.BlockSpec((rows,...  29.4 us
    pallas_call x2, Pallas kernels, stacked_back(): pl.pallas_call(stacked_back_kernel, grid=(groups,), in_specs=[pl.BlockSpe...  29.4 us
    reduce_scatter x2, waiting for transfers between devices, ffn_scatter(): lax.psum_scatter(term, ('h', 't'), scatter_dimension=0, tiled=True)  27.2 us
    dynamic_update_slice x24, local copies, waits for them, and re-layouts, assemble(): out = lax.dynamic_update_slice_in_dim(out, part[:, columns], start, 0)  19.1 us
    pallas_call x1, Pallas kernels, attention_backward(): pl.pallas_call(functools.partial(backward_kernel, 256), grid=(heads,), in...  19 us
    pallas_call x1, Pallas kernels, stacked_product(): pl.pallas_call(stacked_kernel, grid=(columns // tile,), in_specs=[pl.Bloc...  18.7 us
  transfers between devices with their start and end apart: 72, of which 28 were waited for; matrix products, arithmetic and copies ran while one was open for 11% of the time, Pallas kernels for 21%

profile of v5, /device:TPU:0, one launch (start us, length us, event | category | flops | bytes accessed | tf_op | source)
XLA Modules:
  0.0 686.0 jit_solution(15560854048755491596)
XLA Ops:
  27.5 14.5 %collective-permute-done.2.refs_2_ = bf16[64,1536]{1,0:T(8,128)(2,1)S(1)} collective-permute-done((bf16[64,1536]{1,0:T(8,128)(2,1)S(1)}, bf16[64,1536]{1,0:T(8,128)(2,1)S(1)}, u32[]{:S(2)}, u32[]{:S(2)}) %collective-permute-start.2) | collective-permute-done | bytes 196640 | tf_op jit(solution)/shard_map/ppermute | solution.py:554
  57.2 23.5 %collective-permute-done.12.refs_4_ = bf16[256,512]{1,0:T(8,128)(2,1)S(1)} collective-permute-done((bf16[256,512]{1,0:T(8,128)(2,1)S(1)}, bf16[256,512]{1,0:T(8,128)(2,1)S(1)}, u32[]{:S(2)}, u32[]{:S(2)}) %collective-permute-start.12) | collective-permute-done | bytes 262176 | tf_op jit(solution)/shard_map/ppermute | solution.py:554
  118.2 11.1 %collective-permute-done.16.refs_6_ = bf16[256,1024]{1,0:T(8,128)(2,1)S(1)} collective-permute-done((bf16[256,1024]{1,0:T(8,128)(2,1)S(1)}, bf16[256,1024]{1,0:T(8,128)(2,1)S(1)}, u32[]{:S(2)}, u32[]{:S(2)}) %collective-permute-start.16) | collective-permute-done | bytes 524320 | tf_op jit(solution)/shard_map/ppermute | solution.py:554
  146.4 10.1 %collective-permute-done.19 = bf16[512,512]{1,0:T(8,128)(2,1)S(1)} collective-permute-done((bf16[512,512]{1,0:T(8,128)(2,1)S(1)}, bf16[512,512]{1,0:T(8,128)(2,1)S(1)}, u32[]{:S(2)}, u32[]{:S(2)}) %collective-permute-start.19) | collective-permute-done | bytes 524320 | tf_op jit(solution)/shard_map/ppermute | solution.py:554
  160.5 12.6 %shard_map.226.a_ref.b_ref = bf16[1024,512]{1,0:T(8,128)(2,1)S(1)} custom-call(f32[1024,1024]{1,0:T(8,128)} %shard_map.224.qkv_ref, f32[2,128]{1,0:T(2,128)S(1)} %convert_element_type.208.gain_ref, f32[1024,128]{1,0:T(8,128)S(1)} %get-tuple-element.569.cos_ref, f32[1024,128]{1,0:T(8,128)S(1)} %get-tuple-element.570.sin_ref, ...), custom_call_target="tpu_custom_call" | custom-call | flops 1048576 | bytes 65536 | tf_op jit(solution)/shard_map/pallas_call | solution.py:477
  194.5 26.1 %collective-permute-done.23 = bf16[128,2048]{1,0:T(8,128)(2,1)S(1)} collective-permute-done((bf16[128,2048]{1,0:T(8,128)(2,1)S(1)}, bf16[128,2048]{1,0:T(8,128)(2,1)S(1)}, u32[]{:S(2)}, u32[]{:S(2)}) %collective-permute-start.23) | collective-permute-done | bytes 524320 | tf_op jit(solution)/shard_map/ppermute | solution.py:554
  226.5 20.5 %collective-permute-done.24 = bf16[128,2048]{1,0:T(8,128)(2,1)S(1)} collective-permute-done((bf16[128,2048]{1,0:T(8,128)(2,1)S(1)}, bf16[128,2048]{1,0:T(8,128)(2,1)S(1)}, u32[]{:S(2)}, u32[]{:S(2)}) %collective-permute-start.24) | collective-permute-done | bytes 524320 | tf_op jit(solution)/shard_map/ppermute | solution.py:554
  262.1 18.9 %collective-permute-done.28 = bf16[256,2048]{1,0:T(8,128)(2,1)S(1)} collective-permute-done((bf16[256,2048]{1,0:T(8,128)(2,1)S(1)}, bf16[256,2048]{1,0:T(8,128)(2,1)S(1)}, u32[]{:S(2)}, u32[]{:S(2)}) %collective-permute-start.28) | collective-permute-done | bytes 1048608 | tf_op jit(solution)/shard_map/ppermute | solution.py:554
  281.0 19.3 %collective-permute-done.29 = bf16[256,2048]{1,0:T(8,128)(2,1)S(1)} collective-permute-done((bf16[256,2048]{1,0:T(8,128)(2,1)S(1)}, bf16[256,2048]{1,0:T(8,128)(2,1)S(1)}, u32[]{:S(2)}, u32[]{:S(2)}) %collective-permute-start.29) | collective-permute-done | bytes 1048608 | tf_op jit(solution)/shard_map/ppermute | solution.py:554
  302.6 18.7 %shard_map.231.pre_ref = f32[1024,3072]{1,0:T(8,128)} custom-call(bf16[1024,2048]{1,0:T(8,128)(2,1)} %pad_maximum_fusion.a_ref, bf16[8,4,64,3072]{3,2,1,0:T(8,128)(2,1)} %bitcast.245), custom_call_target="tpu_custom_call" | custom-call | flops 1048576 | bytes 65536 | tf_op jit(solution)/shard_map/pallas_call | solution.py:142
  321.2 16.2 %shard_map.232 = (bf16[1024,1536]{1,0:T(8,128)(2,1)}, bf16[1024,3072]{1,0:T(8,128)(2,1)}) custom-call(f32[1024,3072]{1,0:T(8,128)} %shard_map.231.pre_ref, bf16[1024,2048]{1,0:T(8,128)(2,1)} %pad_maximum_fusion.1.grad_ref.a_ref, bf16[8,4,64,1536]{3,2,1,0:T(8,128)(2,1)} %bitcast.249), custom_call_target="tpu_custom_call" | custom-call | flops 1048576 | bytes 65536 | tf_op jit(solution)/shard_map/pallas_call | solution.py:528
  337.5 10.7 %shard_map.233 = bf16[8,4,64,1536]{3,2,1,0:T(8,128)(2,1)} custom-call(bf16[1024,2048]{1,0:T(8,128)(2,1)} %pad_maximum_fusion.1.grad_ref.a_ref, bf16[1024,1536]{1,0:T(8,128)(2,1)} %get-tuple-element.333.b_ref.a_ref), custom_call_target="tpu_custom_call" | custom-call | flops 1048576 | bytes 65536 | tf_op jit(solution)/shard_map/pallas_call | solution.py:190
  348.3 18.7 %shard_map.234 = (bf16[256,2048]{1,0:T(8,128)(2,1)}, bf16[256,2048]{1,0:T(8,128)(2,1)}, bf16[256,2048]{1,0:T(8,128)(2,1)}, bf16[256,2048]{1,0:T(8,128)(2,1)}) custom-call(bf16[1024,3072]{1,0:T(8,128)(2,1)} %get-tuple-element.340.a_ref.b_ref, bf16[8,4,64,3072]{3,2,1,0:T(8,128)(2,1)} %bitcast.246), custom_call_target="tpu_custom_call" | custom-call | flops 1048576 | bytes 65536 | tf_op jit(solution)/shard_map/pallas_call | solution.py:168
  370.5 10.7 %shard_map.236 = (bf16[256,2048]{1,0:T(8,128)(2,1)}, bf16[256,2048]{1,0:T(8,128)(2,1)}, bf16[256,2048]{1,0:T(8,128)(2,1)}, bf16[256,2048]{1,0:T(8,128)(2,1)}) custom-call(bf16[1024,1536]{1,0:T(8,128)(2,1)} %get-tuple-element.333.b_ref.a_ref, bf16[8,4,64,1536]{3,2,1,0:T(8,128)(2,1)} %bitcast.250), custom_call_target="tpu_custom_call" | custom-call | flops 1048576 | bytes 65536 | tf_op jit(solution)/shard_map/pallas_call | solution.py:168
  381.2 18.7 %shard_map.235 = bf16[8,4,64,3072]{3,2,1,0:T(8,128)(2,1)} custom-call(bf16[1024,2048]{1,0:T(8,128)(2,1)} %pad_maximum_fusion.a_ref, bf16[1024,3072]{1,0:T(8,128)(2,1)} %get-tuple-element.340.a_ref.b_ref), custom_call_target="tpu_custom_call" | custom-call | flops 1048576 | bytes 65536 | tf_op jit(solution)/shard_map/pallas_call | solution.py:190
  399.9 12.2 %collective-permute-done.32 = bf16[256,2048]{1,0:T(8,128)(2,1)} collective-permute-done((bf16[256,2048]{1,0:T(8,128)(2,1)}, bf16[256,2048]{1,0:T(8,128)(2,1)}, u32[]{:S(2)}, u32[]{:S(2)}) %collective-permute-start.32) | collective-permute-done | bytes 1048608 | tf_op jit(solution)/shard_map/ppermute | solution.py:554
  429.7 14.1 %collective-permute-done.34 = bf16[1,128,2048]{2,1,0:T(8,128)(2,1)S(1)} collective-permute-done((bf16[1,128,2048]{2,1,0:T(8,128)(2,1)S(1)}, bf16[1,128,2048]{2,1,0:T(8,128)(2,1)S(1)}, u32[]{:S(2)}, u32[]{:S(2)}) %collective-permute-start.34) | collective-permute-done | bytes 524320 | tf_op jit(solution)/shard_map/ppermute | solution.py:554
  448.4 13.1 %collective-permute-done.37 = bf16[1,128,2048]{2,1,0:T(8,128)(2,1)S(1)} collective-permute-done((bf16[1,128,2048]{2,1,0:T(8,128)(2,1)S(1)}, bf16[1,128,2048]{2,1,0:T(8,128)(2,1)S(1)}, u32[]{:S(2)}, u32[]{:S(2)}) %collective-permute-start.37) | collective-permute-done | bytes 524320 | tf_op jit(solution)/shard_map/ppermute | solution.py:554
  488.0 19.0 %shard_map.239 = (bf16[1024,1024]{1,0:T(8,128)(2,1)S(1)}, f32[2,8,128]{2,1,0:T(8,128)S(1)}) custom-call(f32[1024,1024]{1,0:T(8,128)} %shard_map.224.qkv_ref, bf16[1024,512]{1,0:T(8,128)(2,1)S(1)} %copy-done.4, f32[2,128]{1,0:T(2,128)S(1)} %convert_element_type.208.gain_ref, f32[1024,128]{1,0:T(8,128)S(1)} %get-tuple-element.569.cos_ref, ...), custom_call_target="tpu_custom_call" | custom-call | flops 1048576 | bytes 65536 | tf_op jit(solution)/shard_map/pallas_call | solution.py:491
  522.0 10.4 %shard_map.241 = (bf16[512,1152]{1,0:T(8,128)(2,1)}, bf16[512,1152]{1,0:T(8,128)(2,1)}, bf16[512,1152]{1,0:T(8,128)(2,1)}, bf16[512,1152]{1,0:T(8,128)(2,1)}) custom-call(s32[1]{0:T(128)} %bitcast.me_ref, bf16[1024,2048]{1,0:T(8,128)(2,1)} %slice_dynamic-update-slice_fusion.a_ref.normed_ref, bf16[1024,1024]{1,0:T(8,128)(2,1)} %copy-done.2, f32[8,2048]{1,0:T(8,128)} %copy-done.44), custom_call_target="tpu_custom_call" | custom-call | flops 1048576 | bytes 65536 | tf_op jit(solution)/shard_map/pallas_call | solution.py:230
  546.8 12.2 %collective-permute-done.56 = bf16[256,512]{1,0:T(8,128)(2,1)S(1)} collective-permute-done((bf16[256,512]{1,0:T(8,128)(2,1)S(1)}, bf16[256,512]{1,0:T(8,128)(2,1)S(1)}, u32[]{:S(2)}, u32[]{:S(2)}) %collective-permute-start.56) | collective-permute-done | bytes 262176 | tf_op jit(solution)/shard_map/ppermute | solution.py:554
  566.4 25.5 %collective-permute-done.54 = bf16[512,1152]{1,0:T(8,128)(2,1)S(1)} collective-permute-done((bf16[512,1152]{1,0:T(8,128)(2,1)S(1)}, bf16[512,1152]{1,0:T(8,128)(2,1)S(1)}, u32[]{:S(2)}, u32[]{:S(2)}) %collective-permute-start.54) | collective-permute-done | bytes 1179680 | tf_op jit(solution)/shard_map/ppermute | solution.py:554
  600.7 27.2 %reduce-scatter.5.cloned.1.call-done = bf16[256,3072]{1,0:T(8,128)(2,1)} async-done(((bf16[2048,3072]{1,0:T(8,128)(2,1)}), bf16[256,3072]{1,0:T(8,128)(2,1)}) %reduce-scatter.5.cloned.1.call-update) | async-done | bytes 1572880 | tf_op jit(solution)/shard_map/reduce_scatter | solution.py:799
  629.5 10.1 %collective-permute-done.59 = bf16[128,2048]{1,0:T(8,128)(2,1)} collective-permute-done((bf16[128,2048]{1,0:T(8,128)(2,1)}, bf16[128,2048]{1,0:T(8,128)(2,1)}, u32[]{:S(2)}, u32[]{:S(2)}) %collective-permute-start.59) | collective-permute-done | bytes 524320 | tf_op jit(solution)/shard_map/ppermute | solution.py:554
  (462 shorter events, 275.9 us)
Async XLA Ops:
  7.2 243.0 %all-gather.5.cloned.1.call-start = ((), (), s32[]{:S(2)}) async-start(), calls=%async_computation.4 | async-start | bytes 14155776 | tf_op jit(solution)/shard_map/all_gather | solution.py:794
  49.5 43.3 %collective-permute-start.6 = (bf16[2,128,2176]{2,1,0:T(8,128)(2,1)S(1)}, bf16[2,128,2176]{2,1,0:T(8,128)(2,1)S(1)}, u32[]{:S(2)}, u32[]{:S(2)}) collective-permute-start(bf16[2,128,2176]{2,1,0:T(8,128)(2,1)S(1)} %constant_dynamic-update-slice_fusion.16), channel_id=1, source_target_pairs={{0,2},{1,3},{2,0},{3,1},{4,6},{5,7},{6,4},{7,5},{8,10},{9,11},{10,... | collective-permute-start | bytes 3342344 | tf_op jit(solution)/shard_map/ppermute | solution.py:554
  55.7 35.3 %collective-permute-start.7 = (bf16[256,1024]{1,0:T(8,128)(2,1)S(1)}, bf16[256,1024]{1,0:T(8,128)(2,1)S(1)}, u32[]{:S(2)}, u32[]{:S(2)}) collective-permute-start(bf16[256,1024]{1,0:T(8,128)(2,1)S(1)} %get-tuple-element.302.refs_0_), channel_id=1, source_target_pairs={{0,4},{4,0},{1,5},{5,1},{2,6},{6,2},{3,7},{7,3},{8,12},{12,8},{9,1... | collective-permute-start | bytes 1572872 | tf_op jit(solution)/shard_map/ppermute | solution.py:554
  96.1 225.1 %all-gather.7.cloned.1.call-start = ((), (), s32[]{:S(2)}) async-start(), calls=%async_computation.5 | async-start | bytes 7077888 | tf_op jit(solution)/shard_map/all_gather | solution.py:794
  133.5 39.6 %collective-permute-start.20 = (bf16[512,512]{1,0:T(8,128)(2,1)S(1)}, bf16[512,512]{1,0:T(8,128)(2,1)S(1)}, u32[]{:S(2)}, u32[]{:S(2)}) collective-permute-start(bf16[512,512]{1,0:T(8,128)(2,1)S(1)} %constant_dynamic-update-slice_fusion.18), channel_id=1, source_target_pairs={{0,24},{8,16},{16,8},{24,0},{1,25},{9,17},{17,9},{25,1},{2,26},{10... | collective-permute-start | bytes 1572872 | tf_op jit(solution)/shard_map/ppermute | solution.py:554
  182.2 66.9 %collective-permute-start.26 = (bf16[256,2048]{1,0:T(8,128)(2,1)}, bf16[256,2048]{1,0:T(8,128)(2,1)S(1)}, u32[]{:S(2)}, u32[]{:S(2)}) collective-permute-start(bf16[256,2048]{1,0:T(8,128)(2,1)} %bitcast.25), channel_id=1, source_target_pairs={{0,16},{8,24},{16,0},{24,8},{1,17},{9,25},{17,1},{25,9},{2,18},{10... | collective-permute-start | bytes 3145736 | tf_op jit(solution)/shard_map/ppermute | solution.py:554
  183.6 66.6 %collective-permute-start.27 = (bf16[256,2048]{1,0:T(8,128)(2,1)}, bf16[256,2048]{1,0:T(8,128)(2,1)}, u32[]{:S(2)}, u32[]{:S(2)}) collective-permute-start(bf16[256,2048]{1,0:T(8,128)(2,1)} %bitcast.25), channel_id=1, source_target_pairs={{0,24},{8,16},{16,8},{24,0},{1,25},{9,17},{17,9},{25,1},{2,26},{10... | collective-permute-start | bytes 3145736 | tf_op jit(solution)/shard_map/ppermute | solution.py:554
  250.2 266.9 %reduce-scatter.3.cloned.1.call-start = ((), (), s32[]{:S(2)}) async-start(), calls=%async_computation.2 | async-start | bytes 7077888 | tf_op jit(solution)/shard_map/reduce_scatter | solution.py:799
  256.3 44.0 %collective-permute-start.29 = (bf16[256,2048]{1,0:T(8,128)(2,1)S(1)}, bf16[256,2048]{1,0:T(8,128)(2,1)S(1)}, u32[]{:S(2)}, u32[]{:S(2)}) collective-permute-start(bf16[256,2048]{1,0:T(8,128)(2,1)S(1)} %fusion.13), channel_id=1, source_target_pairs={{0,16},{8,24},{16,0},{24,8},{1,17},{9,25},{17,1},{25,9},{2,18},{10... | collective-permute-start | bytes 3145736 | tf_op jit(solution)/shard_map/ppermute | solution.py:554
  257.8 42.5 %collective-permute-start.30 = (bf16[256,2048]{1,0:T(8,128)(2,1)S(1)}, bf16[256,2048]{1,0:T(8,128)(2,1)S(1)}, u32[]{:S(2)}, u32[]{:S(2)}) collective-permute-start(bf16[256,2048]{1,0:T(8,128)(2,1)S(1)} %fusion.13), channel_id=1, source_target_pairs={{0,24},{8,16},{16,8},{24,0},{1,25},{9,17},{17,9},{25,1},{2,26},{10... | collective-permute-start | bytes 3145736 | tf_op jit(solution)/shard_map/ppermute | solution.py:554
  348.2 279.7 %reduce-scatter.5.cloned.1.call-start = ((), (), s32[]{:S(2)}) async-start(), calls=%async_computation.3 | async-start | bytes 14155776 | tf_op jit(solution)/shard_map/reduce_scatter | solution.py:799
  368.4 43.7 %collective-permute-start.32 = (bf16[256,2048]{1,0:T(8,128)(2,1)}, bf16[256,2048]{1,0:T(8,128)(2,1)}, u32[]{:S(2)}, u32[]{:S(2)}) collective-permute-start(bf16[256,2048]{1,0:T(8,128)(2,1)} %get-tuple-element.347), channel_id=1, source_target_pairs={{0,16},{8,24},{16,0},{24,8},{1,17},{9,25},{17,1},{25,9},{2,18},{10... | collective-permute-start | bytes 3145736 | tf_op jit(solution)/shard_map/ppermute | solution.py:554
  369.2 42.9 %collective-permute-start.33 = (bf16[256,2048]{1,0:T(8,128)(2,1)}, bf16[256,2048]{1,0:T(8,128)(2,1)}, u32[]{:S(2)}, u32[]{:S(2)}) collective-permute-start(bf16[256,2048]{1,0:T(8,128)(2,1)} %get-tuple-element.348), channel_id=1, source_target_pairs={{0,24},{8,16},{16,8},{24,0},{1,25},{9,17},{17,9},{25,1},{2,26},{10... | collective-permute-start | bytes 3145736 | tf_op jit(solution)/shard_map/ppermute | solution.py:554
  467.1 39.9 %collective-permute-start.41 = (bf16[256,2048]{1,0:T(8,128)(2,1)}, bf16[256,2048]{1,0:T(8,128)(2,1)}, u32[]{:S(2)}, u32[]{:S(2)}) collective-permute-start(bf16[256,2048]{1,0:T(8,128)(2,1)} %get-tuple-element.370), channel_id=1, source_target_pairs={{0,24},{8,16},{16,8},{24,0},{1,25},{9,17},{17,9},{25,1},{2,26},{10... | collective-permute-start | bytes 3145736 | tf_op jit(solution)/shard_map/ppermute | solution.py:554
  483.2 35.2 %collective-permute-start.42 = (bf16[512,512]{1,0:T(8,128)(2,1)}, bf16[512,512]{1,0:T(8,128)(2,1)}, u32[]{:S(2)}, u32[]{:S(2)}) collective-permute-start(bf16[512,512]{1,0:T(8,128)(2,1)} %get-tuple-element.375), channel_id=1, source_target_pairs={{0,8},{8,0},{16,24},{24,16},{1,9},{9,1},{17,25},{25,17},{2,10},{10... | collective-permute-start | bytes 1572872 | tf_op jit(solution)/shard_map/ppermute | solution.py:554
  483.4 35.0 %collective-permute-start.43 = (bf16[512,512]{1,0:T(8,128)(2,1)}, bf16[512,512]{1,0:T(8,128)(2,1)}, u32[]{:S(2)}, u32[]{:S(2)}) collective-permute-start(bf16[512,512]{1,0:T(8,128)(2,1)} %get-tuple-element.376), channel_id=1, source_target_pairs={{0,16},{8,24},{16,0},{24,8},{1,17},{9,25},{17,1},{25,9},{2,18},{10... | collective-permute-start | bytes 1572872 | tf_op jit(solution)/shard_map/ppermute | solution.py:554
  483.7 34.7 %collective-permute-start.44 = (bf16[512,512]{1,0:T(8,128)(2,1)}, bf16[512,512]{1,0:T(8,128)(2,1)}, u32[]{:S(2)}, u32[]{:S(2)}) collective-permute-start(bf16[512,512]{1,0:T(8,128)(2,1)} %get-tuple-element.377), channel_id=1, source_target_pairs={{0,24},{8,16},{16,8},{24,0},{1,25},{9,17},{17,9},{25,1},{2,26},{10... | collective-permute-start | bytes 1572872 | tf_op jit(solution)/shard_map/ppermute | solution.py:554
  538.7 53.2 %collective-permute-start.54 = (bf16[512,1152]{1,0:T(8,128)(2,1)S(1)}, bf16[512,1152]{1,0:T(8,128)(2,1)S(1)}, u32[]{:S(2)}, u32[]{:S(2)}) collective-permute-start(bf16[512,1152]{1,0:T(8,128)(2,1)S(1)} %copy-done.87), channel_id=1, source_target_pairs={{0,16},{8,24},{16,0},{24,8},{1,17},{9,25},{17,1},{25,9},{2,18},{10... | collective-permute-start | bytes 3538952 | tf_op jit(solution)/shard_map/ppermute | solution.py:554
  540.1 51.8 %collective-permute-start.55 = (bf16[512,1152]{1,0:T(8,128)(2,1)S(1)}, bf16[512,1152]{1,0:T(8,128)(2,1)S(1)}, u32[]{:S(2)}, u32[]{:S(2)}) collective-permute-start(bf16[512,1152]{1,0:T(8,128)(2,1)S(1)} %copy-done.86), channel_id=1, source_target_pairs={{0,24},{8,16},{16,8},{24,0},{1,25},{9,17},{17,9},{25,1},{2,26},{10... | collective-permute-start | bytes 3538952 | tf_op jit(solution)/shard_map/ppermute | solution.py:554
  543.9 48.0 %collective-permute-start.51 = (bf16[128,2048]{1,0:T(8,128)(2,1)S(1)}, bf16[128,2048]{1,0:T(8,128)(2,1)S(1)}, u32[]{:S(2)}, u32[]{:S(2)}) collective-permute-start(bf16[128,2048]{1,0:T(8,128)(2,1)S(1)} %get-tuple-element.543), channel_id=1, source_target_pairs={{0,2},{1,3},{2,0},{3,1},{4,6},{5,7},{6,4},{7,5},{8,10},{9,11},{10,... | collective-permute-start | bytes 1572872 | tf_op jit(solution)/shard_map/ppermute | solution.py:554
  591.9 37.6 %collective-permute-start.58 = (f32[2,128]{1,0:T(2,128)S(1)}, f32[2,128]{1,0:T(2,128)S(1)}, u32[]{:S(2)}, u32[]{:S(2)}) collective-permute-start(f32[2,128]{1,0:T(2,128)S(1)} %add.389), channel_id=1, source_target_pairs={{0,2},{1,3},{2,0},{3,1},{4,6},{5,7},{6,4},{7,5},{8,10},{9,11},{10,... | collective-permute-start | bytes 3080 | tf_op jit(solution)/shard_map/ppermute | solution.py:554
  594.7 34.8 %collective-permute-start.52 = (bf16[128,2048]{1,0:T(8,128)(2,1)}, bf16[128,2048]{1,0:T(8,128)(2,1)}, u32[]{:S(2)}, u32[]{:S(2)}) collective-permute-start(bf16[128,2048]{1,0:T(8,128)(2,1)} %fusion.15), channel_id=1, source_target_pairs={{0,4},{4,0},{1,5},{5,1},{2,6},{6,2},{3,7},{7,3},{8,12},{12,8},{9,1... | collective-permute-start | bytes 1572872 | tf_op jit(solution)/shard_map/ppermute | solution.py:554
  595.3 44.3 %collective-permute-start.59 = (bf16[128,2048]{1,0:T(8,128)(2,1)}, bf16[128,2048]{1,0:T(8,128)(2,1)}, u32[]{:S(2)}, u32[]{:S(2)}) collective-permute-start(bf16[128,2048]{1,0:T(8,128)(2,1)} %get-tuple-element.408), channel_id=1, source_target_pairs={{0,2},{1,3},{2,0},{3,1},{4,6},{5,7},{6,4},{7,5},{8,10},{9,11},{10,... | collective-permute-start | bytes 1572872 | tf_op jit(solution)/shard_map/ppermute | solution.py:554
  599.8 54.2 %collective-permute-start.60 = (bf16[256,1152]{1,0:T(8,128)(2,1)}, bf16[256,1152]{1,0:T(8,128)(2,1)}, u32[]{:S(2)}, u32[]{:S(2)}) collective-permute-start(bf16[256,1152]{1,0:T(8,128)(2,1)} %fusion.17), channel_id=1, source_target_pairs={{0,4},{4,0},{1,5},{5,1},{2,6},{6,2},{3,7},{7,3},{8,12},{12,8},{9,1... | collective-permute-start | bytes 1769480 | tf_op jit(solution)/shard_map/ppermute | solution.py:554
  (142 other events, 2111.4 us)
Sparse Core Ops, SparseCore 0:
  96.2 122.7 all-gather.4
  250.3 64.7 all-gather.6
  348.3 71.4 reduce-scatter.2
  467.2 160.6 reduce-scatter.4

commit v6 on v5

--- a/solution.py
+++ b/solution.py
@@ -392,12 +392,12 @@
 
 
 def probabilities(keys, queries, first_query, earliest):
-    scores = dot(keys, queries, 1, 1) * score_scaling
+    scores = dot(keys, queries, 1, 1)
     key_index = lax.broadcasted_iota(jnp.int32, scores.shape, 0)
     query_index = lax.broadcasted_iota(jnp.int32, scores.shape, 1) + first_query
     allowed = (key_index <= query_index) & (key_index >= earliest)
     masked = jnp.where(allowed, scores, -1e30)
-    shifted = jnp.exp(masked - jnp.max(masked, axis=0, keepdims=True))
+    shifted = jnp.exp2((masked - jnp.max(masked, axis=0, keepdims=True)) * (score_scaling * 1.4426950408889634))
     return shifted * (1.0 / jnp.sum(shifted, axis=0, keepdims=True))
 
 

time: 691 us -> 690 us (level)
  transfers between devices with their start and end apart: 72 -> 72, of which waited for: 28 -> 29; matrix products, arithmetic and copies ran while one was open for 11% -> 11% of each run, Pallas kernels for 21% -> 21%
where the time goes in v6:
time: 690 us; the launch traced here: 686 us
  waiting for transfers between devices  312 us (45%)
  Pallas kernels  175 us (25%)
  starting transfers between devices  82.7 us (12%)
  other arithmetic  51.2 us (7%)
  local copies, waits for them, and re-layouts  49.3 us (7%)
  between operations  15.6 us (2%)
    ppermute x68, waiting for transfers between devices, swap(): lax.ppermute(x, axis, [(i, i ^ bit) for i in range(lax.axis_size(axis))])  284 us
    ppermute x68, starting transfers between devices, swap(): lax.ppermute(x, axis, [(i, i ^ bit) for i in range(lax.axis_size(axis))])  82.4 us
    pallas_call x2, Pallas kernels, stacked_back(): pl.pallas_call(stacked_back_kernel, grid=(groups,), in_specs=[pl.BlockSpe...  29.6 us
    pallas_call x2, Pallas kernels, term_product(): pl.pallas_call(term_kernel, grid=(groups,), in_specs=[pl.BlockSpec((rows,...  29.4 us
    reduce_scatter x2, waiting for transfers between devices, ffn_scatter(): lax.psum_scatter(term, ('h', 't'), scatter_dimension=0, tiled=True)  27.4 us
    dynamic_update_slice x24, local copies, waits for them, and re-layouts, assemble(): out = lax.dynamic_update_slice_in_dim(out, part[:, columns], start, 0)  19.1 us
    pallas_call x1, Pallas kernels, attention_backward(): pl.pallas_call(functools.partial(backward_kernel, 256), grid=(heads,), in...  19 us
    pallas_call x1, Pallas kernels, stacked_product(): pl.pallas_call(stacked_kernel, grid=(columns // tile,), in_specs=[pl.Bloc...  18.7 us
  transfers between devices with their start and end apart: 72, of which 29 were waited for; matrix products, arithmetic and copies ran while one was open for 11% of the time, Pallas kernels for 21%

profile of v6, /device:TPU:0, one launch (start us, length us, event | category | flops | bytes accessed | tf_op | source)
XLA Modules:
  0.0 686.0 jit_solution(12876593687688482691)
XLA Ops:
  27.5 14.5 %collective-permute-done.2.refs_2_ = bf16[64,1536]{1,0:T(8,128)(2,1)S(1)} collective-permute-done((bf16[64,1536]{1,0:T(8,128)(2,1)S(1)}, bf16[64,1536]{1,0:T(8,128)(2,1)S(1)}, u32[]{:S(2)}, u32[]{:S(2)}) %collective-permute-start.2) | collective-permute-done | bytes 196640 | tf_op jit(solution)/shard_map/ppermute | solution.py:554
  57.2 23.5 %collective-permute-done.12.refs_4_ = bf16[256,512]{1,0:T(8,128)(2,1)S(1)} collective-permute-done((bf16[256,512]{1,0:T(8,128)(2,1)S(1)}, bf16[256,512]{1,0:T(8,128)(2,1)S(1)}, u32[]{:S(2)}, u32[]{:S(2)}) %collective-permute-start.12) | collective-permute-done | bytes 262176 | tf_op jit(solution)/shard_map/ppermute | solution.py:554
  118.2 11.1 %collective-permute-done.16.refs_6_ = bf16[256,1024]{1,0:T(8,128)(2,1)S(1)} collective-permute-done((bf16[256,1024]{1,0:T(8,128)(2,1)S(1)}, bf16[256,1024]{1,0:T(8,128)(2,1)S(1)}, u32[]{:S(2)}, u32[]{:S(2)}) %collective-permute-start.16) | collective-permute-done | bytes 524320 | tf_op jit(solution)/shard_map/ppermute | solution.py:554
  146.4 10.1 %collective-permute-done.19 = bf16[512,512]{1,0:T(8,128)(2,1)S(1)} collective-permute-done((bf16[512,512]{1,0:T(8,128)(2,1)S(1)}, bf16[512,512]{1,0:T(8,128)(2,1)S(1)}, u32[]{:S(2)}, u32[]{:S(2)}) %collective-permute-start.19) | collective-permute-done | bytes 524320 | tf_op jit(solution)/shard_map/ppermute | solution.py:554
  160.5 12.5 %shard_map.226.a_ref.b_ref = bf16[1024,512]{1,0:T(8,128)(2,1)S(1)} custom-call(f32[1024,1024]{1,0:T(8,128)} %shard_map.224.qkv_ref, f32[2,128]{1,0:T(2,128)S(1)} %convert_element_type.208.gain_ref, f32[1024,128]{1,0:T(8,128)S(1)} %get-tuple-element.569.cos_ref, f32[1024,128]{1,0:T(8,128)S(1)} %get-tuple-element.570.sin_ref, ...), custom_call_target="tpu_custom_call" | custom-call | flops 1048576 | bytes 65536 | tf_op jit(solution)/shard_map/pallas_call | solution.py:477
  194.3 26.3 %collective-permute-done.23 = bf16[128,2048]{1,0:T(8,128)(2,1)S(1)} collective-permute-done((bf16[128,2048]{1,0:T(8,128)(2,1)S(1)}, bf16[128,2048]{1,0:T(8,128)(2,1)S(1)}, u32[]{:S(2)}, u32[]{:S(2)}) %collective-permute-start.23) | collective-permute-done | bytes 524320 | tf_op jit(solution)/shard_map/ppermute | solution.py:554
  226.5 20.5 %collective-permute-done.24 = bf16[128,2048]{1,0:T(8,128)(2,1)S(1)} collective-permute-done((bf16[128,2048]{1,0:T(8,128)(2,1)S(1)}, bf16[128,2048]{1,0:T(8,128)(2,1)S(1)}, u32[]{:S(2)}, u32[]{:S(2)}) %collective-permute-start.24) | collective-permute-done | bytes 524320 | tf_op jit(solution)/shard_map/ppermute | solution.py:554
  262.1 18.9 %collective-permute-done.28 = bf16[256,2048]{1,0:T(8,128)(2,1)S(1)} collective-permute-done((bf16[256,2048]{1,0:T(8,128)(2,1)S(1)}, bf16[256,2048]{1,0:T(8,128)(2,1)S(1)}, u32[]{:S(2)}, u32[]{:S(2)}) %collective-permute-start.28) | collective-permute-done | bytes 1048608 | tf_op jit(solution)/shard_map/ppermute | solution.py:554
  281.0 19.4 %collective-permute-done.29 = bf16[256,2048]{1,0:T(8,128)(2,1)S(1)} collective-permute-done((bf16[256,2048]{1,0:T(8,128)(2,1)S(1)}, bf16[256,2048]{1,0:T(8,128)(2,1)S(1)}, u32[]{:S(2)}, u32[]{:S(2)}) %collective-permute-start.29) | collective-permute-done | bytes 1048608 | tf_op jit(solution)/shard_map/ppermute | solution.py:554
  302.7 18.7 %shard_map.231.pre_ref = f32[1024,3072]{1,0:T(8,128)} custom-call(bf16[1024,2048]{1,0:T(8,128)(2,1)} %pad_maximum_fusion.a_ref, bf16[8,4,64,3072]{3,2,1,0:T(8,128)(2,1)} %bitcast.245), custom_call_target="tpu_custom_call" | custom-call | flops 1048576 | bytes 65536 | tf_op jit(solution)/shard_map/pallas_call | solution.py:142
  321.4 16.2 %shard_map.232 = (bf16[1024,1536]{1,0:T(8,128)(2,1)}, bf16[1024,3072]{1,0:T(8,128)(2,1)}) custom-call(f32[1024,3072]{1,0:T(8,128)} %shard_map.231.pre_ref, bf16[1024,2048]{1,0:T(8,128)(2,1)} %pad_maximum_fusion.1.grad_ref.a_ref, bf16[8,4,64,1536]{3,2,1,0:T(8,128)(2,1)} %bitcast.249), custom_call_target="tpu_custom_call" | custom-call | flops 1048576 | bytes 65536 | tf_op jit(solution)/shard_map/pallas_call | solution.py:528
  337.6 10.7 %shard_map.233 = bf16[8,4,64,1536]{3,2,1,0:T(8,128)(2,1)} custom-call(bf16[1024,2048]{1,0:T(8,128)(2,1)} %pad_maximum_fusion.1.grad_ref.a_ref, bf16[1024,1536]{1,0:T(8,128)(2,1)} %get-tuple-element.333.b_ref.a_ref), custom_call_target="tpu_custom_call" | custom-call | flops 1048576 | bytes 65536 | tf_op jit(solution)/shard_map/pallas_call | solution.py:190
  348.4 18.9 %shard_map.234 = (bf16[256,2048]{1,0:T(8,128)(2,1)}, bf16[256,2048]{1,0:T(8,128)(2,1)}, bf16[256,2048]{1,0:T(8,128)(2,1)}, bf16[256,2048]{1,0:T(8,128)(2,1)}) custom-call(bf16[1024,3072]{1,0:T(8,128)(2,1)} %get-tuple-element.340.a_ref.b_ref, bf16[8,4,64,3072]{3,2,1,0:T(8,128)(2,1)} %bitcast.246), custom_call_target="tpu_custom_call" | custom-call | flops 1048576 | bytes 65536 | tf_op jit(solution)/shard_map/pallas_call | solution.py:168
  370.8 10.7 %shard_map.236 = (bf16[256,2048]{1,0:T(8,128)(2,1)}, bf16[256,2048]{1,0:T(8,128)(2,1)}, bf16[256,2048]{1,0:T(8,128)(2,1)}, bf16[256,2048]{1,0:T(8,128)(2,1)}) custom-call(bf16[1024,1536]{1,0:T(8,128)(2,1)} %get-tuple-element.333.b_ref.a_ref, bf16[8,4,64,1536]{3,2,1,0:T(8,128)(2,1)} %bitcast.250), custom_call_target="tpu_custom_call" | custom-call | flops 1048576 | bytes 65536 | tf_op jit(solution)/shard_map/pallas_call | solution.py:168
  381.5 18.7 %shard_map.235 = bf16[8,4,64,3072]{3,2,1,0:T(8,128)(2,1)} custom-call(bf16[1024,2048]{1,0:T(8,128)(2,1)} %pad_maximum_fusion.a_ref, bf16[1024,3072]{1,0:T(8,128)(2,1)} %get-tuple-element.340.a_ref.b_ref), custom_call_target="tpu_custom_call" | custom-call | flops 1048576 | bytes 65536 | tf_op jit(solution)/shard_map/pallas_call | solution.py:190
  400.2 12.1 %collective-permute-done.32 = bf16[256,2048]{1,0:T(8,128)(2,1)} collective-permute-done((bf16[256,2048]{1,0:T(8,128)(2,1)}, bf16[256,2048]{1,0:T(8,128)(2,1)}, u32[]{:S(2)}, u32[]{:S(2)}) %collective-permute-start.32) | collective-permute-done | bytes 1048608 | tf_op jit(solution)/shard_map/ppermute | solution.py:554
  429.9 14.1 %collective-permute-done.34 = bf16[1,128,2048]{2,1,0:T(8,128)(2,1)S(1)} collective-permute-done((bf16[1,128,2048]{2,1,0:T(8,128)(2,1)S(1)}, bf16[1,128,2048]{2,1,0:T(8,128)(2,1)S(1)}, u32[]{:S(2)}, u32[]{:S(2)}) %collective-permute-start.34) | collective-permute-done | bytes 524320 | tf_op jit(solution)/shard_map/ppermute | solution.py:554
  448.7 13.1 %collective-permute-done.37 = bf16[1,128,2048]{2,1,0:T(8,128)(2,1)S(1)} collective-permute-done((bf16[1,128,2048]{2,1,0:T(8,128)(2,1)S(1)}, bf16[1,128,2048]{2,1,0:T(8,128)(2,1)S(1)}, u32[]{:S(2)}, u32[]{:S(2)}) %collective-permute-start.37) | collective-permute-done | bytes 524320 | tf_op jit(solution)/shard_map/ppermute | solution.py:554
  488.2 19.0 %shard_map.239 = (bf16[1024,1024]{1,0:T(8,128)(2,1)S(1)}, f32[2,8,128]{2,1,0:T(8,128)S(1)}) custom-call(f32[1024,1024]{1,0:T(8,128)} %shard_map.224.qkv_ref, bf16[1024,512]{1,0:T(8,128)(2,1)S(1)} %copy-done.4, f32[2,128]{1,0:T(2,128)S(1)} %convert_element_type.208.gain_ref, f32[1024,128]{1,0:T(8,128)S(1)} %get-tuple-element.569.cos_ref, ...), custom_call_target="tpu_custom_call" | custom-call | flops 1048576 | bytes 65536 | tf_op jit(solution)/shard_map/pallas_call | solution.py:491
  522.2 10.4 %shard_map.241 = (bf16[512,1152]{1,0:T(8,128)(2,1)}, bf16[512,1152]{1,0:T(8,128)(2,1)}, bf16[512,1152]{1,0:T(8,128)(2,1)}, bf16[512,1152]{1,0:T(8,128)(2,1)}) custom-call(s32[1]{0:T(128)} %bitcast.me_ref, bf16[1024,2048]{1,0:T(8,128)(2,1)} %slice_dynamic-update-slice_fusion.a_ref.normed_ref, bf16[1024,1024]{1,0:T(8,128)(2,1)} %copy-done.2, f32[8,2048]{1,0:T(8,128)} %copy-done.44), custom_call_target="tpu_custom_call" | custom-call | flops 1048576 | bytes 65536 | tf_op jit(solution)/shard_map/pallas_call | solution.py:230
  547.0 12.2 %collective-permute-done.56 = bf16[256,512]{1,0:T(8,128)(2,1)S(1)} collective-permute-done((bf16[256,512]{1,0:T(8,128)(2,1)S(1)}, bf16[256,512]{1,0:T(8,128)(2,1)S(1)}, u32[]{:S(2)}, u32[]{:S(2)}) %collective-permute-start.56) | collective-permute-done | bytes 262176 | tf_op jit(solution)/shard_map/ppermute | solution.py:554
  566.5 25.5 %collective-permute-done.54 = bf16[512,1152]{1,0:T(8,128)(2,1)S(1)} collective-permute-done((bf16[512,1152]{1,0:T(8,128)(2,1)S(1)}, bf16[512,1152]{1,0:T(8,128)(2,1)S(1)}, u32[]{:S(2)}, u32[]{:S(2)}) %collective-permute-start.54) | collective-permute-done | bytes 1179680 | tf_op jit(solution)/shard_map/ppermute | solution.py:554
  600.8 27.4 %reduce-scatter.5.cloned.1.call-done = bf16[256,3072]{1,0:T(8,128)(2,1)} async-done(((bf16[2048,3072]{1,0:T(8,128)(2,1)}), bf16[256,3072]{1,0:T(8,128)(2,1)}) %reduce-scatter.5.cloned.1.call-update) | async-done | bytes 1572880 | tf_op jit(solution)/shard_map/reduce_scatter | solution.py:799
  629.9 10.0 %collective-permute-done.59 = bf16[128,2048]{1,0:T(8,128)(2,1)} collective-permute-done((bf16[128,2048]{1,0:T(8,128)(2,1)}, bf16[128,2048]{1,0:T(8,128)(2,1)}, u32[]{:S(2)}, u32[]{:S(2)}) %collective-permute-start.59) | collective-permute-done | bytes 524320 | tf_op jit(solution)/shard_map/ppermute | solution.py:554
  (462 shorter events, 275.8 us)
Async XLA Ops:
  7.2 243.0 %all-gather.5.cloned.1.call-start = ((), (), s32[]{:S(2)}) async-start(), calls=%async_computation.4 | async-start | bytes 14155776 | tf_op jit(solution)/shard_map/all_gather | solution.py:794
  49.5 43.3 %collective-permute-start.6 = (bf16[2,128,2176]{2,1,0:T(8,128)(2,1)S(1)}, bf16[2,128,2176]{2,1,0:T(8,128)(2,1)S(1)}, u32[]{:S(2)}, u32[]{:S(2)}) collective-permute-start(bf16[2,128,2176]{2,1,0:T(8,128)(2,1)S(1)} %constant_dynamic-update-slice_fusion.16), channel_id=1, source_target_pairs={{0,2},{1,3},{2,0},{3,1},{4,6},{5,7},{6,4},{7,5},{8,10},{9,11},{10,... | collective-permute-start | bytes 3342344 | tf_op jit(solution)/shard_map/ppermute | solution.py:554
  55.7 35.3 %collective-permute-start.7 = (bf16[256,1024]{1,0:T(8,128)(2,1)S(1)}, bf16[256,1024]{1,0:T(8,128)(2,1)S(1)}, u32[]{:S(2)}, u32[]{:S(2)}) collective-permute-start(bf16[256,1024]{1,0:T(8,128)(2,1)S(1)} %get-tuple-element.302.refs_0_), channel_id=1, source_target_pairs={{0,4},{4,0},{1,5},{5,1},{2,6},{6,2},{3,7},{7,3},{8,12},{12,8},{9,1... | collective-permute-start | bytes 1572872 | tf_op jit(solution)/shard_map/ppermute | solution.py:554
  96.1 225.2 %all-gather.7.cloned.1.call-start = ((), (), s32[]{:S(2)}) async-start(), calls=%async_computation.5 | async-start | bytes 7077888 | tf_op jit(solution)/shard_map/all_gather | solution.py:794
  133.5 39.5 %collective-permute-start.20 = (bf16[512,512]{1,0:T(8,128)(2,1)S(1)}, bf16[512,512]{1,0:T(8,128)(2,1)S(1)}, u32[]{:S(2)}, u32[]{:S(2)}) collective-permute-start(bf16[512,512]{1,0:T(8,128)(2,1)S(1)} %constant_dynamic-update-slice_fusion.18), channel_id=1, source_target_pairs={{0,24},{8,16},{16,8},{24,0},{1,25},{9,17},{17,9},{25,1},{2,26},{10... | collective-permute-start | bytes 1572872 | tf_op jit(solution)/shard_map/ppermute | solution.py:554
  182.1 67.0 %collective-permute-start.26 = (bf16[256,2048]{1,0:T(8,128)(2,1)}, bf16[256,2048]{1,0:T(8,128)(2,1)S(1)}, u32[]{:S(2)}, u32[]{:S(2)}) collective-permute-start(bf16[256,2048]{1,0:T(8,128)(2,1)} %bitcast.25), channel_id=1, source_target_pairs={{0,16},{8,24},{16,0},{24,8},{1,17},{9,25},{17,1},{25,9},{2,18},{10... | collective-permute-start | bytes 3145736 | tf_op jit(solution)/shard_map/ppermute | solution.py:554
  183.6 66.6 %collective-permute-start.27 = (bf16[256,2048]{1,0:T(8,128)(2,1)}, bf16[256,2048]{1,0:T(8,128)(2,1)}, u32[]{:S(2)}, u32[]{:S(2)}) collective-permute-start(bf16[256,2048]{1,0:T(8,128)(2,1)} %bitcast.25), channel_id=1, source_target_pairs={{0,24},{8,16},{16,8},{24,0},{1,25},{9,17},{17,9},{25,1},{2,26},{10... | collective-permute-start | bytes 3145736 | tf_op jit(solution)/shard_map/ppermute | solution.py:554
  250.2 267.1 %reduce-scatter.3.cloned.1.call-start = ((), (), s32[]{:S(2)}) async-start(), calls=%async_computation.2 | async-start | bytes 7077888 | tf_op jit(solution)/shard_map/reduce_scatter | solution.py:799
  256.4 44.1 %collective-permute-start.29 = (bf16[256,2048]{1,0:T(8,128)(2,1)S(1)}, bf16[256,2048]{1,0:T(8,128)(2,1)S(1)}, u32[]{:S(2)}, u32[]{:S(2)}) collective-permute-start(bf16[256,2048]{1,0:T(8,128)(2,1)S(1)} %fusion.13), channel_id=1, source_target_pairs={{0,16},{8,24},{16,0},{24,8},{1,17},{9,25},{17,1},{25,9},{2,18},{10... | collective-permute-start | bytes 3145736 | tf_op jit(solution)/shard_map/ppermute | solution.py:554
  257.8 42.6 %collective-permute-start.30 = (bf16[256,2048]{1,0:T(8,128)(2,1)S(1)}, bf16[256,2048]{1,0:T(8,128)(2,1)S(1)}, u32[]{:S(2)}, u32[]{:S(2)}) collective-permute-start(bf16[256,2048]{1,0:T(8,128)(2,1)S(1)} %fusion.13), channel_id=1, source_target_pairs={{0,24},{8,16},{16,8},{24,0},{1,25},{9,17},{17,9},{25,1},{2,26},{10... | collective-permute-start | bytes 3145736 | tf_op jit(solution)/shard_map/ppermute | solution.py:554
  348.3 279.9 %reduce-scatter.5.cloned.1.call-start = ((), (), s32[]{:S(2)}) async-start(), calls=%async_computation.3 | async-start | bytes 14155776 | tf_op jit(solution)/shard_map/reduce_scatter | solution.py:799
  368.6 43.7 %collective-permute-start.32 = (bf16[256,2048]{1,0:T(8,128)(2,1)}, bf16[256,2048]{1,0:T(8,128)(2,1)}, u32[]{:S(2)}, u32[]{:S(2)}) collective-permute-start(bf16[256,2048]{1,0:T(8,128)(2,1)} %get-tuple-element.347), channel_id=1, source_target_pairs={{0,16},{8,24},{16,0},{24,8},{1,17},{9,25},{17,1},{25,9},{2,18},{10... | collective-permute-start | bytes 3145736 | tf_op jit(solution)/shard_map/ppermute | solution.py:554
  369.4 42.9 %collective-permute-start.33 = (bf16[256,2048]{1,0:T(8,128)(2,1)}, bf16[256,2048]{1,0:T(8,128)(2,1)}, u32[]{:S(2)}, u32[]{:S(2)}) collective-permute-start(bf16[256,2048]{1,0:T(8,128)(2,1)} %get-tuple-element.348), channel_id=1, source_target_pairs={{0,24},{8,16},{16,8},{24,0},{1,25},{9,17},{17,9},{25,1},{2,26},{10... | collective-permute-start | bytes 3145736 | tf_op jit(solution)/shard_map/ppermute | solution.py:554
  467.4 39.8 %collective-permute-start.41 = (bf16[256,2048]{1,0:T(8,128)(2,1)}, bf16[256,2048]{1,0:T(8,128)(2,1)}, u32[]{:S(2)}, u32[]{:S(2)}) collective-permute-start(bf16[256,2048]{1,0:T(8,128)(2,1)} %get-tuple-element.370), channel_id=1, source_target_pairs={{0,24},{8,16},{16,8},{24,0},{1,25},{9,17},{17,9},{25,1},{2,26},{10... | collective-permute-start | bytes 3145736 | tf_op jit(solution)/shard_map/ppermute | solution.py:554
  483.4 35.1 %collective-permute-start.42 = (bf16[512,512]{1,0:T(8,128)(2,1)}, bf16[512,512]{1,0:T(8,128)(2,1)}, u32[]{:S(2)}, u32[]{:S(2)}) collective-permute-start(bf16[512,512]{1,0:T(8,128)(2,1)} %get-tuple-element.375), channel_id=1, source_target_pairs={{0,8},{8,0},{16,24},{24,16},{1,9},{9,1},{17,25},{25,17},{2,10},{10... | collective-permute-start | bytes 1572872 | tf_op jit(solution)/shard_map/ppermute | solution.py:554
  483.5 35.0 %collective-permute-start.43 = (bf16[512,512]{1,0:T(8,128)(2,1)}, bf16[512,512]{1,0:T(8,128)(2,1)}, u32[]{:S(2)}, u32[]{:S(2)}) collective-permute-start(bf16[512,512]{1,0:T(8,128)(2,1)} %get-tuple-element.376), channel_id=1, source_target_pairs={{0,16},{8,24},{16,0},{24,8},{1,17},{9,25},{17,1},{25,9},{2,18},{10... | collective-permute-start | bytes 1572872 | tf_op jit(solution)/shard_map/ppermute | solution.py:554
  483.9 34.7 %collective-permute-start.44 = (bf16[512,512]{1,0:T(8,128)(2,1)}, bf16[512,512]{1,0:T(8,128)(2,1)}, u32[]{:S(2)}, u32[]{:S(2)}) collective-permute-start(bf16[512,512]{1,0:T(8,128)(2,1)} %get-tuple-element.377), channel_id=1, source_target_pairs={{0,24},{8,16},{16,8},{24,0},{1,25},{9,17},{17,9},{25,1},{2,26},{10... | collective-permute-start | bytes 1572872 | tf_op jit(solution)/shard_map/ppermute | solution.py:554
  538.9 53.2 %collective-permute-start.54 = (bf16[512,1152]{1,0:T(8,128)(2,1)S(1)}, bf16[512,1152]{1,0:T(8,128)(2,1)S(1)}, u32[]{:S(2)}, u32[]{:S(2)}) collective-permute-start(bf16[512,1152]{1,0:T(8,128)(2,1)S(1)} %copy-done.87), channel_id=1, source_target_pairs={{0,16},{8,24},{16,0},{24,8},{1,17},{9,25},{17,1},{25,9},{2,18},{10... | collective-permute-start | bytes 3538952 | tf_op jit(solution)/shard_map/ppermute | solution.py:554
  540.3 51.8 %collective-permute-start.55 = (bf16[512,1152]{1,0:T(8,128)(2,1)S(1)}, bf16[512,1152]{1,0:T(8,128)(2,1)S(1)}, u32[]{:S(2)}, u32[]{:S(2)}) collective-permute-start(bf16[512,1152]{1,0:T(8,128)(2,1)S(1)} %copy-done.86), channel_id=1, source_target_pairs={{0,24},{8,16},{16,8},{24,0},{1,25},{9,17},{17,9},{25,1},{2,26},{10... | collective-permute-start | bytes 3538952 | tf_op jit(solution)/shard_map/ppermute | solution.py:554
  544.0 48.0 %collective-permute-start.51 = (bf16[128,2048]{1,0:T(8,128)(2,1)S(1)}, bf16[128,2048]{1,0:T(8,128)(2,1)S(1)}, u32[]{:S(2)}, u32[]{:S(2)}) collective-permute-start(bf16[128,2048]{1,0:T(8,128)(2,1)S(1)} %get-tuple-element.543), channel_id=1, source_target_pairs={{0,2},{1,3},{2,0},{3,1},{4,6},{5,7},{6,4},{7,5},{8,10},{9,11},{10,... | collective-permute-start | bytes 1572872 | tf_op jit(solution)/shard_map/ppermute | solution.py:554
  592.1 37.7 %collective-permute-start.58 = (f32[2,128]{1,0:T(2,128)S(1)}, f32[2,128]{1,0:T(2,128)S(1)}, u32[]{:S(2)}, u32[]{:S(2)}) collective-permute-start(f32[2,128]{1,0:T(2,128)S(1)} %add.389), channel_id=1, source_target_pairs={{0,2},{1,3},{2,0},{3,1},{4,6},{5,7},{6,4},{7,5},{8,10},{9,11},{10,... | collective-permute-start | bytes 3080 | tf_op jit(solution)/shard_map/ppermute | solution.py:554
  594.8 35.0 %collective-permute-start.52 = (bf16[128,2048]{1,0:T(8,128)(2,1)}, bf16[128,2048]{1,0:T(8,128)(2,1)}, u32[]{:S(2)}, u32[]{:S(2)}) collective-permute-start(bf16[128,2048]{1,0:T(8,128)(2,1)} %fusion.15), channel_id=1, source_target_pairs={{0,4},{4,0},{1,5},{5,1},{2,6},{6,2},{3,7},{7,3},{8,12},{12,8},{9,1... | collective-permute-start | bytes 1572872 | tf_op jit(solution)/shard_map/ppermute | solution.py:554
  595.5 44.3 %collective-permute-start.59 = (bf16[128,2048]{1,0:T(8,128)(2,1)}, bf16[128,2048]{1,0:T(8,128)(2,1)}, u32[]{:S(2)}, u32[]{:S(2)}) collective-permute-start(bf16[128,2048]{1,0:T(8,128)(2,1)} %get-tuple-element.408), channel_id=1, source_target_pairs={{0,2},{1,3},{2,0},{3,1},{4,6},{5,7},{6,4},{7,5},{8,10},{9,11},{10,... | collective-permute-start | bytes 1572872 | tf_op jit(solution)/shard_map/ppermute | solution.py:554
  600.0 54.3 %collective-permute-start.60 = (bf16[256,1152]{1,0:T(8,128)(2,1)}, bf16[256,1152]{1,0:T(8,128)(2,1)}, u32[]{:S(2)}, u32[]{:S(2)}) collective-permute-start(bf16[256,1152]{1,0:T(8,128)(2,1)} %fusion.17), channel_id=1, source_target_pairs={{0,4},{4,0},{1,5},{5,1},{2,6},{6,2},{3,7},{7,3},{8,12},{12,8},{9,1... | collective-permute-start | bytes 1769480 | tf_op jit(solution)/shard_map/ppermute | solution.py:554
  (142 other events, 2110.9 us)
Sparse Core Ops, SparseCore 0:
  96.2 122.7 all-gather.4
  250.3 64.7 all-gather.6
  348.5 71.3 reduce-scatter.2
  467.5 160.6 reduce-scatter.4
